TPU v7x, 32 devices: a whole 2x2x4 slice. The times are simulated.
32 devices in a mesh: ctx: 16 (over z, y, x), tp: 2 (over core).
Axes of the slice: x: 2, y: 2, z: 4, core: 2. Of those that a mesh axis runs over, the one named last changes fastest.
Arguments:
- queries: bfloat16 [4096, 8192], P('ctx', 'tp'), may hold values from -128 to 128
- cotangent: bfloat16 [4096, 8192], P('ctx', 'tp'), may hold values from -96 to 96
- image_keys: bfloat16 [16, 64, 1024], P('ctx', None, 'tp'), may hold values from -8 to 8
- image_values: bfloat16 [16, 64, 1024], P('ctx', None, 'tp'), may hold values from -6 to 6
- attn_gate: float32 [1], replicated, may hold values from 0.4 to 1.5
- block_mask: int32 [32, 16], P('ctx'), may hold values from 0 to 1, as said below
- image_owner: int32 [16], replicated, may hold values from 0 to 15, each once
Outputs:
- query_grad: bfloat16 [4096, 8192], P('ctx', 'tp')
- key_grad: bfloat16 [16, 64, 1024], P('ctx', None, 'tp')
- value_grad: bfloat16 [16, 64, 1024], P('ctx', None, 'tp')
- gate_grad: float32 [1], replicated
Inputs may be any that keep to these rules, and one draw needn't show every extreme that they name: `block_mask`: every text block reads at least one image; the 2 blocks of one index of ctx together read exactly 8 distinct images.
All inputs are finite; a program needn't handle non-finite values.
Results may differ from a plain program's by a relative error of at most 0.02.
Values may be sent and summed in bfloat16 or wider, within the bound.
No kernel may reach another device: no remote copies, remote signals or barrier semaphores. Data moves between devices by JAX's collectives and lax.ppermute only.
A program may use at most 64 MiB of HBM per device.

v0:
```python
import math

import jax
import jax.numpy as jnp
from jax import lax
from jax.sharding import PartitionSpec as P

HD = 128
BLK = 128


def per_device(queries, cotangent, image_keys, image_values, attn_gate, block_mask, image_owner):
    tok_dev = queries.shape[0]
    local_kv = image_keys.shape[2] // HD
    local_heads = queries.shape[1] // HD
    groups = local_heads // local_kv
    img_tok = image_keys.shape[1]
    inv_root = 1.0 / math.sqrt(HD)
    read_most = lax.axis_size("ctx") // 2
    gathered_keys, gathered_values = (
        lax.all_gather(image_keys, "ctx", axis=0, tiled=True),
        lax.all_gather(image_values, "ctx", axis=0, tiled=True),
    )
    n_images = gathered_keys.shape[0]
    read_any = jnp.max(block_mask, axis=0)
    ranking = read_any * (2 * n_images) + (n_images - 1 - jnp.arange(n_images, dtype=jnp.int32))
    top_vals, image_ids = lax.top_k(ranking, read_most)
    is_read = read_any[image_ids] > 0
    slot_ids = image_owner[image_ids]
    block_keep = (block_mask[:, image_ids] > 0) & is_read[None, :]
    keep_mask = jnp.repeat(jnp.repeat(block_keep, BLK, axis=0), img_tok, axis=1)
    key_rows = jnp.take(gathered_keys, slot_ids, axis=0).reshape(read_most * img_tok, local_kv, HD)
    value_rows = jnp.take(gathered_values, slot_ids, axis=0).reshape(
        read_most * img_tok, local_kv, HD
    )
    query_heads = queries.reshape(tok_dev, local_kv, groups, HD).transpose(2, 0, 1, 3)
    cot_heads = cotangent.reshape(tok_dev, local_kv, groups, HD).transpose(2, 0, 1, 3)
    gate_value = jnp.tanh(attn_gate[0])

    def head_step(state_in, head_inputs):
        key_acc, value_acc, gate_acc = state_in
        query_one, cot_one = head_inputs
        scores = (
            jnp.einsum("tkd,skd->kts", query_one, key_rows, preferred_element_type=jnp.float32)
            * inv_root
        )
        scores = jnp.where(keep_mask, scores, -1e30)
        row_max = jnp.max(scores, axis=-1, keepdims=True)
        exp_terms = jnp.where(keep_mask, jnp.exp(scores - row_max), 0.0)
        prob_full = exp_terms / jnp.sum(exp_terms, axis=-1, keepdims=True)
        prob_half = prob_full.astype(jnp.bfloat16)
        attended = jnp.einsum(
            "kts,skd->tkd", prob_half, value_rows, preferred_element_type=jnp.float32
        )
        cot_f = cot_one.astype(jnp.float32)
        gate_part = jnp.sum(cot_f * attended)
        attn_grad = (gate_value * cot_f).astype(jnp.bfloat16)
        prob_grad = jnp.einsum(
            "tkd,skd->kts", attn_grad, value_rows, preferred_element_type=jnp.float32
        )
        row_delta = jnp.sum(attn_grad.astype(jnp.float32) * attended, axis=-1).T
        score_grad = (prob_full * (prob_grad - row_delta[:, :, None]) * inv_root).astype(
            jnp.bfloat16
        )
        query_grad = jnp.einsum(
            "kts,skd->tkd", score_grad, key_rows, preferred_element_type=jnp.float32
        ).astype(jnp.bfloat16)
        key_acc = key_acc + jnp.einsum(
            "kts,tkd->skd", score_grad, query_one, preferred_element_type=jnp.float32
        )
        value_acc = value_acc + jnp.einsum(
            "kts,tkd->skd", prob_half, attn_grad, preferred_element_type=jnp.float32
        )
        return ((key_acc, value_acc, gate_acc + gate_part), query_grad)

    zero_grads = jnp.zeros((read_most * img_tok, local_kv, HD), jnp.float32)
    init_state = (zero_grads, zero_grads, jnp.zeros((), jnp.float32))
    (key_acc, value_acc, gate_acc), head_grads = lax.scan(
        head_step, init_state, (query_heads, cot_heads)
    )
    query_grad = head_grads.transpose(1, 2, 0, 3).reshape(tok_dev, local_heads * HD)
    stacked = jnp.concatenate(
        [
            key_acc.reshape(read_most, img_tok, local_kv * HD),
            value_acc.reshape(read_most, img_tok, local_kv * HD),
        ],
        axis=-1,
    )
    stacked = jnp.where(is_read[:, None, None], stacked, 0.0)
    buffer = (
        jnp.zeros((n_images, img_tok, 2 * local_kv * HD), jnp.float32).at[slot_ids].add(stacked)
    )
    received = lax.all_to_all(buffer, "ctx", split_axis=0, concat_axis=0, tiled=True)
    summed = jnp.sum(received, axis=0, keepdims=True)
    key_grad = summed[:, :, : local_kv * HD].astype(jnp.bfloat16)
    value_grad = summed[:, :, local_kv * HD :].astype(jnp.bfloat16)
    gate_total = lax.psum(gate_acc, ("ctx", "tp"))
    term_count = tok_dev * lax.axis_size("ctx") * local_heads * lax.axis_size("tp") * HD
    gate_grad = ((1.0 - gate_value * gate_value) * gate_total / math.sqrt(term_count)).reshape(1)
    return (query_grad, key_grad, value_grad, gate_grad)


def solution(mesh):
    in_specs = (
        P("ctx", "tp"),
        P("ctx", "tp"),
        P("ctx", None, "tp"),
        P("ctx", None, "tp"),
        P(),
        P("ctx", None),
        P(),
    )
    out_specs = (P("ctx", "tp"), P("ctx", None, "tp"), P("ctx", None, "tp"), P())
    return jax.shard_map(
        per_device, mesh=mesh, in_specs=in_specs, out_specs=out_specs, check_vma=False
    )
```

profile of v0, /device:TPU:0, one launch (start us, length us, event | category | flops | bytes accessed | tf_op | source)
XLA Modules:
  0.0 397.2 jit_solution(3330988328590648862)
XLA Ops:
  10.2 1.2 top_k.11
  14.2 3.3 copy.40
  17.4 4.1 %copy.41 = bf16[256,4096]{0,1:T(8,128)(2,1)} copy(bf16[256,4096]{1,0:T(8,128)(2,1)} %param.12) | data formatting | bytes 4194304 | tf_op args[1]
  21.7 47.1 %all-gather.3.cloned.1.call-done = bf16[16,64,512]{2,1,0:T(8,128)(2,1)} async-done(((bf16[1,64,512]{2,1,0:T(8,128)(2,1)}), bf16[16,64,512]{2,1,0:T(8,128)(2,1)}) %all-gather.3.cloned.1.call-update) | async-done | bytes 1048592 | tf_op jit(solution)/shard_map/all_gather | solution.py:21
  68.8 2.6 gather_fusion.3
  71.4 54.3 %all-gather.5.cloned.1.call-done = bf16[16,64,512]{2,1,0:T(8,128)(2,1)} async-done(((bf16[1,64,512]{2,1,0:T(8,128)(2,1)}), bf16[16,64,512]{2,1,0:T(8,128)(2,1)}) %all-gather.5.cloned.1.call-update) | async-done | bytes 1048592 | tf_op jit(solution)/shard_map/all_gather | solution.py:22
  125.7 2.6 gather_fusion.4
  128.2 2.4 broadcast_select_fusion
  130.6 2.0 reshape.71
  132.6 1.9 copy.45
  134.5 2.0 reshape.73
  136.5 2.1 copy.47
  138.6 114.1 %while.17 = (s32[]{:T(128)}, f32[512,4,128]{0,2,1:T(8,128)S(1)}, f32[512,4,128]{0,2,1:T(8,128)}, f32[]{:T(128)}, bf16[8,256,4,128]{3,1,2,0:T(8,128)(2,1)}, /*ind...) while((s32[]{:T(128)}, f32[512,4,128]{0,2,1:T(8,128)S(1)}, ...), condition=%wide.region_7.9_spmd.clone, body=%wide.region_2.8_spmd.clone.sunk | while | flops 815660544 | bytes 50490676 | solution.py:78
  138.9 3.8 fusion.73
  143.9 3.3 fusion.76
  150.5 1.5 fusion.75
  152.9 3.9 fusion.73
  157.9 3.5 fusion.76
  161.5 1.1 fusion.74
  164.8 1.5 fusion.75
  167.2 3.9 fusion.73
  172.2 3.5 fusion.76
  179.1 1.5 fusion.75
  181.5 3.9 fusion.73
  186.5 3.5 fusion.76
  190.1 1.1 fusion.74
  193.4 1.5 fusion.75
  195.8 3.9 fusion.73
  200.8 3.5 fusion.76
  207.7 1.5 fusion.75
  210.1 3.9 fusion.73
  215.2 3.5 fusion.76
  222.0 1.5 fusion.75
  224.4 3.9 fusion.73
  229.5 3.5 fusion.76
  236.3 1.5 fusion.75
  238.7 3.9 fusion.73
  243.8 3.5 fusion.76
  250.6 1.5 fusion.75
  254.3 1.4 reshape.76
  255.8 1.5 maximum_select_fusion
  257.3 2.5 broadcast_in_dim.71
  259.8 4.4 %scatter_fusion = f32[16,64,1024]{2,1,0:T(8,128)} fusion(f32[16,64,1024]{2,1,0:T(8,128)} %broadcast_in_dim.71, s32[8]{0:T(128)S(1)} %fusion.35, f32[8,64,1024]{2,1,0:T(8,128)S(1)} %maximum_select_fusion), kind=kCustom, calls=%fused_computation.5 | custom fusion | flops 524288 | bytes 6291488 | tf_op jit(solution)/shard_map/scatter-add | solution.py:91
  264.2 4.7 %all-to-all-start = ((f32[16,64,1024]{2,1,0:T(8,128)}), f32[16,64,1024]{2,1,0:T(8,128)}, u32[]{:S(2)}, u32[]{:S(2)}) async-start(f32[16,64,1024]{2,1,0:T(8,128)} %scatter_fusion), calls=%async_computation | async-start | bytes 8388608 | tf_op jit(solution)/shard_map/all_to_all | solution.py:93
  268.8 112.9 %psum.7 = f32[]{:T(128)} all-reduce(f32[]{:T(128)} %get-tuple-element.72), channel_id=1, replica_groups=mesh['ctx'=16,'tp'=2] {'ctx','tp'}, use_global_device_ids=true, to_apply=%region_10.12 | all-reduce | flops 1 | bytes 8 | tf_op jit(solution)/shard_map/psum | solution.py:97
  381.7 1.4 copy.48
  383.0 2.3 copy.59
  386.0 2.5 reduce_sum.36
  (169 shorter events, 42.9 us)
Async XLA Ops:
  7.2 4.9 %copy-start = (s32[16]{0:T(128)S(1)}, s32[16]{0:T(128)}, u32[]{:S(2)}) copy-start(s32[16]{0:T(128)} %param.17) | copy-start | bytes 196
  7.2 61.6 %all-gather.3.cloned.1.call-start = ((), (), s32[]{:S(2)}) async-start(), calls=%async_computation.1 | async-start | bytes 1114112 | tf_op jit(solution)/shard_map/all_gather | solution.py:21
  7.9 117.7 %all-gather.5.cloned.1.call-start = ((), (), s32[]{:S(2)}) async-start(), calls=%async_computation.2 | async-start | bytes 1114112 | tf_op jit(solution)/shard_map/all_gather | solution.py:22
  138.6 4.1 %copy-start.1 = (bf16[8,256,4,128]{1,3,0,2:T(8,128)(2,1)}, bf16[8,256,4,128]{1,3,0,2:T(8,128)(2,1)S(1)}, u32[]{:S(2)}) copy-start(bf16[8,256,4,128]{1,3,0,2:T(8,128)(2,1)S(1)} %get-tuple-element.270) | copy-start | bytes 6291460 | tf_op jit(solution)/shard_map/while
  143.9 3.3 copy-start.6
  143.9 3.3 copy-start.7
  148.3 1.0 copy-start.5
  150.5 2.1 copy-start.2
  152.6 4.2 %copy-start.1 = (bf16[8,256,4,128]{1,3,0,2:T(8,128)(2,1)}, bf16[8,256,4,128]{1,3,0,2:T(8,128)(2,1)S(1)}, u32[]{:S(2)}) copy-start(bf16[8,256,4,128]{1,3,0,2:T(8,128)(2,1)S(1)} %get-tuple-element.270) | copy-start | bytes 6291460 | tf_op jit(solution)/shard_map/while
  157.9 3.6 copy-start.6
  157.9 3.5 copy-start.7
  162.6 1.0 copy-start.5
  164.8 2.1 copy-start.2
  166.9 4.2 %copy-start.1 = (bf16[8,256,4,128]{1,3,0,2:T(8,128)(2,1)}, bf16[8,256,4,128]{1,3,0,2:T(8,128)(2,1)S(1)}, u32[]{:S(2)}) copy-start(bf16[8,256,4,128]{1,3,0,2:T(8,128)(2,1)S(1)} %get-tuple-element.270) | copy-start | bytes 6291460 | tf_op jit(solution)/shard_map/while
  172.2 3.6 copy-start.6
  172.2 3.5 copy-start.7
  176.9 1.0 copy-start.5
  179.1 2.1 copy-start.2
  181.2 4.2 %copy-start.1 = (bf16[8,256,4,128]{1,3,0,2:T(8,128)(2,1)}, bf16[8,256,4,128]{1,3,0,2:T(8,128)(2,1)S(1)}, u32[]{:S(2)}) copy-start(bf16[8,256,4,128]{1,3,0,2:T(8,128)(2,1)S(1)} %get-tuple-element.270) | copy-start | bytes 6291460 | tf_op jit(solution)/shard_map/while
  186.5 3.6 copy-start.6
  186.5 3.5 copy-start.7
  191.2 1.0 copy-start.5
  193.4 2.1 copy-start.2
  195.5 4.2 %copy-start.1 = (bf16[8,256,4,128]{1,3,0,2:T(8,128)(2,1)}, bf16[8,256,4,128]{1,3,0,2:T(8,128)(2,1)S(1)}, u32[]{:S(2)}) copy-start(bf16[8,256,4,128]{1,3,0,2:T(8,128)(2,1)S(1)} %get-tuple-element.270) | copy-start | bytes 6291460 | tf_op jit(solution)/shard_map/while
  200.8 3.6 copy-start.6
  200.8 3.5 copy-start.7
  205.5 1.0 copy-start.5
  207.7 2.1 copy-start.2
  209.8 4.2 %copy-start.1 = (bf16[8,256,4,128]{1,3,0,2:T(8,128)(2,1)}, bf16[8,256,4,128]{1,3,0,2:T(8,128)(2,1)S(1)}, u32[]{:S(2)}) copy-start(bf16[8,256,4,128]{1,3,0,2:T(8,128)(2,1)S(1)} %get-tuple-element.270) | copy-start | bytes 6291460 | tf_op jit(solution)/shard_map/while
  215.1 3.6 copy-start.6
  215.1 3.5 copy-start.7
  219.8 1.0 copy-start.5
  222.0 2.1 copy-start.2
  224.1 4.2 %copy-start.1 = (bf16[8,256,4,128]{1,3,0,2:T(8,128)(2,1)}, bf16[8,256,4,128]{1,3,0,2:T(8,128)(2,1)S(1)}, u32[]{:S(2)}) copy-start(bf16[8,256,4,128]{1,3,0,2:T(8,128)(2,1)S(1)} %get-tuple-element.270) | copy-start | bytes 6291460 | tf_op jit(solution)/shard_map/while
  229.4 3.6 copy-start.6
  229.4 3.5 copy-start.7
  234.1 1.0 copy-start.5
  236.3 2.1 copy-start.2
  238.4 4.2 %copy-start.1 = (bf16[8,256,4,128]{1,3,0,2:T(8,128)(2,1)}, bf16[8,256,4,128]{1,3,0,2:T(8,128)(2,1)S(1)}, u32[]{:S(2)}) copy-start(bf16[8,256,4,128]{1,3,0,2:T(8,128)(2,1)S(1)} %get-tuple-element.270) | copy-start | bytes 6291460 | tf_op jit(solution)/shard_map/while
  243.7 3.6 copy-start.6
  243.7 3.5 copy-start.7
  248.4 1.0 copy-start.5
  250.6 2.1 copy-start.2
  252.7 1.2 copy-start.4
  264.2 117.5 %copy-start.3 = (bf16[8,256,4,128]{3,1,2,0:T(8,128)(2,1)S(1)}, bf16[8,256,4,128]{3,1,2,0:T(8,128)(2,1)}, u32[]{:S(2)}) copy-start(bf16[8,256,4,128]{3,1,2,0:T(8,128)(2,1)} %get-tuple-element.69) | copy-start | bytes 6291460
  264.2 121.9 %all-to-all-start = ((f32[16,64,1024]{2,1,0:T(8,128)}), f32[16,64,1024]{2,1,0:T(8,128)}, u32[]{:S(2)}, u32[]{:S(2)}) async-start(f32[16,64,1024]{2,1,0:T(8,128)} %scatter_fusion), calls=%async_computation | async-start | bytes 8388608 | tf_op jit(solution)/shard_map/all_to_all | solution.py:93
Sparse Core Ops, SparseCore 0:
  10.8 57.9 all-gather.2
  71.5 54.0 all-gather.4
where the time goes:
time: 399 us; the launch traced here: 397 us
  blocking collectives  113 us (28%)
  waiting for transfers between devices  103 us (26%)
  matrix products  92.8 us (23%)
  local copies, waits for them, and re-layouts  48.8 us (12%)
  between operations  16.7 us (4%)
  other arithmetic  12.9 us (3%)
  loops' own time  5.67 us (1%)
  starting transfers between devices  4.74 us (1%)
    psum x1, blocking collectives, per_device(): gate_total = lax.psum(gate_acc, ('ctx', 'tp'))  113 us
    all_gather x1, waiting for transfers between devices, per_device(): lax.all_gather(image_values, 'ctx', axis=0, tiled=True)  54.3 us
    all_gather x1, waiting for transfers between devices, per_device(): lax.all_gather(image_keys, 'ctx', axis=0, tiled=True)  47.1 us
    sub x8, matrix products, head_step(): exp_terms = jnp.where(keep_mask, jnp.exp(scores - row_max), 0.0)  30.8 us
    dot_general x8, matrix products, head_step(): jnp.einsum('kts,tkd->skd', prob_half, attn_grad, preferred_element_type=j...  28 us
    unnamed x12, local copies, waits for them, and re-layouts  14.9 us
    dot_general x8, matrix products, head_step(): jnp.einsum('kts,tkd->skd', score_grad, query_one, preferred_element_type=...  11.7 us
    dot_general x8, matrix products, head_step(): jnp.einsum('kts,skd->tkd', prob_half, value_rows, preferred_element_type=...  9.19 us
  transfers between devices with their start and end apart: 3, of which 2 were waited for; matrix products, arithmetic and copies ran while one was open for 5% of the time, Pallas kernels for 0%

commit v1 on v0

v1 whole, which is shorter than its diff:
```python
import functools
import math

import jax
import jax.numpy as jnp
from jax import lax
from jax.experimental import pallas as pl
from jax.experimental.pallas import tpu as pltpu
from jax.sharding import PartitionSpec as P

HD = 128
BLK = 128
PAIR = 2
CHUNKS = 2
NT = (((1,), (1,)), ((), ()))


def attention_kernel(
    n_outer,
    has_prev,
    mask_ref,
    owner_ref,
    me_ref,
    gate_ref,
    q_ref,
    cot_ref,
    k_own,
    k_x,
    k_yd,
    v_own,
    v_y,
    v_xd,
    *rest,
):
    if has_prev:
        rest = rest[1:]
    (
        dq_ref,
        dk_own,
        dk_x,
        dk_yd,
        dv_own,
        dv_y,
        dv_xd,
        gate_out,
        k_all,
        v_all,
        k_sel,
        v_sel,
        kt_sel,
        dk_acc,
        dv_acc,
        dk_all,
        dv_all,
        gate_acc,
        place,
        bias,
    ) = rest
    n_blocks, n_images = mask_ref.shape
    img_tok = k_own.shape[1]
    read_most = n_images // 2
    groups = q_ref.shape[1] // HD
    step = pl.program_id(0)
    gate_value = gate_ref[0]
    inv_root = 1.0 / math.sqrt(HD)
    to_exp2 = math.log2(math.e) * inv_root

    @pl.when(step == 0)
    def _():
        gate_acc[...] = jnp.zeros_like(gate_acc)
        me = me_ref[0]
        for j in range(read_most):
            place[j] = 0
            for b in range(n_blocks):
                bias[b, j] = jnp.float32(-1e30)

        def look(i, count):
            reads = [mask_ref[b, i] > 0 for b in range(n_blocks)]
            any_read = functools.reduce(jnp.logical_or, reads)

            @pl.when(jnp.logical_and(any_read, count < read_most))
            def _():
                slot = owner_ref[i]
                column = jnp.bitwise_xor(lax.rem(slot, 4), lax.rem(me, 4))
                back = lax.rem(lax.div(me, 4) - lax.div(slot, 4) + n_outer, n_outer)
                place[count] = column * n_outer + back
                for b in range(n_blocks):
                    bias[b, count] = jnp.where(reads[b], 0.0, -1e30).astype(jnp.float32)

            return count + any_read.astype(jnp.int32)

        lax.fori_loop(0, n_images, look, jnp.int32(0))

    n = n_outer
    k_all[0:n] = k_own[...]
    k_all[n : 2 * n] = k_x[...]
    k_all[2 * n : 4 * n] = k_yd[...]
    v_all[0:n] = v_own[...]
    v_all[n : 2 * n] = v_xd[0:n]
    v_all[2 * n : 3 * n] = v_y[...]
    v_all[3 * n : 4 * n] = v_xd[n : 2 * n]
    for j in range(read_most):
        rows = slice(j * img_tok, (j + 1) * img_tok)
        k_sel[rows] = k_all[place[j]]
        v_sel[rows] = v_all[place[j]]
    kt_sel[...] = k_sel[...].astype(jnp.float32).T.astype(jnp.bfloat16)
    dk_acc[...] = jnp.zeros_like(dk_acc)
    dv_acc[...] = jnp.zeros_like(dv_acc)

    pairs = groups // PAIR

    def one(it, carry):
        b = it // pairs
        g = it % pairs
        rows = pl.ds(pl.multiple_of(b * BLK, BLK), BLK)

        def heads_of(ref):
            return jnp.concatenate(
                [
                    ref[rows, pl.ds(pl.multiple_of((g * PAIR + u) * HD, HD), HD)]
                    for u in range(PAIR)
                ],
                axis=0,
            )

        query = heads_of(q_ref)
        cot = heads_of(cot_ref)
        scores = lax.dot_general(k_sel[...], query, NT, preferred_element_type=jnp.float32)
        scores = jnp.concatenate(
            [scores[j * img_tok : (j + 1) * img_tok] + bias[b, j] for j in range(read_most)],
            axis=0,
        )
        row_max = jnp.max(scores, axis=0, keepdims=True)
        terms = jnp.exp2((scores - row_max) * to_exp2)
        prob = terms * (1.0 / jnp.sum(terms, axis=0, keepdims=True))
        prob_half = prob.astype(jnp.bfloat16)
        prob_grad = lax.dot_general(v_sel[...], cot, NT, preferred_element_type=jnp.float32)
        delta = jnp.sum(prob_half.astype(jnp.float32) * prob_grad, axis=0, keepdims=True)
        score_grad = (prob * (prob_grad - delta)).astype(jnp.bfloat16)
        dq_t = jnp.dot(kt_sel[...], score_grad, preferred_element_type=jnp.float32)
        dq = (dq_t.T * (gate_value * inv_root)).astype(jnp.bfloat16)
        for u in range(PAIR):
            lanes = pl.ds(pl.multiple_of((g * PAIR + u) * HD, HD), HD)
            dq_ref[rows, lanes] = dq[u * BLK : (u + 1) * BLK]
        dk_acc[...] += jnp.dot(score_grad, query, preferred_element_type=jnp.float32)
        dv_acc[...] += jnp.dot(prob_half, cot, preferred_element_type=jnp.float32)
        gate_acc[0:1, :] += delta
        return carry

    lax.fori_loop(0, n_blocks * pairs, one, 0)

    dk_all[...] = jnp.zeros_like(dk_all)
    dv_all[...] = jnp.zeros_like(dv_all)
    for j in range(read_most):
        rows = slice(j * img_tok, (j + 1) * img_tok)
        dk_all[place[j]] = dk_acc[rows] * (gate_value * inv_root)
        dv_all[place[j]] = dv_acc[rows] * gate_value
    dk_own[...] = dk_all[0:n]
    dk_x[...] = dk_all[n : 2 * n]
    dk_yd[...] = dk_all[2 * n : 4 * n].astype(jnp.bfloat16)
    dv_own[...] = dv_all[0:n]
    dv_xd[0:n] = dv_all[n : 2 * n].astype(jnp.bfloat16)
    dv_y[...] = dv_all[2 * n : 3 * n]
    dv_xd[n : 2 * n] = dv_all[3 * n : 4 * n].astype(jnp.bfloat16)

    @pl.when(step == pl.num_programs(0) - 1)
    def _():
        gate_out[...] = jnp.full(gate_out.shape, jnp.sum(gate_acc[...]), jnp.float32)


def attention(first, heads, n_outer, prev, scalars, queries, cotangent, keys, values):
    tokens = queries.shape[0]
    local_kv = keys[0].shape[2] // HD * (1 if heads is None else 1)
    img_tok = keys[0].shape[1]
    n_images = scalars[0].shape[1]
    total_kv = scalars[4]
    groups = queries.shape[1] // HD // total_kv
    width = groups * HD
    n_keys = n_images // 2 * img_tok
    n = n_outer
    smem = pl.BlockSpec(memory_space=pltpu.SMEM)
    wide = pl.BlockSpec((tokens, width), lambda i: (0, first + i))

    def cols(count):
        return pl.BlockSpec((count, img_tok, HD), lambda i: (0, 0, i))

    in_specs = [smem] * 4 + [wide, wide]
    in_specs += [cols(n), cols(n), cols(2 * n)] * 2
    args = [*scalars[:4], queries, cotangent, *keys, *values]
    aliases = {}
    if prev is not None:
        in_specs.append(pl.BlockSpec(memory_space=pl.ANY))
        aliases = {len(args): 0}
        args.append(prev)
    span = heads * HD
    f32, bf16 = jnp.float32, jnp.bfloat16
    out_shape = [jax.ShapeDtypeStruct(queries.shape, bf16)]
    for _ in range(2):
        out_shape += [
            jax.ShapeDtypeStruct((n, img_tok, span), f32),
            jax.ShapeDtypeStruct((n, img_tok, span), f32),
            jax.ShapeDtypeStruct((2 * n, img_tok, span), bf16),
        ]
    out_shape.append(jax.ShapeDtypeStruct((8, HD), f32))
    out_specs = [wide] + [cols(n), cols(n), cols(2 * n)] * 2
    out_specs.append(pl.BlockSpec((8, HD), lambda i: (0, 0)))
    rows = tokens * groups * heads
    return pl.pallas_call(
        functools.partial(attention_kernel, n, prev is not None),
        grid=(heads,),
        in_specs=in_specs,
        out_specs=out_specs,
        out_shape=out_shape,
        input_output_aliases=aliases,
        scratch_shapes=[
            pltpu.VMEM((4 * n, img_tok, HD), bf16),
            pltpu.VMEM((4 * n, img_tok, HD), bf16),
            pltpu.VMEM((n_keys, HD), bf16),
            pltpu.VMEM((n_keys, HD), bf16),
            pltpu.VMEM((HD, n_keys), bf16),
            pltpu.VMEM((n_keys, HD), f32),
            pltpu.VMEM((n_keys, HD), f32),
            pltpu.VMEM((4 * n, img_tok, HD), f32),
            pltpu.VMEM((4 * n, img_tok, HD), f32),
            pltpu.VMEM((8, PAIR * BLK), f32),
            pltpu.SMEM((n_images // 2,), jnp.int32),
            pltpu.SMEM((scalars[0].shape[0], n_images // 2), f32),
        ],
        compiler_params=pltpu.CompilerParams(
            dimension_semantics=("arbitrary",), vmem_limit_bytes=48 * 1024 * 1024
        ),
        cost_estimate=pl.CostEstimate(
            flops=10 * rows * n_keys * HD,
            bytes_accessed=6 * rows * HD,
            transcendentals=rows * n_keys,
        ),
        name="attention_backward",
    )(*args)


def per_device(queries, cotangent, image_keys, image_values, attn_gate, block_mask, image_owner):
    n_ctx = lax.axis_size("ctx")
    n_tp = lax.axis_size("tp")
    n = n_ctx // 4
    local_kv = image_keys.shape[2] // HD
    chunks = min(CHUNKS, local_kv)
    heads = local_kv // chunks
    me = lax.axis_index("ctx").astype(jnp.int32).reshape(1)
    gate_value = jnp.tanh(attn_gate)
    f32, bf16 = jnp.float32, jnp.bfloat16

    def swap(value, bit):
        return lax.ppermute(value, "ctx", [(i, i ^ bit) for i in range(n_ctx)])

    def turn(value, by):
        pairs = [(i, (i // 4 + by) % n * 4 + i % 4) for i in range(n_ctx)]
        return lax.ppermute(value, "ctx", pairs)

    lanes = [slice(c * heads * HD, (c + 1) * heads * HD) for c in range(chunks)]
    columns = []
    for c in range(chunks):
        own = jnp.concatenate([image_keys[0, :, lanes[c]], image_values[0, :, lanes[c]]], axis=0)
        columns.append(jnp.stack([own] + [turn(own, k) for k in range(1, n)]))
    img_tok = image_keys.shape[1]
    gathered = []
    for c in range(chunks):
        k_own, v_own = columns[c][:, :img_tok], columns[c][:, img_tok:]
        k_x, v_y = swap(k_own, 1), swap(v_own, 2)
        k_yd = swap(jnp.concatenate([k_own, k_x]), 2)
        v_xd = swap(jnp.concatenate([v_own, v_y]), 1)
        gathered.append(((k_own, k_x, k_yd), (v_own, v_y, v_xd)))

    scalars = (block_mask, image_owner, me, gate_value, local_kv)
    dq = None
    key_parts, value_parts, gate_parts = [], [], []
    for c in range(chunks):
        keys, values = gathered[c]
        dq, dk_own, dk_x, dk_yd, dv_own, dv_y, dv_xd, gate_part = attention(
            c * heads, heads, n, dq, scalars, queries, cotangent, keys, values
        )
        gate_parts.append(gate_part)
        k_back, v_back = swap(dk_yd, 2), swap(dv_xd, 1)
        k_send = (dk_x + k_back[n:].astype(f32)).astype(bf16)
        v_send = (dv_y + v_back[n:].astype(f32)).astype(bf16)
        k_last, v_last = swap(k_send, 1), swap(v_send, 2)
        k_sum = dk_own + k_back[:n].astype(f32) + k_last.astype(f32)
        v_sum = dv_own + v_back[:n].astype(f32) + v_last.astype(f32)
        both = jnp.concatenate([k_sum, v_sum], axis=1)
        total = both[0]
        sends = both.astype(bf16)
        for k in range(1, n):
            total = total + turn(sends[k], -k).astype(f32)
        key_parts.append(total[:img_tok])
        value_parts.append(total[img_tok:])
    key_grad = jnp.concatenate(key_parts, axis=1).astype(bf16)[None]
    value_grad = jnp.concatenate(value_parts, axis=1).astype(bf16)[None]

    gate_sum = functools.reduce(jnp.add, gate_parts)

    def add_turns(value, axis, size, stride=1):
        total = value
        for k in range(1, size):
            pairs = [(i, (i + k) % size) for i in range(size)]
            total = total + lax.ppermute(value, axis, pairs)
        return total

    gate_sum = add_turns(gate_sum, "tp", n_tp)
    gate_sum = gate_sum + swap(gate_sum, 1)
    gate_sum = gate_sum + swap(gate_sum, 2)
    total = gate_sum
    for k in range(1, n):
        total = total + turn(gate_sum, k)
    term_count = queries.shape[0] * n_ctx * queries.shape[1] * n_tp
    gate_grad = (1.0 - gate_value * gate_value) * total[0, :1] / math.sqrt(term_count)
    return (dq, key_grad, value_grad, gate_grad)


def solution(mesh):
    in_specs = (
        P("ctx", "tp"),
        P("ctx", "tp"),
        P("ctx", None, "tp"),
        P("ctx", None, "tp"),
        P(),
        P("ctx", None),
        P(),
    )
    out_specs = (P("ctx", "tp"), P("ctx", None, "tp"), P("ctx", None, "tp"), P())
    return jax.shard_map(
        per_device, mesh=mesh, in_specs=in_specs, out_specs=out_specs, check_vma=False
    )
```

time: 399 us -> 115 us (0.29)
  blocking collectives: 113 us -> 0 us
  matrix products: 92.8 us -> 0 us
  waiting for transfers between devices: 103 us -> 22.1 us
  local copies, waits for them, and re-layouts: 48.8 us -> 1.43 us
  starting transfers between devices: 4.74 us -> 48.4 us
  Pallas kernels: 0 us -> 34.6 us
  between operations: 16.7 us -> 3.36 us
  other arithmetic: 12.9 us -> 4.74 us
  loops' own time: 5.67 us -> 0 us
    psum x1 -> x0, blocking collectives: 113 us -> none  [per_device(): gate_total = lax.psum(gate_acc, ('ctx', 'tp'))]
    all_gather x2 -> x0, waiting for transfers between devices: 101 us -> none  [the longest x1 54.3 us: per_device(): lax.all_gather(image_values, 'ctx', axis=0, tiled=True)]
    dot_general x40 -> x0, matrix products: 62 us -> none  [the longest x8 28 us: head_step(): jnp.einsum('kts,tkd->skd', prob_half, attn_grad, preferred_element_type=j...]
    ppermute x0 -> x34, starting transfers between devices: none -> 48.4 us  [the longest x15 24.8 us: turn(): return lax.ppermute(value, 'ctx', pairs)]
    pallas_call x0 -> x2, Pallas kernels: none -> 34.6 us  [attention(): pl.pallas_call(functools.partial(attention_kernel, n, prev is not None),...]
    sub x8 -> x0, matrix products: 30.8 us -> none  [head_step(): exp_terms = jnp.where(keep_mask, jnp.exp(scores - row_max), 0.0)]
    ppermute x0 -> x34, waiting for transfers between devices: none -> 22.1 us  [the longest x18 15.5 us: swap(): return lax.ppermute(value, 'ctx', [(i, i ^ bit) for i in range(n_ctx)])]
    unnamed x12 -> x6, local copies, waits for them, and re-layouts: 14.9 us -> 0.02 us
  transfers between devices with their start and end apart: 3 -> 34, of which waited for: 2 -> 13; matrix products, arithmetic and copies ran while one was open for 5% -> 4% of each run, Pallas kernels for 0% -> 30%
where the time goes in v1:
time: 115 us
  starting transfers between devices  48.4 us (42%)
  Pallas kernels  34.6 us (30%)
  waiting for transfers between devices  22.1 us (19%)
  other arithmetic  4.74 us (4%)
  between operations  3.36 us (3%)
  local copies, waits for them, and re-layouts  1.43 us (1%)
    pallas_call x2, Pallas kernels, attention(): pl.pallas_call(functools.partial(attention_kernel, n, prev is not None),...  34.6 us
    ppermute x15, starting transfers between devices, turn(): return lax.ppermute(value, 'ctx', pairs)  24.8 us
    ppermute x18, starting transfers between devices, swap(): return lax.ppermute(value, 'ctx', [(i, i ^ bit) for i in range(n_ctx)])  23.7 us
    ppermute x18, waiting for transfers between devices, swap(): return lax.ppermute(value, 'ctx', [(i, i ^ bit) for i in range(n_ctx)])  15.5 us
    ppermute x15, waiting for transfers between devices, turn(): return lax.ppermute(value, 'ctx', pairs)  5.48 us
  transfers between devices with their start and end apart: 34, of which 13 were waited for; matrix products, arithmetic and copies ran while one was open for 4% of the time, Pallas kernels for 30%

profile of v1, /device:TPU:0, one launch (start us, length us, event | category | flops | bytes accessed | tf_op | source)
XLA Modules:
  0.0 114.7 jit_solution(3674292180143826287)
XLA Ops:
  0.6 0.8 slice_bitcast_fusion.10
  1.5 4.1 %collective-permute-start.8 = (bf16[128,256]{1,0:T(8,128)(2,1)S(1)}, bf16[128,256]{1,0:T(8,128)(2,1)S(1)}, u32[]{:S(2)}, u32[]{:S(2)}) collective-permute-start(bf16[128,256]{1,0:T(8,128)(2,1)S(1)} %get-tuple-element.51), channel_id=1, source_target_pairs={{0,16},{2,18},{4,20},{6,22},{8,24},{10,26},{12,28},{14,30},{16,0},... | collective-permute-start | bytes 196616 | tf_op jit(solution)/shard_map/ppermute | solution.py:257
  5.6 1.6 %collective-permute-start.7 = (bf16[128,256]{1,0:T(8,128)(2,1)S(1)}, bf16[128,256]{1,0:T(8,128)(2,1)S(1)}, u32[]{:S(2)}, u32[]{:S(2)}) collective-permute-start(bf16[128,256]{1,0:T(8,128)(2,1)S(1)} %get-tuple-element.51), channel_id=1, source_target_pairs={{0,8},{2,10},{4,12},{6,14},{8,16},{10,18},{12,20},{14,22},{16,24},... | collective-permute-start | bytes 196616 | tf_op jit(solution)/shard_map/ppermute | solution.py:257
  7.2 2.2 %collective-permute-start.9 = (bf16[128,256]{1,0:T(8,128)(2,1)S(1)}, bf16[128,256]{1,0:T(8,128)(2,1)S(1)}, u32[]{:S(2)}, u32[]{:S(2)}) collective-permute-start(bf16[128,256]{1,0:T(8,128)(2,1)S(1)} %get-tuple-element.51), channel_id=1, source_target_pairs={{0,24},{2,26},{4,28},{6,30},{8,0},{10,2},{12,4},{14,6},{16,8},{18,... | collective-permute-start | bytes 196616 | tf_op jit(solution)/shard_map/ppermute | solution.py:257
  9.5 0.6 collective-permute-start
  10.0 3.3 %collective-permute-start.2 = (bf16[128,256]{1,0:T(8,128)(2,1)S(1)}, bf16[128,256]{1,0:T(8,128)(2,1)S(1)}, u32[]{:S(2)}, u32[]{:S(2)}) collective-permute-start(bf16[128,256]{1,0:T(8,128)(2,1)S(1)} %get-tuple-element.57), channel_id=1, source_target_pairs={{0,24},{2,26},{4,28},{6,30},{8,0},{10,2},{12,4},{14,6},{16,8},{18,... | collective-permute-start | bytes 196616 | tf_op jit(solution)/shard_map/ppermute | solution.py:257
  13.5 1.6 %collective-permute-start.12 = (bf16[4,64,256]{2,1,0:T(8,128)(2,1)S(1)}, bf16[4,64,256]{2,1,0:T(8,128)(2,1)S(1)}, u32[]{:S(2)}, u32[]{:S(2)}) collective-permute-start(bf16[4,64,256]{2,1,0:T(8,128)(2,1)S(1)} %get-tuple-element.42.v_own), channel_id=1, source_target_pairs={{0,4},{2,6},{4,0},{6,2},{8,12},{10,14},{12,8},{14,10},{16,20},{18,... | collective-permute-start | bytes 393224 | tf_op jit(solution)/shard_map/ppermute | solution.py:253
  15.1 1.5 %collective-permute-start.10 = (bf16[4,64,256]{2,1,0:T(8,128)(2,1)S(1)}, bf16[4,64,256]{2,1,0:T(8,128)(2,1)S(1)}, u32[]{:S(2)}, u32[]{:S(2)}) collective-permute-start(bf16[4,64,256]{2,1,0:T(8,128)(2,1)S(1)} %get-tuple-element.43.k_own), channel_id=1, source_target_pairs={{0,2},{2,0},{4,6},{6,4},{8,10},{10,8},{12,14},{14,12},{16,18},{18,... | collective-permute-start | bytes 393224 | tf_op jit(solution)/shard_map/ppermute | solution.py:253
  17.0 1.8 %collective-permute-start.5 = (bf16[4,64,256]{2,1,0:T(8,128)(2,1)S(1)}, bf16[4,64,256]{2,1,0:T(8,128)(2,1)S(1)}, u32[]{:S(2)}, u32[]{:S(2)}) collective-permute-start(bf16[4,64,256]{2,1,0:T(8,128)(2,1)S(1)} %get-tuple-element.44.v_own), channel_id=1, source_target_pairs={{0,4},{2,6},{4,0},{6,2},{8,12},{10,14},{12,8},{14,10},{16,20},{18,... | collective-permute-start | bytes 393224 | tf_op jit(solution)/shard_map/ppermute | solution.py:253
  18.8 0.7 pad_maximum_fusion.7
  19.5 1.5 %collective-permute-start.13 = (bf16[8,64,256]{2,1,0:T(8,128)(2,1)}, bf16[8,64,256]{2,1,0:T(8,128)(2,1)}, u32[]{:S(2)}, u32[]{:S(2)}) collective-permute-start(bf16[8,64,256]{2,1,0:T(8,128)(2,1)} %pad_maximum_fusion.7), channel_id=1, source_target_pairs={{0,2},{2,0},{4,6},{6,4},{8,10},{10,8},{12,14},{14,12},{16,18},{18,... | collective-permute-start | bytes 786440 | tf_op jit(solution)/shard_map/ppermute | solution.py:253
  21.0 0.7 pad_maximum_fusion.6
  21.7 1.3 %collective-permute-start.11 = (bf16[8,64,256]{2,1,0:T(8,128)(2,1)}, bf16[8,64,256]{2,1,0:T(8,128)(2,1)}, u32[]{:S(2)}, u32[]{:S(2)}) collective-permute-start(bf16[8,64,256]{2,1,0:T(8,128)(2,1)} %pad_maximum_fusion.6), channel_id=1, source_target_pairs={{0,4},{2,6},{4,0},{6,2},{8,12},{10,14},{12,8},{14,10},{16,20},{18,... | collective-permute-start | bytes 786440 | tf_op jit(solution)/shard_map/ppermute | solution.py:253
  23.0 0.5 collective-permute-start.3
  23.5 0.7 pad_maximum_fusion.4
  24.3 1.5 %collective-permute-start.6 = (bf16[8,64,256]{2,1,0:T(8,128)(2,1)}, bf16[8,64,256]{2,1,0:T(8,128)(2,1)S(1)}, u32[]{:S(2)}, u32[]{:S(2)}) collective-permute-start(bf16[8,64,256]{2,1,0:T(8,128)(2,1)} %pad_maximum_fusion.4), channel_id=1, source_target_pairs={{0,2},{2,0},{4,6},{6,4},{8,10},{10,8},{12,14},{14,12},{16,18},{18,... | collective-permute-start | bytes 786440 | tf_op jit(solution)/shard_map/ppermute | solution.py:253
  25.8 6.0 %collective-permute-done.3.k_x = bf16[4,64,256]{2,1,0:T(8,128)(2,1)S(1)} collective-permute-done((bf16[4,64,256]{2,1,0:T(8,128)(2,1)S(1)}, bf16[4,64,256]{2,1,0:T(8,128)(2,1)S(1)}, u32[]{:S(2)}, u32[]{:S(2)}) %collective-permute-start.3) | collective-permute-done | bytes 131104 | tf_op jit(solution)/shard_map/ppermute | solution.py:253
  31.8 0.7 pad_maximum_fusion.3
  32.5 1.0 collective-permute-start.4
  34.3 17.3 %attention_backward.2 = (bf16[256,4096]{1,0:T(8,128)(2,1)}, f32[4,64,256]{2,1,0:T(8,128)S(1)}, f32[4,64,256]{2,1,0:T(8,128)S(1)}, bf16[8,64,256]{2,1,0:T(8,128)(...) custom-call(s32[2,16]{1,0:T(2,128)S(1)} %copy-done.1, ...), custom_call_target="tpu_custom_call" | custom-call | flops 2684354560 | bytes 3145728 | tf_op jit(solution)/shard_map/attention_backward/pallas_call | solution.py:208
  51.6 1.0 collective-permute-start.14
  52.6 17.3 %attention_backward.3 = (bf16[256,4096]{1,0:T(8,128)(2,1)}, f32[4,64,256]{2,1,0:T(8,128)S(1)}, f32[4,64,256]{2,1,0:T(8,128)S(1)}, bf16[8,64,256]{2,1,0:T(8,128)(...) custom-call(s32[2,16]{1,0:T(2,128)S(1)} %copy-done.1, ...), custom_call_target="tpu_custom_call", output_to_operand_aliasing={{0}: (12, {})} | custom-call | flops 2684354560 | bytes 3145728 | tf_op jit(solution)/shard_map/attention_backward/pallas_call | solution.py:208
  69.9 1.2 %collective-permute-done.28 = f32[8,128]{1,0:T(8,128)S(1)} collective-permute-done((f32[8,128]{1,0:T(8,128)S(1)}, f32[8,128]{1,0:T(8,128)S(1)}, u32[]{:S(2)}, u32[]{:S(2)}) %collective-permute-start.28) | collective-permute-done | bytes 4128 | tf_op jit(solution)/shard_map/ppermute | solution.py:304
  71.1 1.5 %collective-permute-start.29 = (f32[8,128]{1,0:T(8,128)S(1)}, f32[8,128]{1,0:T(8,128)S(1)}, u32[]{:S(2)}, u32[]{:S(2)}) collective-permute-start(f32[8,128]{1,0:T(8,128)S(1)} %add.94), channel_id=1, source_target_pairs={{0,2},{2,0},{4,6},{6,4},{8,10},{10,8},{12,14},{14,12},{16,18},{18,... | collective-permute-start | bytes 12296 | tf_op jit(solution)/shard_map/ppermute | solution.py:253
  72.6 2.1 %collective-permute-done.29 = f32[8,128]{1,0:T(8,128)S(1)} collective-permute-done((f32[8,128]{1,0:T(8,128)S(1)}, f32[8,128]{1,0:T(8,128)S(1)}, u32[]{:S(2)}, u32[]{:S(2)}) %collective-permute-start.29) | collective-permute-done | bytes 4128 | tf_op jit(solution)/shard_map/ppermute | solution.py:253
  74.7 1.0 collective-permute-start.30
  75.7 2.6 %collective-permute-done.30 = f32[8,128]{1,0:T(8,128)S(1)} collective-permute-done((f32[8,128]{1,0:T(8,128)S(1)}, f32[8,128]{1,0:T(8,128)S(1)}, u32[]{:S(2)}, u32[]{:S(2)}) %collective-permute-start.30) | collective-permute-done | bytes 4128 | tf_op jit(solution)/shard_map/ppermute | solution.py:253
  78.3 3.0 %collective-permute-start.33 = (f32[8,128]{1,0:T(8,128)S(1)}, f32[8,128]{1,0:T(8,128)S(1)}, u32[]{:S(2)}, u32[]{:S(2)}) collective-permute-start(f32[8,128]{1,0:T(8,128)S(1)} %add.96), channel_id=1, source_target_pairs={{0,24},{2,26},{4,28},{6,30},{8,0},{10,2},{12,4},{14,6},{16,8},{18,... | collective-permute-start | bytes 12296 | tf_op jit(solution)/shard_map/ppermute | solution.py:257
  81.6 2.0 %collective-permute-start.31 = (f32[8,128]{1,0:T(8,128)S(1)}, f32[8,128]{1,0:T(8,128)S(1)}, u32[]{:S(2)}, u32[]{:S(2)}) collective-permute-start(f32[8,128]{1,0:T(8,128)S(1)} %add.96), channel_id=1, source_target_pairs={{0,8},{2,10},{4,12},{6,14},{8,16},{10,18},{12,20},{14,22},{16,24},... | collective-permute-start | bytes 12296 | tf_op jit(solution)/shard_map/ppermute | solution.py:257
  83.6 1.5 %collective-permute-start.16 = (bf16[8,64,256]{2,1,0:T(8,128)(2,1)S(1)}, bf16[8,64,256]{2,1,0:T(8,128)(2,1)S(1)}, u32[]{:S(2)}, u32[]{:S(2)}) collective-permute-start(bf16[8,64,256]{2,1,0:T(8,128)(2,1)S(1)} %get-tuple-element.26), channel_id=1, source_target_pairs={{0,2},{2,0},{4,6},{6,4},{8,10},{10,8},{12,14},{14,12},{16,18},{18,... | collective-permute-start | bytes 786440 | tf_op jit(solution)/shard_map/ppermute | solution.py:253
  85.1 1.4 %collective-permute-start.21 = (bf16[8,64,256]{2,1,0:T(8,128)(2,1)S(1)}, bf16[8,64,256]{2,1,0:T(8,128)(2,1)S(1)}, u32[]{:S(2)}, u32[]{:S(2)}) collective-permute-start(bf16[8,64,256]{2,1,0:T(8,128)(2,1)S(1)} %get-tuple-element.29), channel_id=1, source_target_pairs={{0,4},{2,6},{4,0},{6,2},{8,12},{10,14},{12,8},{14,10},{16,20},{18,... | collective-permute-start | bytes 786440 | tf_op jit(solution)/shard_map/ppermute | solution.py:253
  86.5 0.8 collective-permute-start.23
  88.5 1.3 %collective-permute-start.15 = (bf16[4,64,256]{2,1,0:T(8,128)(2,1)S(1)}, bf16[4,64,256]{2,1,0:T(8,128)(2,1)S(1)}, u32[]{:S(2)}, u32[]{:S(2)}) collective-permute-start(bf16[4,64,256]{2,1,0:T(8,128)(2,1)S(1)} %add_convert_fusion.3), channel_id=1, source_target_pairs={{0,2},{2,0},{4,6},{6,4},{8,10},{10,8},{12,14},{14,12},{16,18},{18,... | collective-permute-start | bytes 393224 | tf_op jit(solution)/shard_map/ppermute | solution.py:253
  89.8 3.0 %collective-permute-done.16 = bf16[8,64,256]{2,1,0:T(8,128)(2,1)S(1)} collective-permute-done((bf16[8,64,256]{2,1,0:T(8,128)(2,1)S(1)}, bf16[8,64,256]{2,1,0:T(8,128)(2,1)S(1)}, u32[]{:S(2)}, u32[]{:S(2)}) %collective-permute-start.16) | collective-permute-done | bytes 262176 | tf_op jit(solution)/shard_map/ppermute | solution.py:253
  92.9 1.4 %collective-permute-start.17 = (bf16[4,64,256]{2,1,0:T(8,128)(2,1)S(1)}, bf16[4,64,256]{2,1,0:T(8,128)(2,1)S(1)}, u32[]{:S(2)}, u32[]{:S(2)}) collective-permute-start(bf16[4,64,256]{2,1,0:T(8,128)(2,1)S(1)} %add_convert_fusion.2), channel_id=1, source_target_pairs={{0,4},{2,6},{4,0},{6,2},{8,12},{10,14},{12,8},{14,10},{16,20},{18,... | collective-permute-start | bytes 393224 | tf_op jit(solution)/shard_map/ppermute | solution.py:253
  94.3 1.7 %collective-permute-start.22 = (bf16[4,64,256]{2,1,0:T(8,128)(2,1)S(1)}, bf16[4,64,256]{2,1,0:T(8,128)(2,1)S(1)}, u32[]{:S(2)}, u32[]{:S(2)}) collective-permute-start(bf16[4,64,256]{2,1,0:T(8,128)(2,1)S(1)} %add_convert_fusion.1), channel_id=1, source_target_pairs={{0,2},{2,0},{4,6},{6,4},{8,10},{10,8},{12,14},{14,12},{16,18},{18,... | collective-permute-start | bytes 393224 | tf_op jit(solution)/shard_map/ppermute | solution.py:253
  96.0 1.3 %collective-permute-done.23 = bf16[8,64,256]{2,1,0:T(8,128)(2,1)S(1)} collective-permute-done((bf16[8,64,256]{2,1,0:T(8,128)(2,1)S(1)}, bf16[8,64,256]{2,1,0:T(8,128)(2,1)S(1)}, u32[]{:S(2)}, u32[]{:S(2)}) %collective-permute-start.23) | collective-permute-done | bytes 262176 | tf_op jit(solution)/shard_map/ppermute | solution.py:253
  97.3 1.4 %collective-permute-start.24 = (bf16[4,64,256]{2,1,0:T(8,128)(2,1)S(1)}, bf16[4,64,256]{2,1,0:T(8,128)(2,1)S(1)}, u32[]{:S(2)}, u32[]{:S(2)}) collective-permute-start(bf16[4,64,256]{2,1,0:T(8,128)(2,1)S(1)} %add_convert_fusion), channel_id=1, source_target_pairs={{0,4},{2,6},{4,0},{6,2},{8,12},{10,14},{12,8},{14,10},{16,20},{18,... | collective-permute-start | bytes 393224 | tf_op jit(solution)/shard_map/ppermute | solution.py:253
  98.9 2.1 %collective-permute-start.18 = (bf16[128,256]{1,0:T(8,128)(2,1)S(1)}, bf16[128,256]{1,0:T(8,128)(2,1)S(1)}, u32[]{:S(2)}, u32[]{:S(2)}) collective-permute-start(bf16[128,256]{1,0:T(8,128)(2,1)S(1)} %get-tuple-element.36), channel_id=1, source_target_pairs={{0,24},{2,26},{4,28},{6,30},{8,0},{10,2},{12,4},{14,6},{16,8},{18,... | collective-permute-start | bytes 196616 | tf_op jit(solution)/shard_map/ppermute | solution.py:257
  101.0 0.8 collective-permute-start.19
  102.4 2.6 %collective-permute-start.25 = (bf16[128,256]{1,0:T(8,128)(2,1)S(1)}, bf16[128,256]{1,0:T(8,128)(2,1)S(1)}, u32[]{:S(2)}, u32[]{:S(2)}) collective-permute-start(bf16[128,256]{1,0:T(8,128)(2,1)S(1)} %get-tuple-element.39), channel_id=1, source_target_pairs={{0,24},{2,26},{4,28},{6,30},{8,0},{10,2},{12,4},{14,6},{16,8},{18,... | collective-permute-start | bytes 196616 | tf_op jit(solution)/shard_map/ppermute | solution.py:257
  105.0 0.6 collective-permute-start.27
  105.7 1.4 %collective-permute-start.26 = (bf16[128,256]{1,0:T(8,128)(2,1)S(1)}, bf16[128,256]{1,0:T(8,128)(2,1)S(1)}, u32[]{:S(2)}, u32[]{:S(2)}) collective-permute-start(bf16[128,256]{1,0:T(8,128)(2,1)S(1)} %get-tuple-element.41), channel_id=1, source_target_pairs={{0,16},{2,18},{4,20},{6,22},{8,24},{10,26},{12,28},{14,30},{16,0},... | collective-permute-start | bytes 196616 | tf_op jit(solution)/shard_map/ppermute | solution.py:257
  107.2 0.7 collective-permute-done.19
  108.0 3.2 %collective-permute-done.27 = bf16[128,256]{1,0:T(8,128)(2,1)S(1)} collective-permute-done((bf16[128,256]{1,0:T(8,128)(2,1)S(1)}, bf16[128,256]{1,0:T(8,128)(2,1)S(1)}, u32[]{:S(2)}, u32[]{:S(2)}) %collective-permute-start.27) | collective-permute-done | bytes 65568 | tf_op jit(solution)/shard_map/ppermute | solution.py:257
  111.2 1.0 collective-permute-done.26
  112.3 0.6 pad_maximum_fusion.11
  112.9 0.6 pad_maximum_fusion.10
  (63 shorter events, 2.5 us)
Async XLA Ops:
  1.5 8.6 %collective-permute-start.8 = (bf16[128,256]{1,0:T(8,128)(2,1)S(1)}, bf16[128,256]{1,0:T(8,128)(2,1)S(1)}, u32[]{:S(2)}, u32[]{:S(2)}) collective-permute-start(bf16[128,256]{1,0:T(8,128)(2,1)S(1)} %get-tuple-element.51), channel_id=1, source_target_pairs={{0,16},{2,18},{4,20},{6,22},{8,24},{10,26},{12,28},{14,30},{16,0},... | collective-permute-start | bytes 196616 | tf_op jit(solution)/shard_map/ppermute | solution.py:257
  5.6 7.8 %collective-permute-start.7 = (bf16[128,256]{1,0:T(8,128)(2,1)S(1)}, bf16[128,256]{1,0:T(8,128)(2,1)S(1)}, u32[]{:S(2)}, u32[]{:S(2)}) collective-permute-start(bf16[128,256]{1,0:T(8,128)(2,1)S(1)} %get-tuple-element.51), channel_id=1, source_target_pairs={{0,8},{2,10},{4,12},{6,14},{8,16},{10,18},{12,20},{14,22},{16,24},... | collective-permute-start | bytes 196616 | tf_op jit(solution)/shard_map/ppermute | solution.py:257
  7.2 6.2 %collective-permute-start.9 = (bf16[128,256]{1,0:T(8,128)(2,1)S(1)}, bf16[128,256]{1,0:T(8,128)(2,1)S(1)}, u32[]{:S(2)}, u32[]{:S(2)}) collective-permute-start(bf16[128,256]{1,0:T(8,128)(2,1)S(1)} %get-tuple-element.51), channel_id=1, source_target_pairs={{0,24},{2,26},{4,28},{6,30},{8,0},{10,2},{12,4},{14,6},{16,8},{18,... | collective-permute-start | bytes 196616 | tf_op jit(solution)/shard_map/ppermute | solution.py:257
  9.4 7.3 %collective-permute-start.1 = (bf16[128,256]{1,0:T(8,128)(2,1)S(1)}, bf16[128,256]{1,0:T(8,128)(2,1)S(1)}, u32[]{:S(2)}, u32[]{:S(2)}) collective-permute-start(bf16[128,256]{1,0:T(8,128)(2,1)S(1)} %get-tuple-element.57), channel_id=1, source_target_pairs={{0,16},{2,18},{4,20},{6,22},{8,24},{10,26},{12,28},{14,30},{16,0},... | collective-permute-start | bytes 196616 | tf_op jit(solution)/shard_map/ppermute | solution.py:257
  9.5 7.2 %collective-permute-start = (bf16[128,256]{1,0:T(8,128)(2,1)S(1)}, bf16[128,256]{1,0:T(8,128)(2,1)S(1)}, u32[]{:S(2)}, u32[]{:S(2)}) collective-permute-start(bf16[128,256]{1,0:T(8,128)(2,1)S(1)} %get-tuple-element.57), channel_id=1, source_target_pairs={{0,8},{2,10},{4,12},{6,14},{8,16},{10,18},{12,20},{14,22},{16,24},... | collective-permute-start | bytes 196616 | tf_op jit(solution)/shard_map/ppermute | solution.py:257
  10.0 6.9 %collective-permute-start.2 = (bf16[128,256]{1,0:T(8,128)(2,1)S(1)}, bf16[128,256]{1,0:T(8,128)(2,1)S(1)}, u32[]{:S(2)}, u32[]{:S(2)}) collective-permute-start(bf16[128,256]{1,0:T(8,128)(2,1)S(1)} %get-tuple-element.57), channel_id=1, source_target_pairs={{0,24},{2,26},{4,28},{6,30},{8,0},{10,2},{12,4},{14,6},{16,8},{18,... | collective-permute-start | bytes 196616 | tf_op jit(solution)/shard_map/ppermute | solution.py:257
  13.4 20.8 %copy-start = (bf16[256,4096]{1,0:T(8,128)(2,1)S(1)}, bf16[256,4096]{1,0:T(8,128)(2,1)}, u32[]{:S(2)}) copy-start(bf16[256,4096]{1,0:T(8,128)(2,1)} %q_ref.3) | copy-start | bytes 6291460
  13.4 20.9 %copy-start.1 = (s32[2,16]{1,0:T(2,128)S(1)}, s32[2,16]{1,0:T(2,128)}, u32[]{:S(2)}) copy-start(s32[2,16]{1,0:T(2,128)} %mask_ref.3) | copy-start | bytes 388
  13.4 20.8 %copy-start.2 = (s32[16]{0:T(128)S(1)}, s32[16]{0:T(128)}, u32[]{:S(2)}) copy-start(s32[16]{0:T(128)} %owner_ref.3) | copy-start | bytes 196
  13.5 5.3 %collective-permute-start.12 = (bf16[4,64,256]{2,1,0:T(8,128)(2,1)S(1)}, bf16[4,64,256]{2,1,0:T(8,128)(2,1)S(1)}, u32[]{:S(2)}, u32[]{:S(2)}) collective-permute-start(bf16[4,64,256]{2,1,0:T(8,128)(2,1)S(1)} %get-tuple-element.42.v_own), channel_id=1, source_target_pairs={{0,4},{2,6},{4,0},{6,2},{8,12},{10,14},{12,8},{14,10},{16,20},{18,... | collective-permute-start | bytes 393224 | tf_op jit(solution)/shard_map/ppermute | solution.py:253
  15.1 5.9 %collective-permute-start.10 = (bf16[4,64,256]{2,1,0:T(8,128)(2,1)S(1)}, bf16[4,64,256]{2,1,0:T(8,128)(2,1)S(1)}, u32[]{:S(2)}, u32[]{:S(2)}) collective-permute-start(bf16[4,64,256]{2,1,0:T(8,128)(2,1)S(1)} %get-tuple-element.43.k_own), channel_id=1, source_target_pairs={{0,2},{2,0},{4,6},{6,4},{8,10},{10,8},{12,14},{14,12},{16,18},{18,... | collective-permute-start | bytes 393224 | tf_op jit(solution)/shard_map/ppermute | solution.py:253
  17.0 6.6 %collective-permute-start.5 = (bf16[4,64,256]{2,1,0:T(8,128)(2,1)S(1)}, bf16[4,64,256]{2,1,0:T(8,128)(2,1)S(1)}, u32[]{:S(2)}, u32[]{:S(2)}) collective-permute-start(bf16[4,64,256]{2,1,0:T(8,128)(2,1)S(1)} %get-tuple-element.44.v_own), channel_id=1, source_target_pairs={{0,4},{2,6},{4,0},{6,2},{8,12},{10,14},{12,8},{14,10},{16,20},{18,... | collective-permute-start | bytes 393224 | tf_op jit(solution)/shard_map/ppermute | solution.py:253
  19.5 14.7 %collective-permute-start.13 = (bf16[8,64,256]{2,1,0:T(8,128)(2,1)}, bf16[8,64,256]{2,1,0:T(8,128)(2,1)}, u32[]{:S(2)}, u32[]{:S(2)}) collective-permute-start(bf16[8,64,256]{2,1,0:T(8,128)(2,1)} %pad_maximum_fusion.7), channel_id=1, source_target_pairs={{0,2},{2,0},{4,6},{6,4},{8,10},{10,8},{12,14},{14,12},{16,18},{18,... | collective-permute-start | bytes 786440 | tf_op jit(solution)/shard_map/ppermute | solution.py:253
  21.7 12.5 %collective-permute-start.11 = (bf16[8,64,256]{2,1,0:T(8,128)(2,1)}, bf16[8,64,256]{2,1,0:T(8,128)(2,1)}, u32[]{:S(2)}, u32[]{:S(2)}) collective-permute-start(bf16[8,64,256]{2,1,0:T(8,128)(2,1)} %pad_maximum_fusion.6), channel_id=1, source_target_pairs={{0,4},{2,6},{4,0},{6,2},{8,12},{10,14},{12,8},{14,10},{16,20},{18,... | collective-permute-start | bytes 786440 | tf_op jit(solution)/shard_map/ppermute | solution.py:253
  23.0 8.8 %collective-permute-start.3 = (bf16[4,64,256]{2,1,0:T(8,128)(2,1)S(1)}, bf16[4,64,256]{2,1,0:T(8,128)(2,1)S(1)}, u32[]{:S(2)}, u32[]{:S(2)}) collective-permute-start(bf16[4,64,256]{2,1,0:T(8,128)(2,1)S(1)} %get-tuple-element.45.k_own), channel_id=1, source_target_pairs={{0,2},{2,0},{4,6},{6,4},{8,10},{10,8},{12,14},{14,12},{16,18},{18,... | collective-permute-start | bytes 393224 | tf_op jit(solution)/shard_map/ppermute | solution.py:253
  24.3 28.3 %collective-permute-start.6 = (bf16[8,64,256]{2,1,0:T(8,128)(2,1)}, bf16[8,64,256]{2,1,0:T(8,128)(2,1)S(1)}, u32[]{:S(2)}, u32[]{:S(2)}) collective-permute-start(bf16[8,64,256]{2,1,0:T(8,128)(2,1)} %pad_maximum_fusion.4), channel_id=1, source_target_pairs={{0,2},{2,0},{4,6},{6,4},{8,10},{10,8},{12,14},{14,12},{16,18},{18,... | collective-permute-start | bytes 786440 | tf_op jit(solution)/shard_map/ppermute | solution.py:253
  32.5 20.1 %collective-permute-start.4 = (bf16[8,64,256]{2,1,0:T(8,128)(2,1)}, bf16[8,64,256]{2,1,0:T(8,128)(2,1)}, u32[]{:S(2)}, u32[]{:S(2)}) collective-permute-start(bf16[8,64,256]{2,1,0:T(8,128)(2,1)} %pad_maximum_fusion.3), channel_id=1, source_target_pairs={{0,4},{2,6},{4,0},{6,2},{8,12},{10,14},{12,8},{14,10},{16,20},{18,... | collective-permute-start | bytes 786440 | tf_op jit(solution)/shard_map/ppermute | solution.py:253
  51.6 36.9 %collective-permute-start.14 = (bf16[8,64,256]{2,1,0:T(8,128)(2,1)S(1)}, bf16[8,64,256]{2,1,0:T(8,128)(2,1)S(1)}, u32[]{:S(2)}, u32[]{:S(2)}) collective-permute-start(bf16[8,64,256]{2,1,0:T(8,128)(2,1)S(1)} %get-tuple-element.23), channel_id=1, source_target_pairs={{0,4},{2,6},{4,0},{6,2},{8,12},{10,14},{12,8},{14,10},{16,20},{18,... | collective-permute-start | bytes 786440 | tf_op jit(solution)/shard_map/ppermute | solution.py:253
  69.9 1.2 %collective-permute-start.28 = (f32[8,128]{1,0:T(8,128)S(1)}, f32[8,128]{1,0:T(8,128)S(1)}, u32[]{:S(2)}, u32[]{:S(2)}) collective-permute-start(f32[8,128]{1,0:T(8,128)S(1)} %add.93), channel_id=1, source_target_pairs={{0,1},{1,0},{2,3},{3,2},{4,5},{5,4},{6,7},{7,6},{8,9},{9,8},{10,11... | collective-permute-start | bytes 12296 | tf_op jit(solution)/shard_map/ppermute | solution.py:304
  71.1 3.6 %collective-permute-start.29 = (f32[8,128]{1,0:T(8,128)S(1)}, f32[8,128]{1,0:T(8,128)S(1)}, u32[]{:S(2)}, u32[]{:S(2)}) collective-permute-start(f32[8,128]{1,0:T(8,128)S(1)} %add.94), channel_id=1, source_target_pairs={{0,2},{2,0},{4,6},{6,4},{8,10},{10,8},{12,14},{14,12},{16,18},{18,... | collective-permute-start | bytes 12296 | tf_op jit(solution)/shard_map/ppermute | solution.py:253
  74.7 3.6 %collective-permute-start.30 = (f32[8,128]{1,0:T(8,128)S(1)}, f32[8,128]{1,0:T(8,128)S(1)}, u32[]{:S(2)}, u32[]{:S(2)}) collective-permute-start(f32[8,128]{1,0:T(8,128)S(1)} %add.95), channel_id=1, source_target_pairs={{0,4},{2,6},{4,0},{6,2},{8,12},{10,14},{12,8},{14,10},{16,20},{18,... | collective-permute-start | bytes 12296 | tf_op jit(solution)/shard_map/ppermute | solution.py:253
  78.3 6.8 %collective-permute-start.33 = (f32[8,128]{1,0:T(8,128)S(1)}, f32[8,128]{1,0:T(8,128)S(1)}, u32[]{:S(2)}, u32[]{:S(2)}) collective-permute-start(f32[8,128]{1,0:T(8,128)S(1)} %add.96), channel_id=1, source_target_pairs={{0,24},{2,26},{4,28},{6,30},{8,0},{10,2},{12,4},{14,6},{16,8},{18,... | collective-permute-start | bytes 12296 | tf_op jit(solution)/shard_map/ppermute | solution.py:257
  81.3 5.2 %collective-permute-start.32 = (f32[8,128]{1,0:T(8,128)S(1)}, f32[8,128]{1,0:T(8,128)S(1)}, u32[]{:S(2)}, u32[]{:S(2)}) collective-permute-start(f32[8,128]{1,0:T(8,128)S(1)} %add.96), channel_id=1, source_target_pairs={{0,16},{2,18},{4,20},{6,22},{8,24},{10,26},{12,28},{14,30},{16,0},... | collective-permute-start | bytes 12296 | tf_op jit(solution)/shard_map/ppermute | solution.py:257
  81.6 5.7 %collective-permute-start.31 = (f32[8,128]{1,0:T(8,128)S(1)}, f32[8,128]{1,0:T(8,128)S(1)}, u32[]{:S(2)}, u32[]{:S(2)}) collective-permute-start(f32[8,128]{1,0:T(8,128)S(1)} %add.96), channel_id=1, source_target_pairs={{0,8},{2,10},{4,12},{6,14},{8,16},{10,18},{12,20},{14,22},{16,24},... | collective-permute-start | bytes 12296 | tf_op jit(solution)/shard_map/ppermute | solution.py:257
  83.6 9.2 %collective-permute-start.16 = (bf16[8,64,256]{2,1,0:T(8,128)(2,1)S(1)}, bf16[8,64,256]{2,1,0:T(8,128)(2,1)S(1)}, u32[]{:S(2)}, u32[]{:S(2)}) collective-permute-start(bf16[8,64,256]{2,1,0:T(8,128)(2,1)S(1)} %get-tuple-element.26), channel_id=1, source_target_pairs={{0,2},{2,0},{4,6},{6,4},{8,10},{10,8},{12,14},{14,12},{16,18},{18,... | collective-permute-start | bytes 786440 | tf_op jit(solution)/shard_map/ppermute | solution.py:253
  85.1 9.2 %collective-permute-start.21 = (bf16[8,64,256]{2,1,0:T(8,128)(2,1)S(1)}, bf16[8,64,256]{2,1,0:T(8,128)(2,1)S(1)}, u32[]{:S(2)}, u32[]{:S(2)}) collective-permute-start(bf16[8,64,256]{2,1,0:T(8,128)(2,1)S(1)} %get-tuple-element.29), channel_id=1, source_target_pairs={{0,4},{2,6},{4,0},{6,2},{8,12},{10,14},{12,8},{14,10},{16,20},{18,... | collective-permute-start | bytes 786440 | tf_op jit(solution)/shard_map/ppermute | solution.py:253
  86.5 10.7 %collective-permute-start.23 = (bf16[8,64,256]{2,1,0:T(8,128)(2,1)S(1)}, bf16[8,64,256]{2,1,0:T(8,128)(2,1)S(1)}, u32[]{:S(2)}, u32[]{:S(2)}) collective-permute-start(bf16[8,64,256]{2,1,0:T(8,128)(2,1)S(1)} %get-tuple-element.32), channel_id=1, source_target_pairs={{0,2},{2,0},{4,6},{6,4},{8,10},{10,8},{12,14},{14,12},{16,18},{18,... | collective-permute-start | bytes 786440 | tf_op jit(solution)/shard_map/ppermute | solution.py:253
  88.5 10.2 %collective-permute-start.15 = (bf16[4,64,256]{2,1,0:T(8,128)(2,1)S(1)}, bf16[4,64,256]{2,1,0:T(8,128)(2,1)S(1)}, u32[]{:S(2)}, u32[]{:S(2)}) collective-permute-start(bf16[4,64,256]{2,1,0:T(8,128)(2,1)S(1)} %add_convert_fusion.3), channel_id=1, source_target_pairs={{0,2},{2,0},{4,6},{6,4},{8,10},{10,8},{12,14},{14,12},{16,18},{18,... | collective-permute-start | bytes 393224 | tf_op jit(solution)/shard_map/ppermute | solution.py:253
  92.9 5.9 %collective-permute-start.17 = (bf16[4,64,256]{2,1,0:T(8,128)(2,1)S(1)}, bf16[4,64,256]{2,1,0:T(8,128)(2,1)S(1)}, u32[]{:S(2)}, u32[]{:S(2)}) collective-permute-start(bf16[4,64,256]{2,1,0:T(8,128)(2,1)S(1)} %add_convert_fusion.2), channel_id=1, source_target_pairs={{0,4},{2,6},{4,0},{6,2},{8,12},{10,14},{12,8},{14,10},{16,20},{18,... | collective-permute-start | bytes 393224 | tf_op jit(solution)/shard_map/ppermute | solution.py:253
  94.3 7.5 %collective-permute-start.22 = (bf16[4,64,256]{2,1,0:T(8,128)(2,1)S(1)}, bf16[4,64,256]{2,1,0:T(8,128)(2,1)S(1)}, u32[]{:S(2)}, u32[]{:S(2)}) collective-permute-start(bf16[4,64,256]{2,1,0:T(8,128)(2,1)S(1)} %add_convert_fusion.1), channel_id=1, source_target_pairs={{0,2},{2,0},{4,6},{6,4},{8,10},{10,8},{12,14},{14,12},{16,18},{18,... | collective-permute-start | bytes 393224 | tf_op jit(solution)/shard_map/ppermute | solution.py:253
  97.3 5.0 %collective-permute-start.24 = (bf16[4,64,256]{2,1,0:T(8,128)(2,1)S(1)}, bf16[4,64,256]{2,1,0:T(8,128)(2,1)S(1)}, u32[]{:S(2)}, u32[]{:S(2)}) collective-permute-start(bf16[4,64,256]{2,1,0:T(8,128)(2,1)S(1)} %add_convert_fusion), channel_id=1, source_target_pairs={{0,4},{2,6},{4,0},{6,2},{8,12},{10,14},{12,8},{14,10},{16,20},{18,... | collective-permute-start | bytes 393224 | tf_op jit(solution)/shard_map/ppermute | solution.py:253
  98.9 6.8 %collective-permute-start.18 = (bf16[128,256]{1,0:T(8,128)(2,1)S(1)}, bf16[128,256]{1,0:T(8,128)(2,1)S(1)}, u32[]{:S(2)}, u32[]{:S(2)}) collective-permute-start(bf16[128,256]{1,0:T(8,128)(2,1)S(1)} %get-tuple-element.36), channel_id=1, source_target_pairs={{0,24},{2,26},{4,28},{6,30},{8,0},{10,2},{12,4},{14,6},{16,8},{18,... | collective-permute-start | bytes 196616 | tf_op jit(solution)/shard_map/ppermute | solution.py:257
  101.0 6.2 %collective-permute-start.20 = (bf16[128,256]{1,0:T(8,128)(2,1)S(1)}, bf16[128,256]{1,0:T(8,128)(2,1)S(1)}, u32[]{:S(2)}, u32[]{:S(2)}) collective-permute-start(bf16[128,256]{1,0:T(8,128)(2,1)S(1)} %get-tuple-element.37), channel_id=1, source_target_pairs={{0,8},{2,10},{4,12},{6,14},{8,16},{10,18},{12,20},{14,22},{16,24},... | collective-permute-start | bytes 196616 | tf_op jit(solution)/shard_map/ppermute | solution.py:257
  101.0 6.9 %collective-permute-start.19 = (bf16[128,256]{1,0:T(8,128)(2,1)S(1)}, bf16[128,256]{1,0:T(8,128)(2,1)S(1)}, u32[]{:S(2)}, u32[]{:S(2)}) collective-permute-start(bf16[128,256]{1,0:T(8,128)(2,1)S(1)} %get-tuple-element.38), channel_id=1, source_target_pairs={{0,16},{2,18},{4,20},{6,22},{8,24},{10,26},{12,28},{14,30},{16,0},... | collective-permute-start | bytes 196616 | tf_op jit(solution)/shard_map/ppermute | solution.py:257
  102.4 5.5 %collective-permute-start.25 = (bf16[128,256]{1,0:T(8,128)(2,1)S(1)}, bf16[128,256]{1,0:T(8,128)(2,1)S(1)}, u32[]{:S(2)}, u32[]{:S(2)}) collective-permute-start(bf16[128,256]{1,0:T(8,128)(2,1)S(1)} %get-tuple-element.39), channel_id=1, source_target_pairs={{0,24},{2,26},{4,28},{6,30},{8,0},{10,2},{12,4},{14,6},{16,8},{18,... | collective-permute-start | bytes 196616 | tf_op jit(solution)/shard_map/ppermute | solution.py:257
  105.0 6.2 %collective-permute-start.27 = (bf16[128,256]{1,0:T(8,128)(2,1)S(1)}, bf16[128,256]{1,0:T(8,128)(2,1)S(1)}, u32[]{:S(2)}, u32[]{:S(2)}) collective-permute-start(bf16[128,256]{1,0:T(8,128)(2,1)S(1)} %get-tuple-element.40), channel_id=1, source_target_pairs={{0,8},{2,10},{4,12},{6,14},{8,16},{10,18},{12,20},{14,22},{16,24},... | collective-permute-start | bytes 196616 | tf_op jit(solution)/shard_map/ppermute | solution.py:257
  105.7 6.6 %collective-permute-start.26 = (bf16[128,256]{1,0:T(8,128)(2,1)S(1)}, bf16[128,256]{1,0:T(8,128)(2,1)S(1)}, u32[]{:S(2)}, u32[]{:S(2)}) collective-permute-start(bf16[128,256]{1,0:T(8,128)(2,1)S(1)} %get-tuple-element.41), channel_id=1, source_target_pairs={{0,16},{2,18},{4,20},{6,22},{8,24},{10,26},{12,28},{14,30},{16,0},... | collective-permute-start | bytes 196616 | tf_op jit(solution)/shard_map/ppermute | solution.py:257

commit v2 on v1

v2 whole, which is shorter than its diff:
```python
import functools
import math

import jax
import jax.numpy as jnp
from jax import lax
from jax.experimental import pallas as pl
from jax.experimental.pallas import tpu as pltpu
from jax.sharding import PartitionSpec as P

HD = 128
BLK = 128
PAIR = 4
UNROLL = 2
CHUNKS = 2
CODE = 16
NT = (((1,), (1,)), ((), ()))
F32, BF16 = jnp.float32, jnp.bfloat16


def coded(value, rows, rounded):
    high = rounded(value)
    middle = rounded(value - high)
    low = value - high - middle
    shape = (rows, value.shape[1])
    row = lax.broadcasted_iota(jnp.int32, shape, 0)
    parts = jnp.where(row == 0, high, jnp.zeros(shape, F32))
    return jnp.where(row == 1, middle, jnp.where(row == 2, low, parts)).astype(BF16)


def rounded_here(value):
    return value.astype(BF16).astype(F32)


def rounded_outside(value):
    return lax.reduce_precision(value, 8, 7)


def decoded(rows):
    rows = rows.astype(F32)
    return rows[0:1] + rows[1:2] + rows[2:3]


def attention_kernel(n, two_step, n_extra, *refs):
    mask_ref, owner_ref, me_ref, gate_ref, gate_in, q_ref, cot_ref = refs[:7]
    k_cols, v_cols = refs[7:11], refs[11:15]
    refs = refs[15 + n_extra :]
    n_out = 6 if two_step else 5
    dq_ref, own_ref = refs[:2]
    back_refs = refs[2:n_out]
    (
        gate_out,
        k_all,
        v_all,
        k_sel,
        v_sel,
        kt_sel,
        dk_acc,
        dv_acc,
        dk_all,
        dv_all,
        gate_acc,
        place,
        bias,
    ) = refs[n_out:]
    n_blocks, n_images = mask_ref.shape
    img_tok = k_all.shape[1]
    read_most = n_images // 2
    groups = q_ref.shape[1] // HD
    step = pl.program_id(0)
    gate_value = gate_ref[0]
    inv_root = 1.0 / math.sqrt(HD)
    to_exp2 = math.log2(math.e) * inv_root

    @pl.when(step == 0)
    def _():
        gate_acc[...] = jnp.zeros_like(gate_acc)
        gate_acc[0:1, 0:HD] = gate_in[0:1, :]
        me = me_ref[0]
        for j in range(read_most):
            place[j] = 0
            for b in range(n_blocks):
                bias[b, j] = jnp.float32(-1e30)

        def look(i, count):
            reads = [mask_ref[b, i] > 0 for b in range(n_blocks)]
            any_read = functools.reduce(jnp.logical_or, reads)

            @pl.when(jnp.logical_and(any_read, count < read_most))
            def _():
                slot = owner_ref[i]
                column = jnp.bitwise_xor(lax.rem(slot, 4), lax.rem(me, 4))
                behind = lax.rem(lax.div(me, 4) - lax.div(slot, 4) + n, n)
                place[count] = column * n + behind
                for b in range(n_blocks):
                    bias[b, count] = jnp.where(reads[b], 0.0, -1e30).astype(F32)

            return count + any_read.astype(jnp.int32)

        lax.fori_loop(0, n_images, look, jnp.int32(0))

    for a in range(4):
        k_all[a * n : (a + 1) * n] = k_cols[a][...]
        v_all[a * n : (a + 1) * n] = v_cols[a][...]
    for j in range(read_most):
        rows = slice(j * img_tok, (j + 1) * img_tok)
        k_sel[rows] = k_all[place[j]]
        v_sel[rows] = v_all[place[j]]
    kt_sel[...] = k_sel[...].astype(F32).T.astype(BF16)
    dk_acc[...] = jnp.zeros_like(dk_acc)
    dv_acc[...] = jnp.zeros_like(dv_acc)

    pairs = groups // PAIR

    def one(it, carry):
        b = it // pairs
        g = it % pairs
        rows = pl.ds(pl.multiple_of(b * BLK, BLK), BLK)

        def heads_of(ref):
            return jnp.concatenate(
                [
                    ref[rows, pl.ds(pl.multiple_of((g * PAIR + u) * HD, HD), HD)]
                    for u in range(PAIR)
                ],
                axis=0,
            )

        query = heads_of(q_ref)
        cot = heads_of(cot_ref)
        scores = lax.dot_general(k_sel[...], query, NT, preferred_element_type=F32)
        scores = jnp.concatenate(
            [scores[j * img_tok : (j + 1) * img_tok] + bias[b, j] for j in range(read_most)],
            axis=0,
        )
        row_max = jnp.max(scores, axis=0, keepdims=True)
        terms = jnp.exp2((scores - row_max) * to_exp2)
        prob = terms * (1.0 / jnp.sum(terms, axis=0, keepdims=True))
        prob_half = prob.astype(BF16)
        prob_grad = lax.dot_general(v_sel[...], cot, NT, preferred_element_type=F32)
        delta = jnp.sum(prob_half.astype(F32) * prob_grad, axis=0, keepdims=True)
        score_grad = (prob * (prob_grad - delta)).astype(BF16)
        dq_t = jnp.dot(kt_sel[...], score_grad, preferred_element_type=F32)
        dq = (dq_t.T * (gate_value * inv_root)).astype(BF16)
        for u in range(PAIR):
            lanes = pl.ds(pl.multiple_of((g * PAIR + u) * HD, HD), HD)
            dq_ref[rows, lanes] = dq[u * BLK : (u + 1) * BLK]
        dk_acc[...] += jnp.dot(score_grad, query, preferred_element_type=F32)
        dv_acc[...] += jnp.dot(prob_half, cot, preferred_element_type=F32)
        gate_acc[0:1, :] += delta
        return carry

    lax.fori_loop(0, n_blocks * pairs, one, 0, unroll=UNROLL)

    dk_all[...] = jnp.zeros_like(dk_all)
    dv_all[...] = jnp.zeros_like(dv_all)
    for j in range(read_most):
        rows = slice(j * img_tok, (j + 1) * img_tok)
        dk_all[place[j]] = dk_acc[rows] * (gate_value * inv_root)
        dv_all[place[j]] = dv_acc[rows] * gate_value
    own_ref[:, :img_tok] = dk_all[0:n]
    own_ref[:, img_tok:] = dv_all[0:n]
    gate_row = sum(gate_acc[0:1, u * HD : (u + 1) * HD] for u in range(PAIR))
    gate_out[...] = jnp.broadcast_to(gate_row, gate_out.shape)
    if two_step:
        dk_x, dk_yd, dv_y, dv_xd = back_refs
        rest = 2 * n * img_tok
        dk_x[...] = dk_all[n : 2 * n]
        dk_yd[:rest] = dk_all[2 * n :].astype(BF16).reshape(rest, HD)
        last = step == pl.num_programs(0) - 1
        dk_yd[rest:] = coded(jnp.where(last, gate_row, 0.0), CODE, rounded_here)
        dv_y[...] = dv_all[2 * n : 3 * n]
        dv_xd[0:n] = dv_all[n : 2 * n].astype(BF16)
        dv_xd[n:] = dv_all[3 * n :].astype(BF16)
    else:
        for a in range(1, 4):
            back_refs[a - 1][:, :img_tok] = dk_all[a * n : (a + 1) * n].astype(BF16)
            back_refs[a - 1][:, img_tok:] = dv_all[a * n : (a + 1) * n].astype(BF16)


def attention(first, heads, n, two_step, prev_dq, gate_in, scalars, queries, cotangent, keys, values):
    tokens = queries.shape[0]
    total_kv = scalars[4]
    n_images = scalars[0].shape[1]
    img_tok = scalars[5]
    groups = queries.shape[1] // HD // total_kv
    width = groups * HD
    n_keys = n_images // 2 * img_tok
    smem = pl.BlockSpec(memory_space=pltpu.SMEM)
    wide = pl.BlockSpec((tokens, width), lambda i: (0, first + i))
    small = pl.BlockSpec((8, HD), lambda i: (0, 0))

    def cols(shape, place=(0, 0)):
        return pl.BlockSpec((*shape, HD), lambda i: (*place, i))

    in_specs = [smem] * 4 + [small, wide, wide]
    args = [*scalars[:4], gate_in, queries, cotangent]
    for array, place in (*keys, *values):
        in_specs.append(cols((n, img_tok), place))
        args.append(array)
    aliases = {}
    if prev_dq is not None:
        aliases[len(args)] = 0
        in_specs.append(pl.BlockSpec(memory_space=pl.ANY))
        args.append(prev_dq)
    span = heads * HD
    outs = [((n, 2 * img_tok), F32)]
    if two_step:
        outs += [((n, img_tok), F32), ((2 * n * img_tok + CODE,), BF16)]
        outs += [((n, img_tok), F32), ((2 * n, img_tok), BF16)]
    else:
        outs += [((n, 2 * img_tok), BF16)] * 3
    out_shape = [jax.ShapeDtypeStruct(queries.shape, BF16)]
    out_shape += [jax.ShapeDtypeStruct((*shape, span), kind) for shape, kind in outs]
    out_shape.append(jax.ShapeDtypeStruct((8, HD), F32))
    out_specs = [wide] + [cols(shape, (0,) * len(shape)) for shape, kind in outs] + [small]
    rows = tokens * groups * heads
    return pl.pallas_call(
        functools.partial(attention_kernel, n, two_step, len(aliases)),
        grid=(heads,),
        in_specs=in_specs,
        out_specs=out_specs,
        out_shape=out_shape,
        input_output_aliases=aliases,
        scratch_shapes=[
            pltpu.VMEM((4 * n, img_tok, HD), BF16),
            pltpu.VMEM((4 * n, img_tok, HD), BF16),
            pltpu.VMEM((n_keys, HD), BF16),
            pltpu.VMEM((n_keys, HD), BF16),
            pltpu.VMEM((HD, n_keys), BF16),
            pltpu.VMEM((n_keys, HD), F32),
            pltpu.VMEM((n_keys, HD), F32),
            pltpu.VMEM((4 * n, img_tok, HD), F32),
            pltpu.VMEM((4 * n, img_tok, HD), F32),
            pltpu.VMEM((8, PAIR * BLK), F32),
            pltpu.SMEM((n_images // 2,), jnp.int32),
            pltpu.SMEM((scalars[0].shape[0], n_images // 2), F32),
        ],
        compiler_params=pltpu.CompilerParams(
            dimension_semantics=("arbitrary",),
            vmem_limit_bytes=(14 + 16 * n_keys // 1024) * 1024 * 1024,
        ),
        cost_estimate=pl.CostEstimate(
            flops=10 * rows * n_keys * HD,
            bytes_accessed=6 * rows * HD,
            transcendentals=rows * n_keys,
        ),
        name="attention_backward",
    )(*args)


def per_device(queries, cotangent, image_keys, image_values, attn_gate, block_mask, image_owner):
    n_ctx = lax.axis_size("ctx")
    n_tp = lax.axis_size("tp")
    n = n_ctx // 4
    img_tok = image_keys.shape[1]
    local_kv = image_keys.shape[2] // HD
    chunks = min(CHUNKS, local_kv)
    heads = local_kv // chunks
    me = lax.axis_index("ctx").astype(jnp.int32).reshape(1)
    gate_value = jnp.tanh(attn_gate)

    def swap(value, bit):
        return lax.ppermute(value, "ctx", [(i, i ^ bit) for i in range(n_ctx)])

    def turn(value, by):
        pairs = [(i, (i // 4 + by) % n * 4 + i % 4) for i in range(n_ctx)]
        return lax.ppermute(value, "ctx", pairs)

    def fetch_column(c):
        lanes = slice(c * heads * HD, (c + 1) * heads * HD)
        own = jnp.concatenate([image_keys[0, :, lanes], image_values[0, :, lanes]], axis=0)
        return jnp.stack([own] + [turn(own, k) for k in range(1, n)])

    def fetch_two_step(column):
        k_own, v_own = column[:, :img_tok], column[:, img_tok:]
        k_x, v_y = swap(k_own, 1), swap(v_own, 2)
        k_yd = swap(jnp.concatenate([k_own, k_x]), 2)
        v_xd = swap(jnp.concatenate([v_own, v_y]), 1)
        first, second = (0, 0), (1, 0)
        keys = [(column, (0, 0)), (k_x, first), (k_yd, first), (k_yd, second)]
        values = [(column, (0, 1)), (v_xd, first), (v_y, first), (v_xd, second)]
        return keys, values

    def fetch_direct(column):
        columns = [column, swap(column, 1), swap(column, 2), swap(column, 3)]
        return [(part, (0, 0)) for part in columns], [(part, (0, 1)) for part in columns]

    def return_direct(own, backs):
        total = own
        for a, back in enumerate(backs):
            total = total + swap(back, a + 1).astype(F32)
        return total, None

    def return_two_step(own, backs):
        dk_x, dk_yd, dv_y, dv_xd = backs
        rest = 2 * n * img_tok
        width = own.shape[2]
        k_back, v_back = swap(dk_yd, 2), swap(dv_xd, 1)
        gate = decoded(dk_yd[rest:]) + decoded(k_back[rest:])
        k_back = k_back[:rest].reshape(2 * n, img_tok, width)
        k_send = (dk_x + k_back[n:].astype(F32)).astype(BF16).reshape(n * img_tok, width)
        v_send = (dv_y + v_back[n:].astype(F32)).astype(BF16)
        k_last = swap(jnp.concatenate([k_send, coded(gate, CODE, rounded_outside)]), 1)
        v_last = swap(v_send, 2)
        gate = gate + decoded(k_last[n * img_tok :])
        k_last = k_last[: n * img_tok].reshape(n, img_tok, width)
        k_sum = own[:, :img_tok] + k_back[:n].astype(F32) + k_last.astype(F32)
        v_sum = own[:, img_tok:] + v_back[:n].astype(F32) + v_last.astype(F32)
        return jnp.concatenate([k_sum, v_sum], axis=1), gate

    def return_column(both, gate):
        total, gate_total = both[0], gate
        sends = both.astype(BF16)
        for k in range(1, n):
            send = sends[k]
            if gate is not None:
                send = jnp.concatenate([send, coded(gate, CODE, rounded_outside)])
            came = turn(send, -k)
            total = total + came[: 2 * img_tok].astype(F32)
            if gate is not None:
                gate_total = gate_total + decoded(came[2 * img_tok :])
        return total, gate_total

    columns = [fetch_column(c) for c in range(chunks)]
    gathered = [(fetch_two_step if c == 0 else fetch_direct)(columns[c]) for c in range(chunks)]
    scalars = (block_mask, image_owner, me, gate_value, local_kv, img_tok)
    dq, gate_part = None, jnp.zeros((8, HD), F32)
    parts = []
    for c in range(chunks):
        last = c == chunks - 1
        keys, values = gathered[c]
        dq, own, *backs, gate_part = attention(
            c * heads, heads, n, last, dq, gate_part, scalars, queries, cotangent, keys, values
        )
        sums = return_two_step(own, backs) if last else return_direct(own, backs)
        total, gate_row = return_column(*sums)
        parts.append(total.astype(BF16))
    grads = jnp.concatenate(parts, axis=1)
    key_grad, value_grad = grads[None, :img_tok], grads[None, img_tok:]
    gate_total = gate_row
    for k in range(1, n_tp):
        pairs = [(i, (i + k) % n_tp) for i in range(n_tp)]
        gate_total = gate_total + lax.ppermute(gate_row, "tp", pairs)
    term_count = queries.shape[0] * n_ctx * queries.shape[1] * n_tp
    gate_grad = (1.0 - gate_value * gate_value) * jnp.sum(gate_total) / math.sqrt(term_count)
    return (dq, key_grad, value_grad, gate_grad)


def solution(mesh):
    in_specs = (
        P("ctx", "tp"),
        P("ctx", "tp"),
        P("ctx", None, "tp"),
        P("ctx", None, "tp"),
        P(),
        P("ctx", None),
        P(),
    )
    out_specs = (P("ctx", "tp"), P("ctx", None, "tp"), P("ctx", None, "tp"), P())
    return jax.shard_map(
        per_device, mesh=mesh, in_specs=in_specs, out_specs=out_specs, check_vma=False
    )
```

time: 115 us -> 89.5 us (0.78)
  starting transfers between devices: 48.4 us -> 32.2 us
  Pallas kernels: 34.6 us -> 25 us
  other arithmetic: 4.74 us -> 3.49 us
  local copies, waits for them, and re-layouts: 1.43 us -> 2.65 us
    pallas_call x2, Pallas kernels: 34.6 us -> 25 us  [attention(): pl.pallas_call(functools.partial(attention_kernel, n, two_step, len(alias...]
    ppermute x18 -> x14, starting transfers between devices: 23.7 us -> 14.1 us  [swap(): return lax.ppermute(value, 'ctx', [(i, i ^ bit) for i in range(n_ctx)])]
    ppermute x15 -> x12, starting transfers between devices: 24.8 us -> 18 us  [turn(): return lax.ppermute(value, 'ctx', pairs)]
    ppermute x15 -> x12, waiting for transfers between devices: 5.48 us -> 8.64 us  [turn(): return lax.ppermute(value, 'ctx', pairs)]
    concatenate x6 -> x4, other arithmetic: 4.21 us -> 1.49 us  [the longest x1 0.74 us: fetch_two_step(): v_xd = swap(jnp.concatenate([v_own, v_y]), 1)]
    ppermute x18 -> x14, waiting for transfers between devices: 15.5 us -> 13.5 us  [swap(): return lax.ppermute(value, 'ctx', [(i, i ^ bit) for i in range(n_ctx)])]
    unnamed x6 -> x8, local copies, waits for them, and re-layouts: 0.02 us -> 1.6 us
  transfers between devices with their start and end apart: 34 -> 27, of which waited for: 13 -> 11; matrix products, arithmetic and copies ran while one was open for 4% -> 3% of each run, Pallas kernels for 30% -> 28%
where the time goes in v2:
time: 89.5 us; the launch traced here: 89.3 us
  starting transfers between devices  32.2 us (36%)
  Pallas kernels  25 us (28%)
  waiting for transfers between devices  22.6 us (25%)
  other arithmetic  3.49 us (4%)
  between operations  3.35 us (4%)
  local copies, waits for them, and re-layouts  2.65 us (3%)
    pallas_call x2, Pallas kernels, attention(): pl.pallas_call(functools.partial(attention_kernel, n, two_step, len(alias...  25 us
    ppermute x12, starting transfers between devices, turn(): return lax.ppermute(value, 'ctx', pairs)  18 us
    ppermute x14, starting transfers between devices, swap(): return lax.ppermute(value, 'ctx', [(i, i ^ bit) for i in range(n_ctx)])  14.1 us
    ppermute x14, waiting for transfers between devices, swap(): return lax.ppermute(value, 'ctx', [(i, i ^ bit) for i in range(n_ctx)])  13.5 us
    ppermute x12, waiting for transfers between devices, turn(): return lax.ppermute(value, 'ctx', pairs)  8.64 us
  transfers between devices with their start and end apart: 27, of which 11 were waited for; matrix products, arithmetic and copies ran while one was open for 3% of the time, Pallas kernels for 28%

profile of v2, /device:TPU:0, one launch (start us, length us, event | category | flops | bytes accessed | tf_op | source)
XLA Modules:
  0.0 89.3 jit_solution(10776629998570471272)
XLA Ops:
  0.7 1.0 %slice_bitcast_fusion.7 = (bf16[64,256]{1,0:T(8,128)(2,1)S(1)}, bf16[64,256]{1,0:T(8,128)(2,1)S(1)}, bf16[64,256]{1,0:T(8,128)(2,1)S(1)}, bf16[64,256]{1,0:T(8,128)(2,1)S(1)}) fusion(bf16[1,64,512]{2,1,0:T(8,128)(2,1)} %param.10, bf16[1,64,512]{2,1,0:T(8,128)(2,1)} %param.9), kind=kLoop, calls=%fused_computation.44 | loop fusion | bytes 262144 | tf_op jit(solution)/shard_map/squeeze | solution.py:272
  1.7 4.1 %collective-permute-start.1 = (bf16[128,256]{1,0:T(8,128)(2,1)S(1)}, bf16[128,256]{1,0:T(8,128)(2,1)S(1)}, u32[]{:S(2)}, u32[]{:S(2)}) collective-permute-start(bf16[128,256]{1,0:T(8,128)(2,1)S(1)} %get-tuple-element.55), channel_id=1, source_target_pairs={{0,16},{2,18},{4,20},{6,22},{8,24},{10,26},{12,28},{14,30},{16,0},... | collective-permute-start | bytes 196616 | tf_op jit(solution)/shard_map/ppermute | solution.py:268
  5.8 1.6 %collective-permute-start = (bf16[128,256]{1,0:T(8,128)(2,1)S(1)}, bf16[128,256]{1,0:T(8,128)(2,1)S(1)}, u32[]{:S(2)}, u32[]{:S(2)}) collective-permute-start(bf16[128,256]{1,0:T(8,128)(2,1)S(1)} %get-tuple-element.55), channel_id=1, source_target_pairs={{0,8},{2,10},{4,12},{6,14},{8,16},{10,18},{12,20},{14,22},{16,24},... | collective-permute-start | bytes 196616 | tf_op jit(solution)/shard_map/ppermute | solution.py:268
  7.3 2.2 %collective-permute-start.2 = (bf16[128,256]{1,0:T(8,128)(2,1)S(1)}, bf16[128,256]{1,0:T(8,128)(2,1)S(1)}, u32[]{:S(2)}, u32[]{:S(2)}) collective-permute-start(bf16[128,256]{1,0:T(8,128)(2,1)S(1)} %get-tuple-element.55), channel_id=1, source_target_pairs={{0,24},{2,26},{4,28},{6,30},{8,0},{10,2},{12,4},{14,6},{16,8},{18,... | collective-permute-start | bytes 196616 | tf_op jit(solution)/shard_map/ppermute | solution.py:268
  9.6 2.4 %collective-permute-done = bf16[128,256]{1,0:T(8,128)(2,1)S(1)} collective-permute-done((bf16[128,256]{1,0:T(8,128)(2,1)S(1)}, bf16[128,256]{1,0:T(8,128)(2,1)S(1)}, u32[]{:S(2)}, u32[]{:S(2)}) %collective-permute-start) | collective-permute-done | bytes 65568 | tf_op jit(solution)/shard_map/ppermute | solution.py:268
  12.0 0.3 collective-permute-done.2
  12.4 1.6 %collective-permute-start.3 = (bf16[4,64,256]{2,1,0:T(8,128)(2,1)S(1)}, bf16[4,64,256]{2,1,0:T(8,128)(2,1)S(1)}, u32[]{:S(2)}, u32[]{:S(2)}) collective-permute-start(bf16[4,64,256]{2,1,0:T(8,128)(2,1)S(1)} %get-tuple-element.45), channel_id=1, source_target_pairs={{0,2},{2,0},{4,6},{6,4},{8,10},{10,8},{12,14},{14,12},{16,18},{18,... | collective-permute-start | bytes 393224 | tf_op jit(solution)/shard_map/ppermute | solution.py:264
  13.9 1.5 %collective-permute-start.5 = (bf16[4,64,256]{2,1,0:T(8,128)(2,1)S(1)}, bf16[4,64,256]{2,1,0:T(8,128)(2,1)S(1)}, u32[]{:S(2)}, u32[]{:S(2)}) collective-permute-start(bf16[4,64,256]{2,1,0:T(8,128)(2,1)S(1)} %get-tuple-element.44), channel_id=1, source_target_pairs={{0,4},{2,6},{4,0},{6,2},{8,12},{10,14},{12,8},{14,10},{16,20},{18,... | collective-permute-start | bytes 393224 | tf_op jit(solution)/shard_map/ppermute | solution.py:264
  15.5 1.8 %collective-permute-start.8 = (bf16[128,256]{1,0:T(8,128)(2,1)S(1)}, bf16[128,256]{1,0:T(8,128)(2,1)S(1)}, u32[]{:S(2)}, u32[]{:S(2)}) collective-permute-start(bf16[128,256]{1,0:T(8,128)(2,1)S(1)} %get-tuple-element.49), channel_id=1, source_target_pairs={{0,16},{2,18},{4,20},{6,22},{8,24},{10,26},{12,28},{14,30},{16,0},... | collective-permute-start | bytes 196616 | tf_op jit(solution)/shard_map/ppermute | solution.py:268
  17.2 2.2 %collective-permute-start.7 = (bf16[128,256]{1,0:T(8,128)(2,1)S(1)}, bf16[128,256]{1,0:T(8,128)(2,1)S(1)}, u32[]{:S(2)}, u32[]{:S(2)}) collective-permute-start(bf16[128,256]{1,0:T(8,128)(2,1)S(1)} %get-tuple-element.49), channel_id=1, source_target_pairs={{0,8},{2,10},{4,12},{6,14},{8,16},{10,18},{12,20},{14,22},{16,24},... | collective-permute-start | bytes 196616 | tf_op jit(solution)/shard_map/ppermute | solution.py:268
  19.4 1.6 %collective-permute-start.9 = (bf16[128,256]{1,0:T(8,128)(2,1)S(1)}, bf16[128,256]{1,0:T(8,128)(2,1)S(1)}, u32[]{:S(2)}, u32[]{:S(2)}) collective-permute-start(bf16[128,256]{1,0:T(8,128)(2,1)S(1)} %get-tuple-element.49), channel_id=1, source_target_pairs={{0,24},{2,26},{4,28},{6,30},{8,0},{10,2},{12,4},{14,6},{16,8},{18,... | collective-permute-start | bytes 196616 | tf_op jit(solution)/shard_map/ppermute | solution.py:268
  21.1 0.7 pad_maximum_fusion.2
  21.8 0.5 collective-permute-start.4
  22.3 0.7 pad_maximum_fusion.3
  23.0 0.5 collective-permute-start.6
  23.6 0.5 collective-permute-done.9
  24.1 2.0 %collective-permute-start.12 = (bf16[4,128,256]{2,1,0:T(8,128)(2,1)S(1)}, bf16[4,128,256]{2,1,0:T(8,128)(2,1)S(1)}, u32[]{:S(2)}, u32[]{:S(2)}) collective-permute-start(bf16[4,128,256]{2,1,0:T(8,128)(2,1)S(1)} %pad_maximum_fusion.4.refs_7_.refs_11_), channel_id=1, source_target_pairs={{0,6},{2,4},{4,2},{6,0},{8,14},{10,12},{12,10},{14,8},{16,22},{18,... | collective-permute-start | bytes 786440 | tf_op jit(solution)/shard_map/ppermute | solution.py:264
  26.1 0.5 collective-permute-start.11
  26.7 1.0 %collective-permute-start.10 = (bf16[4,128,256]{2,1,0:T(8,128)(2,1)S(1)}, bf16[4,128,256]{2,1,0:T(8,128)(2,1)}, u32[]{:S(2)}, u32[]{:S(2)}) collective-permute-start(bf16[4,128,256]{2,1,0:T(8,128)(2,1)S(1)} %pad_maximum_fusion.4.refs_7_.refs_11_), channel_id=1, source_target_pairs={{0,2},{2,0},{4,6},{6,4},{8,10},{10,8},{12,14},{14,12},{16,18},{18,... | collective-permute-start | bytes 786440 | tf_op jit(solution)/shard_map/ppermute | solution.py:264
  28.4 5.4 %collective-permute-done.4.refs_9_.refs_10_ = bf16[8,64,256]{2,1,0:T(8,128)(2,1)S(1)} collective-permute-done((bf16[8,64,256]{2,1,0:T(8,128)(2,1)}, bf16[8,64,256]{2,1,0:T(8,128)(2,1)S(1)}, u32[]{:S(2)}, u32[]{:S(2)}) %collective-permute-start.4) | collective-permute-done | bytes 262176 | tf_op jit(solution)/shard_map/ppermute | solution.py:264
  33.8 1.6 %copy-done.1 = bf16[256,4096]{1,0:T(8,128)(2,1)S(1)} copy-done((bf16[256,4096]{1,0:T(8,128)(2,1)S(1)}, bf16[256,4096]{1,0:T(8,128)(2,1)}, u32[]{:S(2)}) %copy-start.1) | copy-done | bytes 2097176
  35.4 12.4 %attention_backward.2 = (bf16[256,4096]{1,0:T(8,128)(2,1)}, f32[4,128,256]{2,1,0:T(8,128)S(1)}, bf16[4,128,256]{2,1,0:T(8,128)(2,1)S(1)}, bf16[4,128,256]{2,1,0:...) custom-call(s32[2,16]{1,0:T(2,128)S(1)} %copy-done.2, s32[16]{0:T(128)S(1)} %copy-done.3, ...), custom_call_target="tpu_custom_call" | custom-call | flops 2684354560 | bytes 3145728 | tf_op jit(solution)/shard_map/attention_backward/pallas_call | solution.py:218
  47.9 0.5 collective-permute-start.13
  48.4 0.3 collective-permute-start.14
  48.7 2.7 %collective-permute-start.15 = (bf16[4,128,256]{2,1,0:T(8,128)(2,1)S(1)}, bf16[4,128,256]{2,1,0:T(8,128)(2,1)S(1)}, u32[]{:S(2)}, u32[]{:S(2)}) collective-permute-start(bf16[4,128,256]{2,1,0:T(8,128)(2,1)S(1)} %get-tuple-element.22), channel_id=1, source_target_pairs={{0,6},{2,4},{4,2},{6,0},{8,14},{10,12},{12,10},{14,8},{16,22},{18,... | collective-permute-start | bytes 786440 | tf_op jit(solution)/shard_map/ppermute | solution.py:264
  51.4 12.6 %attention_backward.3 = (bf16[256,4096]{1,0:T(8,128)(2,1)}, f32[4,128,256]{2,1,0:T(8,128)S(1)}, f32[4,64,256]{2,1,0:T(8,128)S(1)}, bf16[528,256]{1,0:T(8,128)(2,...) custom-call(s32[2,16]{1,0:T(2,128)S(1)} %copy-done.2, ...), custom_call_target="tpu_custom_call", output_to_operand_aliasing={{0}: (15, {})} | custom-call | flops 2684354560 | bytes 3145728 | tf_op jit(solution)/shard_map/attention_backward/pallas_call | solution.py:218
  63.9 0.5 collective-permute-start.21
  64.5 0.3 collective-permute-start.19
  64.8 0.2 fusion.24
  64.9 0.9 %collective-permute-start.16 = (bf16[128,256]{1,0:T(8,128)(2,1)S(1)}, bf16[128,256]{1,0:T(8,128)(2,1)S(1)}, u32[]{:S(2)}, u32[]{:S(2)}) collective-permute-start(bf16[128,256]{1,0:T(8,128)(2,1)S(1)} %get-tuple-element.41), channel_id=1, source_target_pairs={{0,24},{2,26},{4,28},{6,30},{8,0},{10,2},{12,4},{14,6},{16,8},{18,... | collective-permute-start | bytes 196616 | tf_op jit(solution)/shard_map/ppermute | solution.py:268
  65.9 1.1 %collective-permute-start.18 = (bf16[128,256]{1,0:T(8,128)(2,1)S(1)}, bf16[128,256]{1,0:T(8,128)(2,1)S(1)}, u32[]{:S(2)}, u32[]{:S(2)}) collective-permute-start(bf16[128,256]{1,0:T(8,128)(2,1)S(1)} %get-tuple-element.42), channel_id=1, source_target_pairs={{0,8},{2,10},{4,12},{6,14},{8,16},{10,18},{12,20},{14,22},{16,24},... | collective-permute-start | bytes 196616 | tf_op jit(solution)/shard_map/ppermute | solution.py:268
  67.0 0.2 collective-permute-start.17
  67.3 3.7 %collective-permute-done.19 = bf16[528,256]{1,0:T(8,128)(2,1)S(1)} collective-permute-done((bf16[528,256]{1,0:T(8,128)(2,1)S(1)}, bf16[528,256]{1,0:T(8,128)(2,1)S(1)}, u32[]{:S(2)}, u32[]{:S(2)}) %collective-permute-start.19) | collective-permute-done | bytes 270368 | tf_op jit(solution)/shard_map/ppermute | solution.py:264
  71.0 0.1 select_convert_fusion.1
  71.1 1.5 %collective-permute-start.20 = (bf16[272,256]{1,0:T(8,128)(2,1)S(1)}, bf16[272,256]{1,0:T(8,128)(2,1)S(1)}, u32[]{:S(2)}, u32[]{:S(2)}) collective-permute-start(bf16[272,256]{1,0:T(8,128)(2,1)S(1)} %pad_maximum_fusion.5), channel_id=1, source_target_pairs={{0,2},{2,0},{4,6},{6,4},{8,10},{10,8},{12,14},{14,12},{16,18},{18,... | collective-permute-start | bytes 417800 | tf_op jit(solution)/shard_map/ppermute | solution.py:264
  72.7 0.6 collective-permute-start.22
  73.3 2.9 %collective-permute-done.20 = bf16[272,256]{1,0:T(8,128)(2,1)S(1)} collective-permute-done((bf16[272,256]{1,0:T(8,128)(2,1)S(1)}, bf16[272,256]{1,0:T(8,128)(2,1)S(1)}, u32[]{:S(2)}, u32[]{:S(2)}) %collective-permute-start.20) | collective-permute-done | bytes 139296 | tf_op jit(solution)/shard_map/ppermute | solution.py:264
  76.3 1.4 %collective-permute-done.22 = bf16[4,64,256]{2,1,0:T(8,128)(2,1)S(1)} collective-permute-done((bf16[4,64,256]{2,1,0:T(8,128)(2,1)S(1)}, bf16[4,64,256]{2,1,0:T(8,128)(2,1)S(1)}, u32[]{:S(2)}, u32[]{:S(2)}) %collective-permute-start.22) | collective-permute-done | bytes 131104 | tf_op jit(solution)/shard_map/ppermute | solution.py:264
  77.7 0.1 convert_add_fusion.4
  77.9 0.1 select_convert_fusion
  78.1 1.4 %collective-permute-start.24 = (bf16[144,256]{1,0:T(8,128)(2,1)S(1)}, bf16[144,256]{1,0:T(8,128)(2,1)S(1)}, u32[]{:S(2)}, u32[]{:S(2)}) collective-permute-start(bf16[144,256]{1,0:T(8,128)(2,1)S(1)} %get-tuple-element.57), channel_id=1, source_target_pairs={{0,16},{2,18},{4,20},{6,22},{8,24},{10,26},{12,28},{14,30},{16,0},... | collective-permute-start | bytes 221192 | tf_op jit(solution)/shard_map/ppermute | solution.py:268
  79.5 0.8 collective-permute-start.25
  80.2 2.1 %collective-permute-done.23 = bf16[144,256]{1,0:T(8,128)(2,1)S(1)} collective-permute-done((bf16[144,256]{1,0:T(8,128)(2,1)S(1)}, bf16[144,256]{1,0:T(8,128)(2,1)S(1)}, u32[]{:S(2)}, u32[]{:S(2)}) %collective-permute-start.23) | collective-permute-done | bytes 73760 | tf_op jit(solution)/shard_map/ppermute | solution.py:268
  82.4 1.0 %collective-permute-done.24 = bf16[144,256]{1,0:T(8,128)(2,1)S(1)} collective-permute-done((bf16[144,256]{1,0:T(8,128)(2,1)S(1)}, bf16[144,256]{1,0:T(8,128)(2,1)S(1)}, u32[]{:S(2)}, u32[]{:S(2)}) %collective-permute-start.24) | collective-permute-done | bytes 73760 | tf_op jit(solution)/shard_map/ppermute | solution.py:268
  83.4 2.2 %collective-permute-done.25 = bf16[144,256]{1,0:T(8,128)(2,1)S(1)} collective-permute-done((bf16[144,256]{1,0:T(8,128)(2,1)S(1)}, bf16[144,256]{1,0:T(8,128)(2,1)S(1)}, u32[]{:S(2)}, u32[]{:S(2)}) %collective-permute-start.25) | collective-permute-done | bytes 73760 | tf_op jit(solution)/shard_map/ppermute | solution.py:268
  85.8 0.7 fusion.14
  86.4 0.4 collective-permute-done.26
  86.9 0.6 add_reduce_fusion
  (55 shorter events, 0.6 us)
Async XLA Ops:
  0.6 33.2 %copy-start.3 = (s32[16]{0:T(128)S(1)}, s32[16]{0:T(128)}, u32[]{:S(2)}) copy-start(s32[16]{0:T(128)} %refs_1_.3) | copy-start | bytes 196
  0.6 33.2 %copy-start.2 = (s32[2,16]{1,0:T(2,128)S(1)}, s32[2,16]{1,0:T(2,128)}, u32[]{:S(2)}) copy-start(s32[2,16]{1,0:T(2,128)} %refs_0_.3) | copy-start | bytes 388
  0.7 33.2 %copy-start = (bf16[256,4096]{1,0:T(8,128)(2,1)S(1)}, bf16[256,4096]{1,0:T(8,128)(2,1)}, u32[]{:S(2)}) copy-start(bf16[256,4096]{1,0:T(8,128)(2,1)} %refs_5_.3) | copy-start | bytes 6291460
  1.7 7.9 %collective-permute-start.1 = (bf16[128,256]{1,0:T(8,128)(2,1)S(1)}, bf16[128,256]{1,0:T(8,128)(2,1)S(1)}, u32[]{:S(2)}, u32[]{:S(2)}) collective-permute-start(bf16[128,256]{1,0:T(8,128)(2,1)S(1)} %get-tuple-element.55), channel_id=1, source_target_pairs={{0,16},{2,18},{4,20},{6,22},{8,24},{10,26},{12,28},{14,30},{16,0},... | collective-permute-start | bytes 196616 | tf_op jit(solution)/shard_map/ppermute | solution.py:268
  5.8 6.2 %collective-permute-start = (bf16[128,256]{1,0:T(8,128)(2,1)S(1)}, bf16[128,256]{1,0:T(8,128)(2,1)S(1)}, u32[]{:S(2)}, u32[]{:S(2)}) collective-permute-start(bf16[128,256]{1,0:T(8,128)(2,1)S(1)} %get-tuple-element.55), channel_id=1, source_target_pairs={{0,8},{2,10},{4,12},{6,14},{8,16},{10,18},{12,20},{14,22},{16,24},... | collective-permute-start | bytes 196616 | tf_op jit(solution)/shard_map/ppermute | solution.py:268
  7.3 5.0 %collective-permute-start.2 = (bf16[128,256]{1,0:T(8,128)(2,1)S(1)}, bf16[128,256]{1,0:T(8,128)(2,1)S(1)}, u32[]{:S(2)}, u32[]{:S(2)}) collective-permute-start(bf16[128,256]{1,0:T(8,128)(2,1)S(1)} %get-tuple-element.55), channel_id=1, source_target_pairs={{0,24},{2,26},{4,28},{6,30},{8,0},{10,2},{12,4},{14,6},{16,8},{18,... | collective-permute-start | bytes 196616 | tf_op jit(solution)/shard_map/ppermute | solution.py:268
  12.4 8.7 %collective-permute-start.3 = (bf16[4,64,256]{2,1,0:T(8,128)(2,1)S(1)}, bf16[4,64,256]{2,1,0:T(8,128)(2,1)S(1)}, u32[]{:S(2)}, u32[]{:S(2)}) collective-permute-start(bf16[4,64,256]{2,1,0:T(8,128)(2,1)S(1)} %get-tuple-element.45), channel_id=1, source_target_pairs={{0,2},{2,0},{4,6},{6,4},{8,10},{10,8},{12,14},{14,12},{16,18},{18,... | collective-permute-start | bytes 393224 | tf_op jit(solution)/shard_map/ppermute | solution.py:264
  13.9 8.4 %collective-permute-start.5 = (bf16[4,64,256]{2,1,0:T(8,128)(2,1)S(1)}, bf16[4,64,256]{2,1,0:T(8,128)(2,1)S(1)}, u32[]{:S(2)}, u32[]{:S(2)}) collective-permute-start(bf16[4,64,256]{2,1,0:T(8,128)(2,1)S(1)} %get-tuple-element.44), channel_id=1, source_target_pairs={{0,4},{2,6},{4,0},{6,2},{8,12},{10,14},{12,8},{14,10},{16,20},{18,... | collective-permute-start | bytes 393224 | tf_op jit(solution)/shard_map/ppermute | solution.py:264
  15.5 8.1 %collective-permute-start.8 = (bf16[128,256]{1,0:T(8,128)(2,1)S(1)}, bf16[128,256]{1,0:T(8,128)(2,1)S(1)}, u32[]{:S(2)}, u32[]{:S(2)}) collective-permute-start(bf16[128,256]{1,0:T(8,128)(2,1)S(1)} %get-tuple-element.49), channel_id=1, source_target_pairs={{0,16},{2,18},{4,20},{6,22},{8,24},{10,26},{12,28},{14,30},{16,0},... | collective-permute-start | bytes 196616 | tf_op jit(solution)/shard_map/ppermute | solution.py:268
  17.2 6.4 %collective-permute-start.7 = (bf16[128,256]{1,0:T(8,128)(2,1)S(1)}, bf16[128,256]{1,0:T(8,128)(2,1)S(1)}, u32[]{:S(2)}, u32[]{:S(2)}) collective-permute-start(bf16[128,256]{1,0:T(8,128)(2,1)S(1)} %get-tuple-element.49), channel_id=1, source_target_pairs={{0,8},{2,10},{4,12},{6,14},{8,16},{10,18},{12,20},{14,22},{16,24},... | collective-permute-start | bytes 196616 | tf_op jit(solution)/shard_map/ppermute | solution.py:268
  19.4 4.7 %collective-permute-start.9 = (bf16[128,256]{1,0:T(8,128)(2,1)S(1)}, bf16[128,256]{1,0:T(8,128)(2,1)S(1)}, u32[]{:S(2)}, u32[]{:S(2)}) collective-permute-start(bf16[128,256]{1,0:T(8,128)(2,1)S(1)} %get-tuple-element.49), channel_id=1, source_target_pairs={{0,24},{2,26},{4,28},{6,30},{8,0},{10,2},{12,4},{14,6},{16,8},{18,... | collective-permute-start | bytes 196616 | tf_op jit(solution)/shard_map/ppermute | solution.py:268
  21.8 12.0 %collective-permute-start.4 = (bf16[8,64,256]{2,1,0:T(8,128)(2,1)}, bf16[8,64,256]{2,1,0:T(8,128)(2,1)S(1)}, u32[]{:S(2)}, u32[]{:S(2)}) collective-permute-start(bf16[8,64,256]{2,1,0:T(8,128)(2,1)} %pad_maximum_fusion.2), channel_id=1, source_target_pairs={{0,4},{2,6},{4,0},{6,2},{8,12},{10,14},{12,8},{14,10},{16,20},{18,... | collective-permute-start | bytes 786440 | tf_op jit(solution)/shard_map/ppermute | solution.py:264
  23.0 10.8 %collective-permute-start.6 = (bf16[8,64,256]{2,1,0:T(8,128)(2,1)}, bf16[8,64,256]{2,1,0:T(8,128)(2,1)}, u32[]{:S(2)}, u32[]{:S(2)}) collective-permute-start(bf16[8,64,256]{2,1,0:T(8,128)(2,1)} %pad_maximum_fusion.3), channel_id=1, source_target_pairs={{0,2},{2,0},{4,6},{6,4},{8,10},{10,8},{12,14},{14,12},{16,18},{18,... | collective-permute-start | bytes 786440 | tf_op jit(solution)/shard_map/ppermute | solution.py:264
  24.1 24.6 %collective-permute-start.12 = (bf16[4,128,256]{2,1,0:T(8,128)(2,1)S(1)}, bf16[4,128,256]{2,1,0:T(8,128)(2,1)S(1)}, u32[]{:S(2)}, u32[]{:S(2)}) collective-permute-start(bf16[4,128,256]{2,1,0:T(8,128)(2,1)S(1)} %pad_maximum_fusion.4.refs_7_.refs_11_), channel_id=1, source_target_pairs={{0,6},{2,4},{4,2},{6,0},{8,14},{10,12},{12,10},{14,8},{16,22},{18,... | collective-permute-start | bytes 786440 | tf_op jit(solution)/shard_map/ppermute | solution.py:264
  26.1 25.2 %collective-permute-start.11 = (bf16[4,128,256]{2,1,0:T(8,128)(2,1)S(1)}, bf16[4,128,256]{2,1,0:T(8,128)(2,1)}, u32[]{:S(2)}, u32[]{:S(2)}) collective-permute-start(bf16[4,128,256]{2,1,0:T(8,128)(2,1)S(1)} %pad_maximum_fusion.4.refs_7_.refs_11_), channel_id=1, source_target_pairs={{0,4},{2,6},{4,0},{6,2},{8,12},{10,14},{12,8},{14,10},{16,20},{18,... | collective-permute-start | bytes 786440 | tf_op jit(solution)/shard_map/ppermute | solution.py:264
  26.7 24.7 %collective-permute-start.10 = (bf16[4,128,256]{2,1,0:T(8,128)(2,1)S(1)}, bf16[4,128,256]{2,1,0:T(8,128)(2,1)}, u32[]{:S(2)}, u32[]{:S(2)}) collective-permute-start(bf16[4,128,256]{2,1,0:T(8,128)(2,1)S(1)} %pad_maximum_fusion.4.refs_7_.refs_11_), channel_id=1, source_target_pairs={{0,2},{2,0},{4,6},{6,4},{8,10},{10,8},{12,14},{14,12},{16,18},{18,... | collective-permute-start | bytes 786440 | tf_op jit(solution)/shard_map/ppermute | solution.py:264
  33.8 1.6 %copy-start.1 = (bf16[256,4096]{1,0:T(8,128)(2,1)S(1)}, bf16[256,4096]{1,0:T(8,128)(2,1)}, u32[]{:S(2)}) copy-start(bf16[256,4096]{1,0:T(8,128)(2,1)} %refs_6_.3) | copy-start | bytes 6291460
  47.9 16.9 %collective-permute-start.13 = (bf16[4,128,256]{2,1,0:T(8,128)(2,1)S(1)}, bf16[4,128,256]{2,1,0:T(8,128)(2,1)S(1)}, u32[]{:S(2)}, u32[]{:S(2)}) collective-permute-start(bf16[4,128,256]{2,1,0:T(8,128)(2,1)S(1)} %get-tuple-element.20), channel_id=1, source_target_pairs={{0,2},{2,0},{4,6},{6,4},{8,10},{10,8},{12,14},{14,12},{16,18},{18,... | collective-permute-start | bytes 786440 | tf_op jit(solution)/shard_map/ppermute | solution.py:264
  48.4 16.4 %collective-permute-start.14 = (bf16[4,128,256]{2,1,0:T(8,128)(2,1)S(1)}, bf16[4,128,256]{2,1,0:T(8,128)(2,1)S(1)}, u32[]{:S(2)}, u32[]{:S(2)}) collective-permute-start(bf16[4,128,256]{2,1,0:T(8,128)(2,1)S(1)} %get-tuple-element.21), channel_id=1, source_target_pairs={{0,4},{2,6},{4,0},{6,2},{8,12},{10,14},{12,8},{14,10},{16,20},{18,... | collective-permute-start | bytes 786440 | tf_op jit(solution)/shard_map/ppermute | solution.py:264
  48.7 16.1 %collective-permute-start.15 = (bf16[4,128,256]{2,1,0:T(8,128)(2,1)S(1)}, bf16[4,128,256]{2,1,0:T(8,128)(2,1)S(1)}, u32[]{:S(2)}, u32[]{:S(2)}) collective-permute-start(bf16[4,128,256]{2,1,0:T(8,128)(2,1)S(1)} %get-tuple-element.22), channel_id=1, source_target_pairs={{0,6},{2,4},{4,2},{6,0},{8,14},{10,12},{12,10},{14,8},{16,22},{18,... | collective-permute-start | bytes 786440 | tf_op jit(solution)/shard_map/ppermute | solution.py:264
  63.9 8.7 %collective-permute-start.21 = (bf16[8,64,256]{2,1,0:T(8,128)(2,1)S(1)}, bf16[8,64,256]{2,1,0:T(8,128)(2,1)S(1)}, u32[]{:S(2)}, u32[]{:S(2)}) collective-permute-start(bf16[8,64,256]{2,1,0:T(8,128)(2,1)S(1)} %get-tuple-element.26), channel_id=1, source_target_pairs={{0,2},{2,0},{4,6},{6,4},{8,10},{10,8},{12,14},{14,12},{16,18},{18,... | collective-permute-start | bytes 786440 | tf_op jit(solution)/shard_map/ppermute | solution.py:264
  64.5 6.5 %collective-permute-start.19 = (bf16[528,256]{1,0:T(8,128)(2,1)S(1)}, bf16[528,256]{1,0:T(8,128)(2,1)S(1)}, u32[]{:S(2)}, u32[]{:S(2)}) collective-permute-start(bf16[528,256]{1,0:T(8,128)(2,1)S(1)} %get-tuple-element.24), channel_id=1, source_target_pairs={{0,4},{2,6},{4,0},{6,2},{8,12},{10,14},{12,8},{14,10},{16,20},{18,... | collective-permute-start | bytes 811016 | tf_op jit(solution)/shard_map/ppermute | solution.py:264
  64.9 13.1 %collective-permute-start.16 = (bf16[128,256]{1,0:T(8,128)(2,1)S(1)}, bf16[128,256]{1,0:T(8,128)(2,1)S(1)}, u32[]{:S(2)}, u32[]{:S(2)}) collective-permute-start(bf16[128,256]{1,0:T(8,128)(2,1)S(1)} %get-tuple-element.41), channel_id=1, source_target_pairs={{0,24},{2,26},{4,28},{6,30},{8,0},{10,2},{12,4},{14,6},{16,8},{18,... | collective-permute-start | bytes 196616 | tf_op jit(solution)/shard_map/ppermute | solution.py:268
  65.9 12.2 %collective-permute-start.18 = (bf16[128,256]{1,0:T(8,128)(2,1)S(1)}, bf16[128,256]{1,0:T(8,128)(2,1)S(1)}, u32[]{:S(2)}, u32[]{:S(2)}) collective-permute-start(bf16[128,256]{1,0:T(8,128)(2,1)S(1)} %get-tuple-element.42), channel_id=1, source_target_pairs={{0,8},{2,10},{4,12},{6,14},{8,16},{10,18},{12,20},{14,22},{16,24},... | collective-permute-start | bytes 196616 | tf_op jit(solution)/shard_map/ppermute | solution.py:268
  67.0 11.0 %collective-permute-start.17 = (bf16[128,256]{1,0:T(8,128)(2,1)S(1)}, bf16[128,256]{1,0:T(8,128)(2,1)S(1)}, u32[]{:S(2)}, u32[]{:S(2)}) collective-permute-start(bf16[128,256]{1,0:T(8,128)(2,1)S(1)} %get-tuple-element.43), channel_id=1, source_target_pairs={{0,16},{2,18},{4,20},{6,22},{8,24},{10,26},{12,28},{14,30},{16,0},... | collective-permute-start | bytes 196616 | tf_op jit(solution)/shard_map/ppermute | solution.py:268
  71.1 5.1 %collective-permute-start.20 = (bf16[272,256]{1,0:T(8,128)(2,1)S(1)}, bf16[272,256]{1,0:T(8,128)(2,1)S(1)}, u32[]{:S(2)}, u32[]{:S(2)}) collective-permute-start(bf16[272,256]{1,0:T(8,128)(2,1)S(1)} %pad_maximum_fusion.5), channel_id=1, source_target_pairs={{0,2},{2,0},{4,6},{6,4},{8,10},{10,8},{12,14},{14,12},{16,18},{18,... | collective-permute-start | bytes 417800 | tf_op jit(solution)/shard_map/ppermute | solution.py:264
  72.7 5.0 %collective-permute-start.22 = (bf16[4,64,256]{2,1,0:T(8,128)(2,1)S(1)}, bf16[4,64,256]{2,1,0:T(8,128)(2,1)S(1)}, u32[]{:S(2)}, u32[]{:S(2)}) collective-permute-start(bf16[4,64,256]{2,1,0:T(8,128)(2,1)S(1)} %add_convert_fusion), channel_id=1, source_target_pairs={{0,4},{2,6},{4,0},{6,2},{8,12},{10,14},{12,8},{14,10},{16,20},{18,... | collective-permute-start | bytes 393224 | tf_op jit(solution)/shard_map/ppermute | solution.py:264
  78.0 4.4 %collective-permute-start.23 = (bf16[144,256]{1,0:T(8,128)(2,1)S(1)}, bf16[144,256]{1,0:T(8,128)(2,1)S(1)}, u32[]{:S(2)}, u32[]{:S(2)}) collective-permute-start(bf16[144,256]{1,0:T(8,128)(2,1)S(1)} %get-tuple-element.56), channel_id=1, source_target_pairs={{0,24},{2,26},{4,28},{6,30},{8,0},{10,2},{12,4},{14,6},{16,8},{18,... | collective-permute-start | bytes 221192 | tf_op jit(solution)/shard_map/ppermute | solution.py:268
  78.1 5.3 %collective-permute-start.24 = (bf16[144,256]{1,0:T(8,128)(2,1)S(1)}, bf16[144,256]{1,0:T(8,128)(2,1)S(1)}, u32[]{:S(2)}, u32[]{:S(2)}) collective-permute-start(bf16[144,256]{1,0:T(8,128)(2,1)S(1)} %get-tuple-element.57), channel_id=1, source_target_pairs={{0,16},{2,18},{4,20},{6,22},{8,24},{10,26},{12,28},{14,30},{16,0},... | collective-permute-start | bytes 221192 | tf_op jit(solution)/shard_map/ppermute | solution.py:268
  79.5 6.2 %collective-permute-start.25 = (bf16[144,256]{1,0:T(8,128)(2,1)S(1)}, bf16[144,256]{1,0:T(8,128)(2,1)S(1)}, u32[]{:S(2)}, u32[]{:S(2)}) collective-permute-start(bf16[144,256]{1,0:T(8,128)(2,1)S(1)} %get-tuple-element.58), channel_id=1, source_target_pairs={{0,8},{2,10},{4,12},{6,14},{8,16},{10,18},{12,20},{14,22},{16,24},... | collective-permute-start | bytes 221192 | tf_op jit(solution)/shard_map/ppermute | solution.py:268
  85.7 1.2 %collective-permute-start.26 = (f32[1,256]{1,0:T(1,128)S(1)}, f32[1,256]{1,0:T(1,128)S(1)}, u32[]{:S(2)}, u32[]{:S(2)}) collective-permute-start(f32[1,256]{1,0:T(1,128)S(1)} %fusion.15), channel_id=1, source_target_pairs={{0,1},{1,0},{2,3},{3,2},{4,5},{5,4},{6,7},{7,6},{8,9},{9,8},{10,11... | collective-permute-start | bytes 3080 | tf_op jit(solution)/shard_map/ppermute | solution.py:344

commit v3 on v2

v3 whole, which is shorter than its diff:
```python
import functools
import math

import jax
import jax.numpy as jnp
from jax import lax
from jax.experimental import pallas as pl
from jax.experimental.pallas import tpu as pltpu
from jax.sharding import PartitionSpec as P

HD = 128
BLK = 128
PAIR = 2
CHUNKS = 2
VMEM_MB = 48
CODE = 16
NT = (((1,), (1,)), ((), ()))
F32, BF16 = jnp.float32, jnp.bfloat16


def coded(value, rows, rounded):
    high = rounded(value)
    middle = rounded(value - high)
    low = value - high - middle
    shape = (rows, value.shape[1])
    row = lax.broadcasted_iota(jnp.int32, shape, 0)
    parts = jnp.where(row == 0, high, jnp.zeros(shape, F32))
    return jnp.where(row == 1, middle, jnp.where(row == 2, low, parts)).astype(BF16)


def rounded_here(value):
    return value.astype(BF16).astype(F32)


def rounded_outside(value):
    return lax.reduce_precision(value, 8, 7)


def decoded(rows):
    rows = rows.astype(F32)
    return rows[0:1] + rows[1:2] + rows[2:3]


def attention_kernel(n, n_blocks, n_images, z_last, first, heads, n_arrays, n_extra, *refs):
    plan_ref, gate_ref, gate_in, q_hbm, cot_hbm = refs[:5]
    columns = refs[5 : 5 + n_arrays]
    refs = refs[5 + n_arrays + n_extra :]
    dq_hbm, own_ref = refs[:2]
    back_refs = refs[2:5]
    (
        gate_out,
        q_ref,
        cot_ref,
        dq_ref,
        k_all,
        v_all,
        k_sel,
        v_sel,
        kt_sel,
        dk_acc,
        dv_acc,
        dk_all,
        dv_all,
        gate_acc,
        fetch_place,
        back_place,
        bias,
        in_sem,
        out_sem,
    ) = refs[5:]
    img_tok = k_all.shape[2]
    read_most = n_images // 2
    width = q_ref.shape[2]
    groups = width // HD
    gate_value = gate_ref[0]
    inv_root = 1.0 / math.sqrt(HD)
    to_exp2 = math.log2(math.e) * inv_root

    def span(h):
        return pl.ds((first + h) * width, width)

    copies = []
    for h in range(heads):
        q_copy = pltpu.make_async_copy(q_hbm.at[:, span(h)], q_ref.at[h], in_sem.at[0, h])
        cot_copy = pltpu.make_async_copy(cot_hbm.at[:, span(h)], cot_ref.at[h], in_sem.at[1, h])
        copies.append((q_copy, cot_copy))
    for copy in copies[0]:
        copy.start()

    gate_acc[...] = jnp.zeros_like(gate_acc)
    gate_acc[0:1, 0:HD] = gate_in[0:1, :]
    me = plan_ref[(n_blocks + 1) * n_images]
    for j in range(read_most):
        fetch_place[j] = 0
        back_place[j] = 0
        for b in range(n_blocks):
            bias[b, j] = jnp.float32(-1e30)

    def look(i, count):
        reads = [plan_ref[b * n_images + i] > 0 for b in range(n_blocks)]
        any_read = functools.reduce(jnp.logical_or, reads)

        @pl.when(jnp.logical_and(any_read, count < read_most))
        def _():
            slot = plan_ref[n_blocks * n_images + i]
            column = jnp.bitwise_xor(lax.rem(slot, 4), lax.rem(me, 4))
            behind = lax.rem(lax.div(me, 4) - lax.div(slot, 4) + n, n)
            back_place[count] = column * n + behind
            fetch_place[count] = behind * 4 + column if z_last else column * n + behind
            for b in range(n_blocks):
                bias[b, count] = jnp.where(reads[b], 0.0, -1e30).astype(F32)

        return count + any_read.astype(jnp.int32)

    lax.fori_loop(0, n_images, look, jnp.int32(0))

    def select(h):
        lanes = slice(h * HD, (h + 1) * HD)
        at = 0
        for column in columns:
            count = column.shape[0]
            k_all[h, at : at + count] = column[:, :img_tok, lanes]
            v_all[h, at : at + count] = column[:, img_tok:, lanes]
            at += count
        for j in range(read_most):
            rows = slice(j * img_tok, (j + 1) * img_tok)
            k_sel[h, rows] = k_all[h, fetch_place[j]]
            v_sel[h, rows] = v_all[h, fetch_place[j]]
        kt_sel[h] = k_sel[h].astype(F32).T.astype(BF16)
        dk_acc[h] = jnp.zeros_like(dk_acc[h])
        dv_acc[h] = jnp.zeros_like(dv_acc[h])

    pairs = groups // PAIR

    def heads_of(ref, h, rows, g):
        lanes = [slice((g * PAIR + u) * HD, (g * PAIR + u + 1) * HD) for u in range(PAIR)]
        return jnp.concatenate([ref[h, rows, lane] for lane in lanes], axis=0)

    def products(item):
        h, b, g = item
        rows = slice(b * BLK, (b + 1) * BLK)
        query, cot = heads_of(q_ref, h, rows, g), heads_of(cot_ref, h, rows, g)
        scores = lax.dot_general(k_sel[h], query, NT, preferred_element_type=F32)
        prob_grad = lax.dot_general(v_sel[h], cot, NT, preferred_element_type=F32)
        return scores, prob_grad

    def softmax(item, scores, prob_grad):
        h, b, g = item
        scores = jnp.concatenate(
            [scores[j * img_tok : (j + 1) * img_tok] + bias[b, j] for j in range(read_most)],
            axis=0,
        )
        row_max = jnp.max(scores, axis=0, keepdims=True)
        terms = jnp.exp2((scores - row_max) * to_exp2)
        prob = terms * (1.0 / jnp.sum(terms, axis=0, keepdims=True))
        prob_half = prob.astype(BF16)
        delta = jnp.sum(prob_half.astype(F32) * prob_grad, axis=0, keepdims=True)
        score_grad = (prob * (prob_grad - delta)).astype(BF16)
        gate_acc[0:1, :] += delta
        return prob_half, score_grad

    def gradients(item, prob_half, score_grad):
        h, b, g = item
        rows = slice(b * BLK, (b + 1) * BLK)
        query, cot = heads_of(q_ref, h, rows, g), heads_of(cot_ref, h, rows, g)
        dq_t = jnp.dot(kt_sel[h], score_grad, preferred_element_type=F32)
        dq = (dq_t.T * (gate_value * inv_root)).astype(BF16)
        for u in range(PAIR):
            lanes = slice((g * PAIR + u) * HD, (g * PAIR + u + 1) * HD)
            dq_ref[h, rows, lanes] = dq[u * BLK : (u + 1) * BLK]
        dk_acc[h] += jnp.dot(score_grad, query, preferred_element_type=F32)
        dv_acc[h] += jnp.dot(prob_half, cot, preferred_element_type=F32)

    def finish(h):
        lanes = slice(h * HD, (h + 1) * HD)
        out_copies.append(
            pltpu.make_async_copy(dq_ref.at[h], dq_hbm.at[:, span(h)], out_sem.at[h])
        )
        out_copies[-1].start()
        dk_all[h] = jnp.zeros_like(dk_all[h])
        dv_all[h] = jnp.zeros_like(dv_all[h])
        for j in range(read_most):
            rows = slice(j * img_tok, (j + 1) * img_tok)
            dk_all[h, back_place[j]] = dk_acc[h, rows] * (gate_value * inv_root)
            dv_all[h, back_place[j]] = dv_acc[h, rows] * gate_value
        own_ref[:, :img_tok, lanes] = dk_all[h, 0:n]
        own_ref[:, img_tok:, lanes] = dv_all[h, 0:n]
        for a in range(1, 4):
            out, rows = back_refs[a - 1], 2 * img_tok
            for k in range(n):
                dk, dv = dk_all[h, a * n + k], dv_all[h, a * n + k]
                out[k * rows : k * rows + img_tok, lanes] = dk.astype(BF16)
                out[k * rows + img_tok : (k + 1) * rows, lanes] = dv.astype(BF16)

    out_copies = []
    items = [(h, b, g) for h in range(heads) for b in range(n_blocks) for g in range(pairs)]
    ready, done = None, None
    for at in range(len(items) + 2):
        fresh = None
        if at < len(items):
            h = items[at][0]
            if at == 0 or items[at - 1][0] != h:
                select(h)
                for copy in copies[h]:
                    copy.wait()
                if h + 1 < heads:
                    for copy in copies[h + 1]:
                        copy.start()
            fresh = (items[at], *products(items[at]))
        middle = None
        if ready is not None:
            middle = (ready[0], *softmax(*ready))
        if done is not None:
            gradients(*done)
            h = done[0][0]
            if done[0] == [item for item in items if item[0] == h][-1]:
                finish(h)
        ready, done = fresh, middle

    gate_row = sum(gate_acc[0:1, u * HD : (u + 1) * HD] for u in range(PAIR))
    gate_out[...] = jnp.broadcast_to(gate_row, gate_out.shape)
    rest = 2 * n * img_tok
    for out in back_refs:
        out[rest:] = jnp.zeros((CODE, heads * HD), BF16)
        out[rest:, :HD] = coded(gate_row, CODE, rounded_here)
    for copy in out_copies:
        copy.wait()


def attention(first, heads, n, z_last, prev_dq, gate_in, scalars, queries, cotangent, columns):
    tokens = queries.shape[0]
    plan, gate_value, n_blocks, n_images, total_kv = scalars
    img_tok = columns[0].shape[1] // 2
    groups = queries.shape[1] // HD // total_kv
    width = groups * HD
    n_keys = n_images // 2 * img_tok
    smem = pl.BlockSpec(memory_space=pltpu.SMEM)
    vmem = pl.BlockSpec(memory_space=pltpu.VMEM)
    hbm = pl.BlockSpec(memory_space=pltpu.HBM)

    span = heads * HD
    in_specs = [smem] * 2 + [vmem, hbm, hbm]
    args = [plan, gate_value, gate_in]
    args += [pltpu.with_memory_space_constraint(x, pltpu.HBM) for x in (queries, cotangent)]
    in_specs += [vmem] * len(columns)
    args += columns
    aliases = {}
    if prev_dq is not None:
        aliases[len(args)] = 0
        in_specs.append(hbm)
        args.append(prev_dq)
    outs = [((n, 2 * img_tok), F32)]
    outs += [((2 * n * img_tok + CODE,), BF16)] * 3
    out_shape = [pltpu.HBM(queries.shape, BF16)]
    out_shape += [jax.ShapeDtypeStruct((*shape, span), kind) for shape, kind in outs]
    out_shape.append(jax.ShapeDtypeStruct((8, HD), F32))
    rows = tokens * groups * heads
    return pl.pallas_call(
        functools.partial(attention_kernel, n, n_blocks, n_images, z_last, first, heads, len(columns), len(aliases)),
        in_specs=in_specs,
        out_specs=[hbm] + [vmem] * (len(out_shape) - 1),
        out_shape=out_shape,
        input_output_aliases=aliases,
        scratch_shapes=[
            pltpu.VMEM((heads, tokens, width), BF16),
            pltpu.VMEM((heads, tokens, width), BF16),
            pltpu.VMEM((heads, tokens, width), BF16),
            pltpu.VMEM((heads, 4 * n, img_tok, HD), BF16),
            pltpu.VMEM((heads, 4 * n, img_tok, HD), BF16),
            pltpu.VMEM((heads, n_keys, HD), BF16),
            pltpu.VMEM((heads, n_keys, HD), BF16),
            pltpu.VMEM((heads, HD, n_keys), BF16),
            pltpu.VMEM((heads, n_keys, HD), F32),
            pltpu.VMEM((heads, n_keys, HD), F32),
            pltpu.VMEM((heads, 4 * n, img_tok, HD), F32),
            pltpu.VMEM((heads, 4 * n, img_tok, HD), F32),
            pltpu.VMEM((8, PAIR * BLK), F32),
            pltpu.SMEM((n_images // 2,), jnp.int32),
            pltpu.SMEM((n_images // 2,), jnp.int32),
            pltpu.SMEM((n_blocks, n_images // 2), F32),
            pltpu.SemaphoreType.DMA((2, heads)),
            pltpu.SemaphoreType.DMA((heads,)),
        ],
        compiler_params=pltpu.CompilerParams(
            vmem_limit_bytes=VMEM_MB * 1024 * 1024,
        ),
        cost_estimate=pl.CostEstimate(
            flops=10 * rows * n_keys * HD,
            bytes_accessed=6 * rows * HD,
            transcendentals=rows * n_keys,
        ),
        name="attention_backward",
    )(*args)


def per_device(queries, cotangent, image_keys, image_values, attn_gate, block_mask, image_owner):
    n_ctx = lax.axis_size("ctx")
    n_tp = lax.axis_size("tp")
    n = n_ctx // 4
    img_tok = image_keys.shape[1]
    local_kv = image_keys.shape[2] // HD
    chunks = min(CHUNKS, local_kv)
    heads = local_kv // chunks
    me = lax.axis_index("ctx").astype(jnp.int32).reshape(1)
    plan = jnp.concatenate([block_mask.reshape(-1), image_owner, me])
    gate_value = jnp.tanh(attn_gate)

    def swap(value, bit):
        return lax.ppermute(value, "ctx", [(i, i ^ bit) for i in range(n_ctx)])

    def turn(value, by):
        pairs = [(i, (i // 4 + by) % n * 4 + i % 4) for i in range(n_ctx)]
        return lax.ppermute(value, "ctx", pairs)

    def own_columns(c):
        lanes = slice(c * heads * HD, (c + 1) * heads * HD)
        return jnp.concatenate([image_keys[0, :, lanes], image_values[0, :, lanes]], axis=0)

    def square_of(own):
        return jnp.stack([own, swap(own, 1), swap(own, 2), swap(own, 3)])

    def column_of(own):
        return jnp.stack([own] + [turn(own, k) for k in range(1, n)])

    def return_square(own, backs):
        rest = 2 * n * img_tok
        total, gate = own, decoded(backs[0][rest:])
        for a, back in enumerate(backs):
            came = swap(back, a + 1)
            total = total + came[:rest].reshape(own.shape).astype(F32)
            gate = gate + decoded(came[rest:])
        return total, gate

    def return_column(both, gate, last):
        total, gate_total = both[0], gate
        sends = both.astype(BF16)
        for k in range(1, n):
            send = sends[k]
            if last:
                send = jnp.concatenate([send, coded(gate, CODE, rounded_outside)])
            came = turn(send, -k)
            total = total + came[: 2 * img_tok].astype(F32)
            if last:
                gate_total = gate_total + decoded(came[2 * img_tok :])
        return total, gate_total

    owns = [own_columns(c) for c in range(chunks)]
    starts = [square_of(own) if c else column_of(own) for c, own in enumerate(owns)]
    if chunks > 1:
        starts = lax.optimization_barrier(starts)
    column = starts[0]
    gathered = [[column, swap(column, 1), swap(column, 2), swap(column, 3)]]
    for square in starts[1:]:
        gathered.append([square] + [turn(square, k) for k in range(1, n)])
    scalars = (plan, gate_value, *block_mask.shape, local_kv)
    dq, gate_part = None, jnp.zeros((8, HD), F32)
    parts = []
    for c in range(chunks):
        dq, own, *backs, gate_part = attention(
            c * heads, heads, n, c > 0, dq, gate_part, scalars, queries, cotangent, gathered[c]
        )
        total, gate_row = return_column(*return_square(own, backs), c == chunks - 1)
        parts.append(total.astype(BF16))
    grads = jnp.concatenate(parts, axis=1)
    key_grad, value_grad = grads[None, :img_tok], grads[None, img_tok:]
    gate_total = gate_row
    for k in range(1, n_tp):
        pairs = [(i, (i + k) % n_tp) for i in range(n_tp)]
        gate_total = gate_total + lax.ppermute(gate_row, "tp", pairs)
    term_count = queries.shape[0] * n_ctx * queries.shape[1] * n_tp
    gate_grad = (1.0 - gate_value * gate_value) * jnp.sum(gate_total) / math.sqrt(term_count)
    return (dq, key_grad, value_grad, gate_grad)


def solution(mesh):
    in_specs = (
        P("ctx", "tp"),
        P("ctx", "tp"),
        P("ctx", None, "tp"),
        P("ctx", None, "tp"),
        P(),
        P("ctx", None),
        P(),
    )
    out_specs = (P("ctx", "tp"), P("ctx", None, "tp"), P("ctx", None, "tp"), P())
    return jax.shard_map(
        per_device, mesh=mesh, in_specs=in_specs, out_specs=out_specs, check_vma=False
    )
```

time: 89.5 us -> 81.2 us (0.907)
  waiting for transfers between devices: 22.6 us -> 15.1 us
  starting transfers between devices: 32.2 us -> 37.6 us
  Pallas kernels: 25 us -> 20.5 us
  local copies, waits for them, and re-layouts: 2.65 us -> 1.72 us
    ppermute x14 -> x12, waiting for transfers between devices: 13.5 us -> 7.2 us  [swap(): return lax.ppermute(value, 'ctx', [(i, i ^ bit) for i in range(n_ctx)])]
    pallas_call x2, Pallas kernels: 25 us -> 20.5 us  [attention(): pl.pallas_call(functools.partial(attention_kernel, n, n_blocks, n_images,...]
    ppermute x12, starting transfers between devices: 18 us -> 22.3 us  [turn(): return lax.ppermute(value, 'ctx', pairs)]
    unnamed x8 -> x0, local copies, waits for them, and re-layouts: 1.6 us -> none
    ppermute x12, waiting for transfers between devices: 8.64 us -> 7.46 us  [turn(): return lax.ppermute(value, 'ctx', pairs)]
    ppermute x14 -> x12, starting transfers between devices: 14.1 us -> 15.2 us  [swap(): return lax.ppermute(value, 'ctx', [(i, i ^ bit) for i in range(n_ctx)])]
  transfers between devices with their start and end apart: 27 -> 25, of which waited for: 11 -> 11; matrix products, arithmetic and copies ran while one was open for 3% -> 4% of each run, Pallas kernels for 28% -> 25%
where the time goes in v3:
time: 81.2 us; the launch traced here: 80.9 us
  starting transfers between devices  37.6 us (46%)
  Pallas kernels  20.5 us (25%)
  waiting for transfers between devices  15.1 us (19%)
  between operations  3.33 us (4%)
  other arithmetic  2.65 us (3%)
  local copies, waits for them, and re-layouts  1.72 us (2%)
    ppermute x12, starting transfers between devices, turn(): return lax.ppermute(value, 'ctx', pairs)  22.3 us
    pallas_call x2, Pallas kernels, attention(): pl.pallas_call(functools.partial(attention_kernel, n, n_blocks, n_images,...  20.5 us
    ppermute x12, starting transfers between devices, swap(): return lax.ppermute(value, 'ctx', [(i, i ^ bit) for i in range(n_ctx)])  15.2 us
    ppermute x12, waiting for transfers between devices, turn(): return lax.ppermute(value, 'ctx', pairs)  7.46 us
    ppermute x12, waiting for transfers between devices, swap(): return lax.ppermute(value, 'ctx', [(i, i ^ bit) for i in range(n_ctx)])  7.2 us
  transfers between devices with their start and end apart: 25, of which 11 were waited for; matrix products, arithmetic and copies ran while one was open for 4% of the time, Pallas kernels for 25%

profile of v3, /device:TPU:0, one launch (start us, length us, event | category | flops | bytes accessed | tf_op | source)
XLA Modules:
  0.0 80.9 jit_solution(2058250891852963592)
XLA Ops:
  0.6 0.8 %slice_bitcast_fusion.8 = (bf16[64,256]{1,0:T(8,128)(2,1)S(1)}, bf16[64,256]{1,0:T(8,128)(2,1)S(1)}, bf16[64,256]{1,0:T(8,128)(2,1)S(1)}, bf16[64,256]{1,0:T(8,128)(2,1)S(1)}) fusion(bf16[1,64,512]{2,1,0:T(8,128)(2,1)} %param.10, bf16[1,64,512]{2,1,0:T(8,128)(2,1)} %param.9), kind=kLoop, calls=%fused_computation.35 | loop fusion | bytes 262144 | tf_op jit(solution)/shard_map/squeeze | solution.py:317
  1.5 3.0 %collective-permute-start.4 = (bf16[128,256]{1,0:T(8,128)(2,1)S(1)}, bf16[128,256]{1,0:T(8,128)(2,1)S(1)}, u32[]{:S(2)}, u32[]{:S(2)}) collective-permute-start(bf16[128,256]{1,0:T(8,128)(2,1)S(1)} %get-tuple-element.45), channel_id=1, source_target_pairs={{0,4},{2,6},{4,0},{6,2},{8,12},{10,14},{12,8},{14,10},{16,20},{18,... | collective-permute-start | bytes 196616 | tf_op jit(solution)/shard_map/ppermute | solution.py:309
  4.5 1.5 %collective-permute-start.3 = (bf16[128,256]{1,0:T(8,128)(2,1)S(1)}, bf16[128,256]{1,0:T(8,128)(2,1)S(1)}, u32[]{:S(2)}, u32[]{:S(2)}) collective-permute-start(bf16[128,256]{1,0:T(8,128)(2,1)S(1)} %get-tuple-element.45), channel_id=1, source_target_pairs={{0,2},{2,0},{4,6},{6,4},{8,10},{10,8},{12,14},{14,12},{16,18},{18,... | collective-permute-start | bytes 196616 | tf_op jit(solution)/shard_map/ppermute | solution.py:309
  6.0 0.0 collective-permute-start.5
  6.1 3.1 %collective-permute-start.1 = (bf16[128,256]{1,0:T(8,128)(2,1)S(1)}, bf16[128,256]{1,0:T(8,128)(2,1)S(1)}, u32[]{:S(2)}, u32[]{:S(2)}) collective-permute-start(bf16[128,256]{1,0:T(8,128)(2,1)S(1)} %get-tuple-element.51), channel_id=1, source_target_pairs={{0,16},{2,18},{4,20},{6,22},{8,24},{10,26},{12,28},{14,30},{16,0},... | collective-permute-start | bytes 196616 | tf_op jit(solution)/shard_map/ppermute | solution.py:313
  9.1 1.6 %collective-permute-start = (bf16[128,256]{1,0:T(8,128)(2,1)S(1)}, bf16[128,256]{1,0:T(8,128)(2,1)S(1)}, u32[]{:S(2)}, u32[]{:S(2)}) collective-permute-start(bf16[128,256]{1,0:T(8,128)(2,1)S(1)} %get-tuple-element.51), channel_id=1, source_target_pairs={{0,8},{2,10},{4,12},{6,14},{8,16},{10,18},{12,20},{14,22},{16,24},... | collective-permute-start | bytes 196616 | tf_op jit(solution)/shard_map/ppermute | solution.py:313
  10.7 2.2 %collective-permute-start.2 = (bf16[128,256]{1,0:T(8,128)(2,1)S(1)}, bf16[128,256]{1,0:T(8,128)(2,1)S(1)}, u32[]{:S(2)}, u32[]{:S(2)}) collective-permute-start(bf16[128,256]{1,0:T(8,128)(2,1)S(1)} %get-tuple-element.51), channel_id=1, source_target_pairs={{0,24},{2,26},{4,28},{6,30},{8,0},{10,2},{12,4},{14,6},{16,8},{18,... | collective-permute-start | bytes 196616 | tf_op jit(solution)/shard_map/ppermute | solution.py:313
  13.0 0.0 collective-permute-done.5
  13.0 2.3 %collective-permute-done = bf16[128,256]{1,0:T(8,128)(2,1)S(1)} collective-permute-done((bf16[128,256]{1,0:T(8,128)(2,1)S(1)}, bf16[128,256]{1,0:T(8,128)(2,1)S(1)}, u32[]{:S(2)}, u32[]{:S(2)}) %collective-permute-start) | collective-permute-done | bytes 65568 | tf_op jit(solution)/shard_map/ppermute | solution.py:313
  15.3 0.4 collective-permute-done.2
  15.7 2.5 %collective-permute-start.8 = (bf16[4,128,256]{2,1,0:T(8,128)(2,1)S(1)}, bf16[4,128,256]{2,1,0:T(8,128)(2,1)S(1)}, u32[]{:S(2)}, u32[]{:S(2)}) collective-permute-start(bf16[4,128,256]{2,1,0:T(8,128)(2,1)S(1)} %pad_maximum_fusion.refs_5_), channel_id=1, source_target_pairs={{0,6},{2,4},{4,2},{6,0},{8,14},{10,12},{12,10},{14,8},{16,22},{18,... | collective-permute-start | bytes 786440 | tf_op jit(solution)/shard_map/ppermute | solution.py:309
  18.2 0.5 collective-permute-start.7
  18.7 0.5 collective-permute-start.6
  19.3 0.8 reshape.32
  20.1 3.3 %collective-permute-start.11 = (bf16[4,128,256]{2,1,0:T(8,128)(2,1)S(1)}, bf16[4,128,256]{2,1,0:T(8,128)(2,1)S(1)}, u32[]{:S(2)}, u32[]{:S(2)}) collective-permute-start(bf16[4,128,256]{2,1,0:T(8,128)(2,1)S(1)} %pad_maximum_fusion.1.refs_5_), channel_id=1, source_target_pairs={{0,24},{2,26},{4,28},{6,30},{8,0},{10,2},{12,4},{14,6},{16,8},{18,... | collective-permute-start | bytes 786440 | tf_op jit(solution)/shard_map/ppermute | solution.py:313
  23.4 0.0 collective-permute-start.10
  23.4 2.1 %collective-permute-done.8.refs_8_ = bf16[4,128,256]{2,1,0:T(8,128)(2,1)S(1)} collective-permute-done((bf16[4,128,256]{2,1,0:T(8,128)(2,1)S(1)}, bf16[4,128,256]{2,1,0:T(8,128)(2,1)S(1)}, u32[]{:S(2)}, u32[]{:S(2)}) %collective-permute-start.8) | collective-permute-done | bytes 262176 | tf_op jit(solution)/shard_map/ppermute | solution.py:309
  25.5 0.2 collective-permute-start.9
  25.7 0.7 pad_add_fusion.refs_0_
  27.1 1.1 %collective-permute-done.7.refs_7_ = bf16[4,128,256]{2,1,0:T(8,128)(2,1)S(1)} collective-permute-done((bf16[4,128,256]{2,1,0:T(8,128)(2,1)S(1)}, bf16[4,128,256]{2,1,0:T(8,128)(2,1)S(1)}, u32[]{:S(2)}, u32[]{:S(2)}) %collective-permute-start.7) | collective-permute-done | bytes 262176 | tf_op jit(solution)/shard_map/ppermute | solution.py:309
  28.2 0.1 collective-permute-done.6.refs_6_
  28.3 9.9 %attention_backward.2 = (bf16[256,4096]{1,0:T(8,128)(2,1)}, f32[4,128,256]{2,1,0:T(8,128)S(1)}, bf16[528,256]{1,0:T(8,128)(2,1)S(1)}, bf16[528,256]{1,0:T(8,128)...) custom-call(s32[49]{0:T(128)S(1)} %pad_add_fusion.refs_0_, f32[1]{0:T(128)S(6)} %tanh.3.refs_1_, ...), custom_call_target="tpu_custom_call" | custom-call | flops 2684354560 | bytes 3145728 | tf_op jit(solution)/shard_map/attention_backward/pallas_call | solution.py:258
  38.2 1.6 %collective-permute-start.12 = (bf16[528,256]{1,0:T(8,128)(2,1)S(1)}, bf16[528,256]{1,0:T(8,128)(2,1)S(1)}, u32[]{:S(2)}, u32[]{:S(2)}) collective-permute-start(bf16[528,256]{1,0:T(8,128)(2,1)S(1)} %get-tuple-element.23), channel_id=1, source_target_pairs={{0,2},{2,0},{4,6},{6,4},{8,10},{10,8},{12,14},{14,12},{16,18},{18,... | collective-permute-start | bytes 811016 | tf_op jit(solution)/shard_map/ppermute | solution.py:309
  39.8 0.7 collective-permute-start.13
  40.5 0.0 collective-permute-done.11.refs_8_
  40.5 1.3 %collective-permute-start.14 = (bf16[528,256]{1,0:T(8,128)(2,1)S(1)}, bf16[528,256]{1,0:T(8,128)(2,1)S(1)}, u32[]{:S(2)}, u32[]{:S(2)}) collective-permute-start(bf16[528,256]{1,0:T(8,128)(2,1)S(1)} %get-tuple-element.25), channel_id=1, source_target_pairs={{0,6},{2,4},{4,2},{6,0},{8,14},{10,12},{12,10},{14,8},{16,22},{18,... | collective-permute-start | bytes 811016 | tf_op jit(solution)/shard_map/ppermute | solution.py:309
  41.8 0.6 collective-permute-done.10.refs_7_
  42.4 10.5 %attention_backward.3 = (bf16[256,4096]{1,0:T(8,128)(2,1)}, f32[4,128,256]{2,1,0:T(8,128)S(1)}, bf16[528,256]{1,0:T(8,128)(2,1)S(1)}, bf16[528,256]{1,0:T(8,128)...) custom-call(s32[49]{0:T(128)S(1)} %pad_add_fusion.refs_0_, ...), custom_call_target="tpu_custom_call", output_to_operand_aliasing={{0}: (9, {})} | custom-call | flops 2684354560 | bytes 3145728 | tf_op jit(solution)/shard_map/attention_backward/pallas_call | solution.py:258
  53.0 1.7 %collective-permute-start.19 = (bf16[528,256]{1,0:T(8,128)(2,1)S(1)}, bf16[528,256]{1,0:T(8,128)(2,1)S(1)}, u32[]{:S(2)}, u32[]{:S(2)}) collective-permute-start(bf16[528,256]{1,0:T(8,128)(2,1)S(1)} %get-tuple-element.28), channel_id=1, source_target_pairs={{0,4},{2,6},{4,0},{6,2},{8,12},{10,14},{12,8},{14,10},{16,20},{18,... | collective-permute-start | bytes 811016 | tf_op jit(solution)/shard_map/ppermute | solution.py:309
  54.7 1.5 %collective-permute-start.18 = (bf16[528,256]{1,0:T(8,128)(2,1)S(1)}, bf16[528,256]{1,0:T(8,128)(2,1)S(1)}, u32[]{:S(2)}, u32[]{:S(2)}) collective-permute-start(bf16[528,256]{1,0:T(8,128)(2,1)S(1)} %get-tuple-element.27), channel_id=1, source_target_pairs={{0,2},{2,0},{4,6},{6,4},{8,10},{10,8},{12,14},{14,12},{16,18},{18,... | collective-permute-start | bytes 811016 | tf_op jit(solution)/shard_map/ppermute | solution.py:309
  56.2 0.0 collective-permute-done.12
  56.2 0.4 collective-permute-start.20
  56.6 0.2 fusion.21
  56.8 2.8 %collective-permute-start.15 = (bf16[128,256]{1,0:T(8,128)(2,1)S(1)}, bf16[128,256]{1,0:T(8,128)(2,1)S(1)}, u32[]{:S(2)}, u32[]{:S(2)}) collective-permute-start(bf16[128,256]{1,0:T(8,128)(2,1)S(1)} %get-tuple-element.39), channel_id=1, source_target_pairs={{0,24},{2,26},{4,28},{6,30},{8,0},{10,2},{12,4},{14,6},{16,8},{18,... | collective-permute-start | bytes 196616 | tf_op jit(solution)/shard_map/ppermute | solution.py:313
  59.6 2.2 %collective-permute-done.19 = bf16[528,256]{1,0:T(8,128)(2,1)S(1)} collective-permute-done((bf16[528,256]{1,0:T(8,128)(2,1)S(1)}, bf16[528,256]{1,0:T(8,128)(2,1)S(1)}, u32[]{:S(2)}, u32[]{:S(2)}) %collective-permute-start.19) | collective-permute-done | bytes 270368 | tf_op jit(solution)/shard_map/ppermute | solution.py:309
  61.8 2.8 %collective-permute-start.16 = (bf16[128,256]{1,0:T(8,128)(2,1)S(1)}, bf16[128,256]{1,0:T(8,128)(2,1)S(1)}, u32[]{:S(2)}, u32[]{:S(2)}) collective-permute-start(bf16[128,256]{1,0:T(8,128)(2,1)S(1)} %get-tuple-element.41), channel_id=1, source_target_pairs={{0,16},{2,18},{4,20},{6,22},{8,24},{10,26},{12,28},{14,30},{16,0},... | collective-permute-start | bytes 196616 | tf_op jit(solution)/shard_map/ppermute | solution.py:313
  64.6 1.7 %collective-permute-done.20 = bf16[528,256]{1,0:T(8,128)(2,1)S(1)} collective-permute-done((bf16[528,256]{1,0:T(8,128)(2,1)S(1)}, bf16[528,256]{1,0:T(8,128)(2,1)S(1)}, u32[]{:S(2)}, u32[]{:S(2)}) %collective-permute-start.20) | collective-permute-done | bytes 270368 | tf_op jit(solution)/shard_map/ppermute | solution.py:309
  66.4 0.2 fusion.19
  66.7 0.1 select_convert_fusion
  66.8 3.0 %collective-permute-start.21 = (bf16[144,256]{1,0:T(8,128)(2,1)S(1)}, bf16[144,256]{1,0:T(8,128)(2,1)S(1)}, u32[]{:S(2)}, u32[]{:S(2)}) collective-permute-start(bf16[144,256]{1,0:T(8,128)(2,1)S(1)} %get-tuple-element.52), channel_id=1, source_target_pairs={{0,24},{2,26},{4,28},{6,30},{8,0},{10,2},{12,4},{14,6},{16,8},{18,... | collective-permute-start | bytes 221192 | tf_op jit(solution)/shard_map/ppermute | solution.py:313
  69.8 1.3 %collective-permute-start.22 = (bf16[144,256]{1,0:T(8,128)(2,1)S(1)}, bf16[144,256]{1,0:T(8,128)(2,1)S(1)}, u32[]{:S(2)}, u32[]{:S(2)}) collective-permute-start(bf16[144,256]{1,0:T(8,128)(2,1)S(1)} %get-tuple-element.53), channel_id=1, source_target_pairs={{0,16},{2,18},{4,20},{6,22},{8,24},{10,26},{12,28},{14,30},{16,0},... | collective-permute-start | bytes 221192 | tf_op jit(solution)/shard_map/ppermute | solution.py:313
  71.1 1.9 %collective-permute-start.23 = (bf16[144,256]{1,0:T(8,128)(2,1)S(1)}, bf16[144,256]{1,0:T(8,128)(2,1)S(1)}, u32[]{:S(2)}, u32[]{:S(2)}) collective-permute-start(bf16[144,256]{1,0:T(8,128)(2,1)S(1)} %get-tuple-element.54), channel_id=1, source_target_pairs={{0,8},{2,10},{4,12},{6,14},{8,16},{10,18},{12,20},{14,22},{16,24},... | collective-permute-start | bytes 221192 | tf_op jit(solution)/shard_map/ppermute | solution.py:313
  73.1 2.7 %collective-permute-done.22 = bf16[144,256]{1,0:T(8,128)(2,1)S(1)} collective-permute-done((bf16[144,256]{1,0:T(8,128)(2,1)S(1)}, bf16[144,256]{1,0:T(8,128)(2,1)S(1)}, u32[]{:S(2)}, u32[]{:S(2)}) %collective-permute-start.22) | collective-permute-done | bytes 73760 | tf_op jit(solution)/shard_map/ppermute | solution.py:313
  75.9 1.4 %collective-permute-done.23 = bf16[144,256]{1,0:T(8,128)(2,1)S(1)} collective-permute-done((bf16[144,256]{1,0:T(8,128)(2,1)S(1)}, bf16[144,256]{1,0:T(8,128)(2,1)S(1)}, u32[]{:S(2)}, u32[]{:S(2)}) %collective-permute-start.23) | collective-permute-done | bytes 73760 | tf_op jit(solution)/shard_map/ppermute | solution.py:313
  77.3 0.1 collective-permute-start.24
  77.4 0.7 fusion.10
  78.1 0.4 collective-permute-done.24
  78.5 0.6 add_reduce_fusion
  (40 shorter events, 0.4 us)
Async XLA Ops:
  1.5 9.2 %collective-permute-start.4 = (bf16[128,256]{1,0:T(8,128)(2,1)S(1)}, bf16[128,256]{1,0:T(8,128)(2,1)S(1)}, u32[]{:S(2)}, u32[]{:S(2)}) collective-permute-start(bf16[128,256]{1,0:T(8,128)(2,1)S(1)} %get-tuple-element.45), channel_id=1, source_target_pairs={{0,4},{2,6},{4,0},{6,2},{8,12},{10,14},{12,8},{14,10},{16,20},{18,... | collective-permute-start | bytes 196616 | tf_op jit(solution)/shard_map/ppermute | solution.py:309
  4.5 8.5 %collective-permute-start.3 = (bf16[128,256]{1,0:T(8,128)(2,1)S(1)}, bf16[128,256]{1,0:T(8,128)(2,1)S(1)}, u32[]{:S(2)}, u32[]{:S(2)}) collective-permute-start(bf16[128,256]{1,0:T(8,128)(2,1)S(1)} %get-tuple-element.45), channel_id=1, source_target_pairs={{0,2},{2,0},{4,6},{6,4},{8,10},{10,8},{12,14},{14,12},{16,18},{18,... | collective-permute-start | bytes 196616 | tf_op jit(solution)/shard_map/ppermute | solution.py:309
  6.0 7.0 %collective-permute-start.5 = (bf16[128,256]{1,0:T(8,128)(2,1)S(1)}, bf16[128,256]{1,0:T(8,128)(2,1)S(1)}, u32[]{:S(2)}, u32[]{:S(2)}) collective-permute-start(bf16[128,256]{1,0:T(8,128)(2,1)S(1)} %get-tuple-element.45), channel_id=1, source_target_pairs={{0,6},{2,4},{4,2},{6,0},{8,14},{10,12},{12,10},{14,8},{16,22},{18,... | collective-permute-start | bytes 196616 | tf_op jit(solution)/shard_map/ppermute | solution.py:309
  6.1 7.0 %collective-permute-start.1 = (bf16[128,256]{1,0:T(8,128)(2,1)S(1)}, bf16[128,256]{1,0:T(8,128)(2,1)S(1)}, u32[]{:S(2)}, u32[]{:S(2)}) collective-permute-start(bf16[128,256]{1,0:T(8,128)(2,1)S(1)} %get-tuple-element.51), channel_id=1, source_target_pairs={{0,16},{2,18},{4,20},{6,22},{8,24},{10,26},{12,28},{14,30},{16,0},... | collective-permute-start | bytes 196616 | tf_op jit(solution)/shard_map/ppermute | solution.py:313
  9.1 6.2 %collective-permute-start = (bf16[128,256]{1,0:T(8,128)(2,1)S(1)}, bf16[128,256]{1,0:T(8,128)(2,1)S(1)}, u32[]{:S(2)}, u32[]{:S(2)}) collective-permute-start(bf16[128,256]{1,0:T(8,128)(2,1)S(1)} %get-tuple-element.51), channel_id=1, source_target_pairs={{0,8},{2,10},{4,12},{6,14},{8,16},{10,18},{12,20},{14,22},{16,24},... | collective-permute-start | bytes 196616 | tf_op jit(solution)/shard_map/ppermute | solution.py:313
  10.7 5.0 %collective-permute-start.2 = (bf16[128,256]{1,0:T(8,128)(2,1)S(1)}, bf16[128,256]{1,0:T(8,128)(2,1)S(1)}, u32[]{:S(2)}, u32[]{:S(2)}) collective-permute-start(bf16[128,256]{1,0:T(8,128)(2,1)S(1)} %get-tuple-element.51), channel_id=1, source_target_pairs={{0,24},{2,26},{4,28},{6,30},{8,0},{10,2},{12,4},{14,6},{16,8},{18,... | collective-permute-start | bytes 196616 | tf_op jit(solution)/shard_map/ppermute | solution.py:313
  15.7 9.8 %collective-permute-start.8 = (bf16[4,128,256]{2,1,0:T(8,128)(2,1)S(1)}, bf16[4,128,256]{2,1,0:T(8,128)(2,1)S(1)}, u32[]{:S(2)}, u32[]{:S(2)}) collective-permute-start(bf16[4,128,256]{2,1,0:T(8,128)(2,1)S(1)} %pad_maximum_fusion.refs_5_), channel_id=1, source_target_pairs={{0,6},{2,4},{4,2},{6,0},{8,14},{10,12},{12,10},{14,8},{16,22},{18,... | collective-permute-start | bytes 786440 | tf_op jit(solution)/shard_map/ppermute | solution.py:309
  18.2 10.0 %collective-permute-start.7 = (bf16[4,128,256]{2,1,0:T(8,128)(2,1)S(1)}, bf16[4,128,256]{2,1,0:T(8,128)(2,1)S(1)}, u32[]{:S(2)}, u32[]{:S(2)}) collective-permute-start(bf16[4,128,256]{2,1,0:T(8,128)(2,1)S(1)} %pad_maximum_fusion.refs_5_), channel_id=1, source_target_pairs={{0,4},{2,6},{4,0},{6,2},{8,12},{10,14},{12,8},{14,10},{16,20},{18,... | collective-permute-start | bytes 786440 | tf_op jit(solution)/shard_map/ppermute | solution.py:309
  18.7 9.5 %collective-permute-start.6 = (bf16[4,128,256]{2,1,0:T(8,128)(2,1)S(1)}, bf16[4,128,256]{2,1,0:T(8,128)(2,1)S(1)}, u32[]{:S(2)}, u32[]{:S(2)}) collective-permute-start(bf16[4,128,256]{2,1,0:T(8,128)(2,1)S(1)} %pad_maximum_fusion.refs_5_), channel_id=1, source_target_pairs={{0,2},{2,0},{4,6},{6,4},{8,10},{10,8},{12,14},{14,12},{16,18},{18,... | collective-permute-start | bytes 786440 | tf_op jit(solution)/shard_map/ppermute | solution.py:309
  20.1 20.5 %collective-permute-start.11 = (bf16[4,128,256]{2,1,0:T(8,128)(2,1)S(1)}, bf16[4,128,256]{2,1,0:T(8,128)(2,1)S(1)}, u32[]{:S(2)}, u32[]{:S(2)}) collective-permute-start(bf16[4,128,256]{2,1,0:T(8,128)(2,1)S(1)} %pad_maximum_fusion.1.refs_5_), channel_id=1, source_target_pairs={{0,24},{2,26},{4,28},{6,30},{8,0},{10,2},{12,4},{14,6},{16,8},{18,... | collective-permute-start | bytes 786440 | tf_op jit(solution)/shard_map/ppermute | solution.py:313
  23.4 19.0 %collective-permute-start.10 = (bf16[4,128,256]{2,1,0:T(8,128)(2,1)S(1)}, bf16[4,128,256]{2,1,0:T(8,128)(2,1)S(1)}, u32[]{:S(2)}, u32[]{:S(2)}) collective-permute-start(bf16[4,128,256]{2,1,0:T(8,128)(2,1)S(1)} %pad_maximum_fusion.1.refs_5_), channel_id=1, source_target_pairs={{0,16},{2,18},{4,20},{6,22},{8,24},{10,26},{12,28},{14,30},{16,0},... | collective-permute-start | bytes 786440 | tf_op jit(solution)/shard_map/ppermute | solution.py:313
  25.5 16.9 %collective-permute-start.9 = (bf16[4,128,256]{2,1,0:T(8,128)(2,1)S(1)}, bf16[4,128,256]{2,1,0:T(8,128)(2,1)S(1)}, u32[]{:S(2)}, u32[]{:S(2)}) collective-permute-start(bf16[4,128,256]{2,1,0:T(8,128)(2,1)S(1)} %pad_maximum_fusion.1.refs_5_), channel_id=1, source_target_pairs={{0,8},{2,10},{4,12},{6,14},{8,16},{10,18},{12,20},{14,22},{16,24},... | collective-permute-start | bytes 786440 | tf_op jit(solution)/shard_map/ppermute | solution.py:313
  38.2 18.0 %collective-permute-start.12 = (bf16[528,256]{1,0:T(8,128)(2,1)S(1)}, bf16[528,256]{1,0:T(8,128)(2,1)S(1)}, u32[]{:S(2)}, u32[]{:S(2)}) collective-permute-start(bf16[528,256]{1,0:T(8,128)(2,1)S(1)} %get-tuple-element.23), channel_id=1, source_target_pairs={{0,2},{2,0},{4,6},{6,4},{8,10},{10,8},{12,14},{14,12},{16,18},{18,... | collective-permute-start | bytes 811016 | tf_op jit(solution)/shard_map/ppermute | solution.py:309
  39.8 16.8 %collective-permute-start.13 = (bf16[528,256]{1,0:T(8,128)(2,1)S(1)}, bf16[528,256]{1,0:T(8,128)(2,1)S(1)}, u32[]{:S(2)}, u32[]{:S(2)}) collective-permute-start(bf16[528,256]{1,0:T(8,128)(2,1)S(1)} %get-tuple-element.24), channel_id=1, source_target_pairs={{0,4},{2,6},{4,0},{6,2},{8,12},{10,14},{12,8},{14,10},{16,20},{18,... | collective-permute-start | bytes 811016 | tf_op jit(solution)/shard_map/ppermute | solution.py:309
  40.5 16.1 %collective-permute-start.14 = (bf16[528,256]{1,0:T(8,128)(2,1)S(1)}, bf16[528,256]{1,0:T(8,128)(2,1)S(1)}, u32[]{:S(2)}, u32[]{:S(2)}) collective-permute-start(bf16[528,256]{1,0:T(8,128)(2,1)S(1)} %get-tuple-element.25), channel_id=1, source_target_pairs={{0,6},{2,4},{4,2},{6,0},{8,14},{10,12},{12,10},{14,8},{16,22},{18,... | collective-permute-start | bytes 811016 | tf_op jit(solution)/shard_map/ppermute | solution.py:309
  53.0 8.8 %collective-permute-start.19 = (bf16[528,256]{1,0:T(8,128)(2,1)S(1)}, bf16[528,256]{1,0:T(8,128)(2,1)S(1)}, u32[]{:S(2)}, u32[]{:S(2)}) collective-permute-start(bf16[528,256]{1,0:T(8,128)(2,1)S(1)} %get-tuple-element.28), channel_id=1, source_target_pairs={{0,4},{2,6},{4,0},{6,2},{8,12},{10,14},{12,8},{14,10},{16,20},{18,... | collective-permute-start | bytes 811016 | tf_op jit(solution)/shard_map/ppermute | solution.py:309
  54.7 11.7 %collective-permute-start.18 = (bf16[528,256]{1,0:T(8,128)(2,1)S(1)}, bf16[528,256]{1,0:T(8,128)(2,1)S(1)}, u32[]{:S(2)}, u32[]{:S(2)}) collective-permute-start(bf16[528,256]{1,0:T(8,128)(2,1)S(1)} %get-tuple-element.27), channel_id=1, source_target_pairs={{0,2},{2,0},{4,6},{6,4},{8,10},{10,8},{12,14},{14,12},{16,18},{18,... | collective-permute-start | bytes 811016 | tf_op jit(solution)/shard_map/ppermute | solution.py:309
  56.2 10.2 %collective-permute-start.20 = (bf16[528,256]{1,0:T(8,128)(2,1)S(1)}, bf16[528,256]{1,0:T(8,128)(2,1)S(1)}, u32[]{:S(2)}, u32[]{:S(2)}) collective-permute-start(bf16[528,256]{1,0:T(8,128)(2,1)S(1)} %get-tuple-element.29), channel_id=1, source_target_pairs={{0,6},{2,4},{4,2},{6,0},{8,14},{10,12},{12,10},{14,8},{16,22},{18,... | collective-permute-start | bytes 811016 | tf_op jit(solution)/shard_map/ppermute | solution.py:309
  56.8 14.3 %collective-permute-start.15 = (bf16[128,256]{1,0:T(8,128)(2,1)S(1)}, bf16[128,256]{1,0:T(8,128)(2,1)S(1)}, u32[]{:S(2)}, u32[]{:S(2)}) collective-permute-start(bf16[128,256]{1,0:T(8,128)(2,1)S(1)} %get-tuple-element.39), channel_id=1, source_target_pairs={{0,24},{2,26},{4,28},{6,30},{8,0},{10,2},{12,4},{14,6},{16,8},{18,... | collective-permute-start | bytes 196616 | tf_op jit(solution)/shard_map/ppermute | solution.py:313
  59.6 13.5 %collective-permute-start.17 = (bf16[128,256]{1,0:T(8,128)(2,1)S(1)}, bf16[128,256]{1,0:T(8,128)(2,1)S(1)}, u32[]{:S(2)}, u32[]{:S(2)}) collective-permute-start(bf16[128,256]{1,0:T(8,128)(2,1)S(1)} %get-tuple-element.40), channel_id=1, source_target_pairs={{0,8},{2,10},{4,12},{6,14},{8,16},{10,18},{12,20},{14,22},{16,24},... | collective-permute-start | bytes 196616 | tf_op jit(solution)/shard_map/ppermute | solution.py:313
  61.8 11.3 %collective-permute-start.16 = (bf16[128,256]{1,0:T(8,128)(2,1)S(1)}, bf16[128,256]{1,0:T(8,128)(2,1)S(1)}, u32[]{:S(2)}, u32[]{:S(2)}) collective-permute-start(bf16[128,256]{1,0:T(8,128)(2,1)S(1)} %get-tuple-element.41), channel_id=1, source_target_pairs={{0,16},{2,18},{4,20},{6,22},{8,24},{10,26},{12,28},{14,30},{16,0},... | collective-permute-start | bytes 196616 | tf_op jit(solution)/shard_map/ppermute | solution.py:313
  66.8 6.3 %collective-permute-start.21 = (bf16[144,256]{1,0:T(8,128)(2,1)S(1)}, bf16[144,256]{1,0:T(8,128)(2,1)S(1)}, u32[]{:S(2)}, u32[]{:S(2)}) collective-permute-start(bf16[144,256]{1,0:T(8,128)(2,1)S(1)} %get-tuple-element.52), channel_id=1, source_target_pairs={{0,24},{2,26},{4,28},{6,30},{8,0},{10,2},{12,4},{14,6},{16,8},{18,... | collective-permute-start | bytes 221192 | tf_op jit(solution)/shard_map/ppermute | solution.py:313
  69.8 6.0 %collective-permute-start.22 = (bf16[144,256]{1,0:T(8,128)(2,1)S(1)}, bf16[144,256]{1,0:T(8,128)(2,1)S(1)}, u32[]{:S(2)}, u32[]{:S(2)}) collective-permute-start(bf16[144,256]{1,0:T(8,128)(2,1)S(1)} %get-tuple-element.53), channel_id=1, source_target_pairs={{0,16},{2,18},{4,20},{6,22},{8,24},{10,26},{12,28},{14,30},{16,0},... | collective-permute-start | bytes 221192 | tf_op jit(solution)/shard_map/ppermute | solution.py:313
  71.1 6.2 %collective-permute-start.23 = (bf16[144,256]{1,0:T(8,128)(2,1)S(1)}, bf16[144,256]{1,0:T(8,128)(2,1)S(1)}, u32[]{:S(2)}, u32[]{:S(2)}) collective-permute-start(bf16[144,256]{1,0:T(8,128)(2,1)S(1)} %get-tuple-element.54), channel_id=1, source_target_pairs={{0,8},{2,10},{4,12},{6,14},{8,16},{10,18},{12,20},{14,22},{16,24},... | collective-permute-start | bytes 221192 | tf_op jit(solution)/shard_map/ppermute | solution.py:313
  77.3 1.2 %collective-permute-start.24 = (f32[1,256]{1,0:T(1,128)S(1)}, f32[1,256]{1,0:T(1,128)S(1)}, u32[]{:S(2)}, u32[]{:S(2)}) collective-permute-start(f32[1,256]{1,0:T(1,128)S(1)} %fusion.11), channel_id=1, source_target_pairs={{0,1},{1,0},{2,3},{3,2},{4,5},{5,4},{6,7},{7,6},{8,9},{9,8},{10,11... | collective-permute-start | bytes 3080 | tf_op jit(solution)/shard_map/ppermute | solution.py:369

commit v4 on v3

v4 whole, which is shorter than its diff:
```python
import functools
import math

import jax
import jax.numpy as jnp
from jax import lax
from jax.experimental import pallas as pl
from jax.experimental.pallas import tpu as pltpu
from jax.sharding import PartitionSpec as P

HD = 128
BLK = 128
JOIN = 4
FIRST = 0
MERGE = 2
CHUNKS = 2
CODE = 16
NT = (((1,), (1,)), ((), ()))
F32, BF16 = jnp.float32, jnp.bfloat16


def coded(value, rows, rounded):
    high = rounded(value)
    middle = rounded(value - high)
    low = value - high - middle
    shape = (rows, value.shape[1])
    row = lax.broadcasted_iota(jnp.int32, shape, 0)
    parts = jnp.where(row == 0, high, jnp.zeros(shape, F32))
    return jnp.where(row == 1, middle, jnp.where(row == 2, low, parts)).astype(BF16)


def rounded_here(value):
    return value.astype(BF16).astype(F32)


def rounded_outside(value):
    return lax.reduce_precision(value, 8, 7)


def decoded(rows):
    rows = rows.astype(F32)
    return rows[0:1] + rows[1:2] + rows[2:3]


def plan_images(n, n_blocks, n_images, plan_ref, place, bias):
    read_most = n_images // 2
    me = plan_ref[(n_blocks + 1) * n_images]
    for j in range(read_most):
        place[0, j] = 0
        place[1, j] = 0
        for b in range(n_blocks):
            bias[b, j] = jnp.float32(-1e30)

    def look(i, count):
        reads = [plan_ref[b * n_images + i] > 0 for b in range(n_blocks)]
        any_read = functools.reduce(jnp.logical_or, reads)

        @pl.when(jnp.logical_and(any_read, count < read_most))
        def _():
            slot = plan_ref[n_blocks * n_images + i]
            column = jnp.bitwise_xor(lax.rem(slot, 4), lax.rem(me, 4))
            behind = lax.rem(lax.div(me, 4) - lax.div(slot, 4) + n, n)
            place[0, count] = column * n + behind
            place[1, count] = behind * 4 + column
            for b in range(n_blocks):
                bias[b, count] = jnp.where(reads[b], 0.0, -1e30).astype(F32)

        return count + any_read.astype(jnp.int32)

    lax.fori_loop(0, n_images, look, jnp.int32(0))


def attention_kernel(n, n_blocks, n_images, lead, first, heads, total_kv, n_columns, *refs):
    gate_ref, gate_in = refs[:2]
    columns = refs[2 : 2 + n_columns]
    refs = refs[2 + n_columns :]
    if lead:
        plan_ref, q_hbm, cot_hbm, place, bias, q_ref, cot_ref = refs[:7]
    else:
        place, bias, q_ref, cot_ref = refs[:4]
    refs = refs[7 if lead else 4 :]
    ds_ref, kt_sel, own_ref = refs[:3]
    back_refs = refs[3:6]
    gate_out, k_all, v_all, k_sel, v_sel, dk_acc, dv_acc, dk_all, dv_all, sem = refs[6:]
    read_most = n_images // 2
    img_tok = k_all.shape[2]
    per_head = ds_ref.shape[1]
    groups = per_head // n_blocks
    width = groups * HD
    gate_value = gate_ref[0]
    inv_root = 1.0 / math.sqrt(HD)
    to_exp2 = math.log2(math.e) * inv_root

    copies = []
    if lead:
        edges = [h * width for h in range(heads + 1)] + [total_kv * width]
        for k in range(heads + 1):
            span = slice(edges[k], edges[k + 1])
            if edges[k + 1] > edges[k]:
                for u, (src, dst) in enumerate(((q_hbm, q_ref), (cot_hbm, cot_ref))):
                    copies.append(
                        pltpu.make_async_copy(src.at[:, span], dst.at[:, span], sem.at[k, u])
                    )
                    copies[-1].start()
        plan_images(n, n_blocks, n_images, plan_ref, place, bias)

    for h in range(heads):
        lanes = slice(h * HD, (h + 1) * HD)
        at = 0
        for column in columns:
            count = column.shape[0]
            k_all[h, at : at + count] = column[:, :img_tok, lanes]
            v_all[h, at : at + count] = column[:, img_tok:, lanes]
            at += count
        for j in range(read_most):
            rows = slice(j * img_tok, (j + 1) * img_tok)
            where = place[0 if lead else 1, j]
            k_sel[h, rows] = k_all[h, where]
            v_sel[h, rows] = v_all[h, where]
        kt_sel[h] = k_sel[h].astype(F32).T.astype(BF16)
    dk_acc[...] = jnp.zeros_like(dk_acc)
    dv_acc[...] = jnp.zeros_like(dv_acc)

    def tile_of(ref, i):
        h, b, g = i // per_head, i % per_head // groups, i % groups
        lane = ((first + h) * groups + g) * HD
        return ref[b * BLK : (b + 1) * BLK, lane : lane + HD]

    def products(i):
        h = i // per_head
        scores = lax.dot_general(k_sel[h], tile_of(q_ref, i), NT, preferred_element_type=F32)
        prob_grad = lax.dot_general(v_sel[h], tile_of(cot_ref, i), NT, preferred_element_type=F32)
        return scores, prob_grad

    def softmax(i, scores, prob_grad):
        h, b = i // per_head, i % per_head // groups
        images = [scores[j * img_tok : (j + 1) * img_tok] for j in range(read_most)]
        tops = [
            jnp.max(image.reshape(img_tok // 8, 8, BLK), axis=0) + bias[b, j]
            for j, image in enumerate(images)
        ]
        row_max = jnp.max(functools.reduce(jnp.maximum, tops), axis=0, keepdims=True)
        terms = [
            jnp.exp2((image - (row_max - bias[b, j])) * to_exp2) for j, image in enumerate(images)
        ]
        terms = jnp.concatenate(terms, axis=0)
        prob = terms * (1.0 / jnp.sum(terms, axis=0, keepdims=True))
        delta = jnp.sum(prob * prob_grad, axis=0, keepdims=True)
        score_grad = (prob * (prob_grad - delta)).astype(BF16)
        ds_ref[h, i % per_head] = score_grad
        return prob.astype(BF16), score_grad

    def gradients(pieces):
        h = pieces[0][0] // per_head
        query = jnp.concatenate([tile_of(q_ref, i) for i, _, _ in pieces], axis=0)
        cot = jnp.concatenate([tile_of(cot_ref, i) for i, _, _ in pieces], axis=0)
        prob_half = jnp.concatenate([p for _, p, _ in pieces], axis=1)
        score_grad = jnp.concatenate([d for _, _, d in pieces], axis=1)
        dk_acc[h] += jnp.dot(score_grad, query, preferred_element_type=F32)
        dv_acc[h] += jnp.dot(prob_half, cot, preferred_element_type=F32)

    items = heads * per_head
    ready, held = None, []
    for at in range(items + 2):
        if at < items and at % per_head == 0:
            for copy in copies[2 * (at // per_head) : 2 * (at // per_head) + 2]:
                copy.wait()
        fresh = products(at) if at < items else None
        middle = (at - 1, *softmax(at - 1, *ready)) if ready is not None else None
        if len(held) == MERGE:
            gradients(held)
            held = []
        if middle is not None:
            held.append(middle)
        ready = fresh

    gate_row = jnp.zeros((1, HD), F32)
    for h in range(heads):
        lanes = slice(h * HD, (h + 1) * HD)
        dk_all[h] = jnp.zeros_like(dk_all[h])
        dv_all[h] = jnp.zeros_like(dv_all[h])
        for j in range(read_most):
            rows = slice(j * img_tok, (j + 1) * img_tok)
            dk_all[h, place[0, j]] = dk_acc[h, rows] * (gate_value * inv_root)
            dv_all[h, place[0, j]] = dv_acc[h, rows] * gate_value
        own_ref[:, :img_tok, lanes] = dk_all[h, 0:n]
        own_ref[:, img_tok:, lanes] = dv_all[h, 0:n]
        for a in range(1, 4):
            out, rows = back_refs[a - 1], 2 * img_tok
            for k in range(n):
                dk, dv = dk_all[h, a * n + k], dv_all[h, a * n + k]
                out[k * rows : k * rows + img_tok, lanes] = dk.astype(BF16)
                out[k * rows + img_tok : (k + 1) * rows, lanes] = dv.astype(BF16)
        gate_row += jnp.sum(dv_acc[h] * v_sel[h].astype(F32), axis=0, keepdims=True)
    gate_row = jnp.broadcast_to(jnp.sum(gate_row, axis=1, keepdims=True), (1, HD))
    gate_row += gate_in[0:1]
    gate_out[...] = jnp.broadcast_to(gate_row, gate_out.shape)
    rest = 2 * n * img_tok
    for out in back_refs:
        for h in range(heads):
            lanes = slice(h * HD, (h + 1) * HD)
            out[rest:, lanes] = coded(gate_row, CODE, rounded_here)
    for copy in copies[2 * heads :]:
        copy.wait()


def attention(at, sizes, gate_value, gate_in, columns, lead_in, shared):
    n, n_blocks, n_images, heads, total_kv, tokens = sizes
    lead = shared is None
    read_most = n_images // 2
    img_tok = columns[0].shape[1] // 2
    queries = lead_in[1]
    groups = queries.shape[1] // HD // total_kv
    per_head = groups * n_blocks
    n_keys = read_most * img_tok
    smem = pl.BlockSpec(memory_space=pltpu.SMEM)
    vmem = pl.BlockSpec(memory_space=pltpu.VMEM)
    hbm = pl.BlockSpec(memory_space=pltpu.HBM)
    span = heads * HD
    args = [gate_value, gate_in, *columns]
    in_specs = [smem] + [vmem] * (1 + len(columns))
    out_shape, out_specs = [], []
    if lead:
        args.append(lead_in[0])
        args += [pltpu.with_memory_space_constraint(x, pltpu.HBM) for x in lead_in[1:]]
        in_specs += [smem, hbm, hbm]
        out_shape += [
            jax.ShapeDtypeStruct((2, read_most), jnp.int32),
            jax.ShapeDtypeStruct((n_blocks, read_most), F32),
            pltpu.VMEM(queries.shape, BF16),
            pltpu.VMEM(queries.shape, BF16),
        ]
        out_specs += [smem, smem, vmem, vmem]
    else:
        args += shared
        in_specs += [smem, smem, vmem, vmem]
    tail_shape = [
        pltpu.VMEM((heads, per_head, n_keys, BLK), BF16),
        pltpu.VMEM((heads, HD, n_keys), BF16),
        jax.ShapeDtypeStruct((n, 2 * img_tok, span), F32),
    ]
    tail_shape += [jax.ShapeDtypeStruct((2 * n * img_tok + CODE, span), BF16)] * 3
    tail_shape.append(jax.ShapeDtypeStruct((8, HD), F32))
    out_shape += tail_shape
    out_specs += [vmem] * len(tail_shape)
    rows = tokens * groups * heads
    kernel = functools.partial(
        attention_kernel, n, n_blocks, n_images, lead, at * heads, heads, total_kv, len(columns)
    )
    return pl.pallas_call(
        kernel,
        in_specs=in_specs,
        out_specs=out_specs,
        out_shape=out_shape,
        scratch_shapes=[
            pltpu.VMEM((heads, 4 * n, img_tok, HD), BF16),
            pltpu.VMEM((heads, 4 * n, img_tok, HD), BF16),
            pltpu.VMEM((heads, n_keys, HD), BF16),
            pltpu.VMEM((heads, n_keys, HD), BF16),
            pltpu.VMEM((heads, n_keys, HD), F32),
            pltpu.VMEM((heads, n_keys, HD), F32),
            pltpu.VMEM((heads, 4 * n, img_tok, HD), F32),
            pltpu.VMEM((heads, 4 * n, img_tok, HD), F32),
            pltpu.SemaphoreType.DMA((heads + 1, 2)),
        ],
        compiler_params=pltpu.CompilerParams(vmem_limit_bytes=vmem_bytes(n_keys)),
        cost_estimate=pl.CostEstimate(
            flops=8 * rows * n_keys * HD,
            bytes_accessed=4 * rows * HD,
            transcendentals=rows * n_keys,
        ),
        name="attention_backward",
    )(*args)


def vmem_bytes(n_keys):
    return min(44, 14 + 15 * n_keys // 1024) * 1024 * 1024


def query_kernel(first, n_blocks, n_extra, gate_ref, ds_ref, kt_ref, *rest):
    dq_hbm, dq_ref, sem = rest[n_extra:]
    heads, per_head = ds_ref.shape[:2]
    groups = per_head // n_blocks
    width = groups * HD
    scale = gate_ref[0] * (1.0 / math.sqrt(HD))
    copies = []
    for h in range(heads):
        for i in range(0, per_head, JOIN):
            b, g = i // groups, i % groups
            score_grad = jnp.concatenate([ds_ref[h, i + u] for u in range(JOIN)], axis=1)
            dq = jnp.dot(kt_ref[h], score_grad, preferred_element_type=F32)
            dq = (dq.T * scale).astype(BF16)
            for u in range(JOIN):
                lanes = slice((g + u) * HD, (g + u + 1) * HD)
                dq_ref[h, b * BLK : (b + 1) * BLK, lanes] = dq[u * BLK : (u + 1) * BLK]
        span = pl.ds((first + h) * width, width)
        copies.append(pltpu.make_async_copy(dq_ref.at[h], dq_hbm.at[:, span], sem.at[h]))
        copies[-1].start()
    for copy in copies:
        copy.wait()


def query_gradient(at, sizes, shape, prev, after, gate_value, ds, kt):
    n, n_blocks, n_images, heads, total_kv, tokens = sizes
    hbm = pl.BlockSpec(memory_space=pltpu.HBM)
    vmem = pl.BlockSpec(memory_space=pltpu.VMEM)
    anywhere = pl.BlockSpec(memory_space=pl.ANY)
    extra = ([] if prev is None else [prev]) + after
    specs = ([] if prev is None else [hbm]) + [anywhere] * len(after)
    return pl.pallas_call(
        functools.partial(query_kernel, at * heads, n_blocks, len(extra)),
        in_specs=[pl.BlockSpec(memory_space=pltpu.SMEM), vmem, vmem] + specs,
        out_specs=hbm,
        out_shape=pltpu.HBM(shape, BF16),
        input_output_aliases={} if prev is None else {3: 0},
        scratch_shapes=[
            pltpu.VMEM((heads, shape[0], shape[1] // total_kv), BF16),
            pltpu.SemaphoreType.DMA((heads,)),
        ],
        compiler_params=pltpu.CompilerParams(vmem_limit_bytes=16 * 1024 * 1024),
        cost_estimate=pl.CostEstimate(
            flops=2 * ds.size * HD, bytes_accessed=2 * ds.size, transcendentals=0
        ),
        name="query_gradient",
    )(gate_value, ds, kt, *extra)


def per_device(queries, cotangent, image_keys, image_values, attn_gate, block_mask, image_owner):
    n_ctx = lax.axis_size("ctx")
    n_tp = lax.axis_size("tp")
    n = n_ctx // 4
    img_tok = image_keys.shape[1]
    local_kv = image_keys.shape[2] // HD
    chunks = min(CHUNKS, local_kv)
    heads = local_kv // chunks
    me = lax.axis_index("ctx").astype(jnp.int32).reshape(1)
    plan = jnp.concatenate([block_mask.reshape(-1), image_owner, me])
    gate_value = jnp.tanh(attn_gate)

    def swap(value, bit):
        return lax.ppermute(value, "ctx", [(i, i ^ bit) for i in range(n_ctx)])

    def turn(value, by):
        pairs = [(i, (i // 4 + by) % n * 4 + i % 4) for i in range(n_ctx)]
        return lax.ppermute(value, "ctx", pairs)

    def own_columns(c):
        lanes = slice(c * heads * HD, (c + 1) * heads * HD)
        return jnp.concatenate([image_keys[0, :, lanes], image_values[0, :, lanes]], axis=0)

    def square_of(own):
        pair = jnp.stack([own, swap(own, 1)])
        return jnp.concatenate([pair, swap(pair, 2)])

    def column_of(own):
        return jnp.stack([own] + [turn(own, k) for k in range(1, n)])

    def square_sum(own, backs, came):
        rest = 2 * n * img_tok
        total, gate = own, decoded(backs[0][rest:])
        for part in came:
            total = total + part[:rest].reshape(own.shape).astype(F32)
            gate = gate + decoded(part[rest:])
        return total, gate

    def return_column(both, gate, last):
        total, gate_total = both[0], gate
        sends = both.astype(BF16)
        for k in range(1, n):
            send = sends[k]
            if last:
                send = jnp.concatenate([send, coded(gate, CODE, rounded_outside)])
            came = turn(send, -k)
            total = total + came[: 2 * img_tok].astype(F32)
            if last:
                gate_total = gate_total + decoded(came[2 * img_tok :])
        return total, gate_total

    owns = [own_columns(c) for c in range(chunks)]
    starts = [square_of(own) if c else column_of(own) for c, own in enumerate(owns)]
    if chunks > 1:
        starts = lax.optimization_barrier(starts)
    column = starts[0]
    gathered = [[column, swap(column, 1), swap(column, 2), swap(column, 3)]]
    for square in starts[1:]:
        gathered.append([square] + [turn(square, k) for k in range(1, n)])
    sizes = (n, *block_mask.shape, heads, local_kv, queries.shape[0])
    lead_in = (plan, queries, cotangent)
    gate_part = jnp.zeros((8, HD), F32)
    shared, parts, dq = None, [], None
    saved, waiting = [], None
    for c in range(chunks):
        last = c == chunks - 1
        outs = attention(c, sizes, gate_value, gate_part, gathered[c], lead_in, shared)
        if shared is None:
            shared, outs = outs[:4], outs[4:]
        ds, kt, own, *backs, gate_part = outs
        saved.append((ds, kt))
        if c:
            held = lax.optimization_barrier((tuple(backs), waiting[2]))
            backs = held[0]
            both, gate = square_sum(waiting[0], waiting[1], held[1])
            total, gate_row = return_column(both, gate, False)
            parts.append(total.astype(BF16))
        came = [swap(back, a + 1) for a, back in enumerate(backs)]
        waiting = (own, backs, tuple(came))
        if last:
            for k, (ds, kt) in enumerate(saved):
                after = came[FIRST : FIRST + 1] if k == c else []
                dq = query_gradient(k, sizes, queries.shape, dq, after, gate_value, ds, kt)
            *came, dq = lax.optimization_barrier((*came, dq))
    both, gate = square_sum(own, backs, came)
    total, gate_row = return_column(both, gate, True)
    parts.append(total.astype(BF16))
    grads = jnp.concatenate(parts, axis=1)
    key_grad, value_grad = grads[None, :img_tok], grads[None, img_tok:]
    gate_total = gate_row
    for k in range(1, n_tp):
        pairs = [(i, (i + k) % n_tp) for i in range(n_tp)]
        gate_total = gate_total + lax.ppermute(gate_row, "tp", pairs)
    term_count = queries.shape[0] * n_ctx * queries.shape[1] * n_tp
    gate_row = gate_total[0, :HD] * (1.0 / math.sqrt(term_count))
    gate_grad = ((1.0 - gate_value * gate_value) * gate_row)[:1]
    return (dq, key_grad, value_grad, gate_grad)


def solution(mesh):
    in_specs = (
        P("ctx", "tp"),
        P("ctx", "tp"),
        P("ctx", None, "tp"),
        P("ctx", None, "tp"),
        P(),
        P("ctx", None),
        P(),
    )
    out_specs = (P("ctx", "tp"), P("ctx", None, "tp"), P("ctx", None, "tp"), P())
    return jax.shard_map(
        per_device, mesh=mesh, in_specs=in_specs, out_specs=out_specs, check_vma=False
    )
```

time: 81.2 us -> 74.6 us (0.919)
  starting transfers between devices: 37.6 us -> 33.7 us
  between operations: 3.33 us -> 1.57 us
  waiting for transfers between devices: 15.1 us -> 14.1 us
    ppermute x12, starting transfers between devices: 22.3 us -> 18.4 us  [turn(): return lax.ppermute(value, 'ctx', pairs)]
    ppermute x12, waiting for transfers between devices: 7.46 us -> 5.94 us  [turn(): return lax.ppermute(value, 'ctx', pairs)]
    ppermute x12 -> x11, waiting for transfers between devices: 7.2 us -> 7.74 us  [swap(): return lax.ppermute(value, 'ctx', [(i, i ^ bit) for i in range(n_ctx)])]
    pallas_call x2 -> x4, Pallas kernels: 20.5 us -> 20.8 us  [the longest x2 17.3 us: attention(): pl.pallas_call(kernel, in_specs=in_specs, out_specs=out_specs, out_shape=...]
    ppermute x12 -> x11, starting transfers between devices: 15.2 us -> 15.2 us  [swap(): return lax.ppermute(value, 'ctx', [(i, i ^ bit) for i in range(n_ctx)])]
  transfers between devices with their start and end apart: 25 -> 24, of which waited for: 11 -> 12; matrix products, arithmetic and copies ran while one was open for 4% -> 4% of each run, Pallas kernels for 25% -> 28%
where the time goes in v4:
time: 74.6 us; the launch traced here: 74.4 us
  starting transfers between devices  33.7 us (45%)
  Pallas kernels  20.8 us (28%)
  waiting for transfers between devices  14.1 us (19%)
  other arithmetic  2.5 us (3%)
  local copies, waits for them, and re-layouts  1.72 us (2%)
  between operations  1.57 us (2%)
    ppermute x12, starting transfers between devices, turn(): return lax.ppermute(value, 'ctx', pairs)  18.4 us
    pallas_call x2, Pallas kernels, attention(): pl.pallas_call(kernel, in_specs=in_specs, out_specs=out_specs, out_shape=...  17.3 us
    ppermute x11, starting transfers between devices, swap(): return lax.ppermute(value, 'ctx', [(i, i ^ bit) for i in range(n_ctx)])  15.2 us
    ppermute x11, waiting for transfers between devices, swap(): return lax.ppermute(value, 'ctx', [(i, i ^ bit) for i in range(n_ctx)])  7.74 us
    ppermute x12, waiting for transfers between devices, turn(): return lax.ppermute(value, 'ctx', pairs)  5.94 us
    pallas_call x2, Pallas kernels, query_gradient(): pl.pallas_call(functools.partial(query_kernel, at * heads, n_blocks, len(...  3.45 us
  transfers between devices with their start and end apart: 24, of which 12 were waited for; matrix products, arithmetic and copies ran while one was open for 4% of the time, Pallas kernels for 28%

profile of v4, /device:TPU:0, one launch (start us, length us, event | category | flops | bytes accessed | tf_op | source)
XLA Modules:
  0.0 74.4 jit_solution(4363332390984671776)
XLA Ops:
  0.6 0.8 %slice_bitcast_fusion.8 = (bf16[64,256]{1,0:T(8,128)(2,1)S(1)}, bf16[64,256]{1,0:T(8,128)(2,1)S(1)}, bf16[64,256]{1,0:T(8,128)(2,1)S(1)}, bf16[64,256]{1,0:T(8,128)(2,1)S(1)}) fusion(bf16[1,64,512]{2,1,0:T(8,128)(2,1)} %param.10, bf16[1,64,512]{2,1,0:T(8,128)(2,1)} %param.9), kind=kLoop, calls=%fused_computation.36 | loop fusion | bytes 262144 | tf_op jit(solution)/shard_map/squeeze | solution.py:349
  1.5 3.0 %collective-permute-start.3 = (bf16[128,256]{1,0:T(8,128)(2,1)S(1)}, bf16[128,256]{1,0:T(8,128)(2,1)S(1)}, u32[]{:S(2)}, u32[]{:S(2)}) collective-permute-start(bf16[128,256]{1,0:T(8,128)(2,1)S(1)} %get-tuple-element.77), channel_id=1, source_target_pairs={{0,2},{2,0},{4,6},{6,4},{8,10},{10,8},{12,14},{14,12},{16,18},{18,... | collective-permute-start | bytes 196616 | tf_op jit(solution)/shard_map/ppermute | solution.py:341
  4.5 1.6 %collective-permute-start = (bf16[128,256]{1,0:T(8,128)(2,1)S(1)}, bf16[128,256]{1,0:T(8,128)(2,1)S(1)}, u32[]{:S(2)}, u32[]{:S(2)}) collective-permute-start(bf16[128,256]{1,0:T(8,128)(2,1)S(1)} %get-tuple-element.83), channel_id=1, source_target_pairs={{0,8},{2,10},{4,12},{6,14},{8,16},{10,18},{12,20},{14,22},{16,24},... | collective-permute-start | bytes 196616 | tf_op jit(solution)/shard_map/ppermute | solution.py:345
  6.1 2.6 %collective-permute-start.1 = (bf16[128,256]{1,0:T(8,128)(2,1)S(1)}, bf16[128,256]{1,0:T(8,128)(2,1)S(1)}, u32[]{:S(2)}, u32[]{:S(2)}) collective-permute-start(bf16[128,256]{1,0:T(8,128)(2,1)S(1)} %get-tuple-element.83), channel_id=1, source_target_pairs={{0,16},{2,18},{4,20},{6,22},{8,24},{10,26},{12,28},{14,30},{16,0},... | collective-permute-start | bytes 196616 | tf_op jit(solution)/shard_map/ppermute | solution.py:345
  8.7 1.3 %collective-permute-start.2 = (bf16[128,256]{1,0:T(8,128)(2,1)S(1)}, bf16[128,256]{1,0:T(8,128)(2,1)S(1)}, u32[]{:S(2)}, u32[]{:S(2)}) collective-permute-start(bf16[128,256]{1,0:T(8,128)(2,1)S(1)} %get-tuple-element.83), channel_id=1, source_target_pairs={{0,24},{2,26},{4,28},{6,30},{8,0},{10,2},{12,4},{14,6},{16,8},{18,... | collective-permute-start | bytes 196616 | tf_op jit(solution)/shard_map/ppermute | solution.py:345
  10.1 1.6 %collective-permute-start.4 = (bf16[2,128,256]{2,1,0:T(8,128)(2,1)S(1)}, bf16[2,128,256]{2,1,0:T(8,128)(2,1)S(1)}, u32[]{:S(2)}, u32[]{:S(2)}) collective-permute-start(bf16[2,128,256]{2,1,0:T(8,128)(2,1)S(1)} %pad_maximum_fusion.2), channel_id=1, source_target_pairs={{0,4},{2,6},{4,0},{6,2},{8,12},{10,14},{12,8},{14,10},{16,20},{18,... | collective-permute-start | bytes 393224 | tf_op jit(solution)/shard_map/ppermute | solution.py:341
  11.7 1.8 %collective-permute-done.1 = bf16[128,256]{1,0:T(8,128)(2,1)S(1)} collective-permute-done((bf16[128,256]{1,0:T(8,128)(2,1)S(1)}, bf16[128,256]{1,0:T(8,128)(2,1)S(1)}, u32[]{:S(2)}, u32[]{:S(2)}) %collective-permute-start.1) | collective-permute-done | bytes 65568 | tf_op jit(solution)/shard_map/ppermute | solution.py:345
  13.5 0.0 collective-permute-done.2
  13.5 1.6 %collective-permute-done.4 = bf16[2,128,256]{2,1,0:T(8,128)(2,1)S(1)} collective-permute-done((bf16[2,128,256]{2,1,0:T(8,128)(2,1)S(1)}, bf16[2,128,256]{2,1,0:T(8,128)(2,1)S(1)}, u32[]{:S(2)}, u32[]{:S(2)}) %collective-permute-start.4) | collective-permute-done | bytes 131104 | tf_op jit(solution)/shard_map/ppermute | solution.py:341
  15.1 0.6 collective-permute-start.5
  15.7 1.5 %collective-permute-start.6 = (bf16[4,128,256]{2,1,0:T(8,128)(2,1)S(1)}, bf16[4,128,256]{2,1,0:T(8,128)(2,1)S(1)}, u32[]{:S(2)}, u32[]{:S(2)}) collective-permute-start(bf16[4,128,256]{2,1,0:T(8,128)(2,1)S(1)} %pad_maximum_fusion.refs_2_), channel_id=1, source_target_pairs={{0,4},{2,6},{4,0},{6,2},{8,12},{10,14},{12,8},{14,10},{16,20},{18,... | collective-permute-start | bytes 786440 | tf_op jit(solution)/shard_map/ppermute | solution.py:341
  17.3 1.4 %collective-permute-start.7 = (bf16[4,128,256]{2,1,0:T(8,128)(2,1)S(1)}, bf16[4,128,256]{2,1,0:T(8,128)(2,1)S(1)}, u32[]{:S(2)}, u32[]{:S(2)}) collective-permute-start(bf16[4,128,256]{2,1,0:T(8,128)(2,1)S(1)} %pad_maximum_fusion.refs_2_), channel_id=1, source_target_pairs={{0,6},{2,4},{4,2},{6,0},{8,14},{10,12},{12,10},{14,8},{16,22},{18,... | collective-permute-start | bytes 786440 | tf_op jit(solution)/shard_map/ppermute | solution.py:341
  19.4 0.8 %reshape.37 = s32[32]{0:T(128)S(1)} reshape(s32[2,16]{1,0:T(2,128)} %param.12) | data formatting | bytes 256 | tf_op jit(solution)/shard_map/reshape | solution.py:337
  20.2 1.1 %collective-permute-start.10 = (bf16[4,128,256]{2,1,0:T(8,128)(2,1)S(1)}, bf16[4,128,256]{2,1,0:T(8,128)(2,1)S(1)}, u32[]{:S(2)}, u32[]{:S(2)}) collective-permute-start(bf16[4,128,256]{2,1,0:T(8,128)(2,1)S(1)} %pad_maximum_fusion.1.refs_2_), channel_id=1, source_target_pairs={{0,24},{2,26},{4,28},{6,30},{8,0},{10,2},{12,4},{14,6},{16,8},{18,... | collective-permute-start | bytes 786440 | tf_op jit(solution)/shard_map/ppermute | solution.py:345
  21.3 0.7 pad_add_fusion.refs_6_
  22.0 0.9 %collective-permute-start.8 = (bf16[4,128,256]{2,1,0:T(8,128)(2,1)S(1)}, bf16[4,128,256]{2,1,0:T(8,128)(2,1)S(1)}, u32[]{:S(2)}, u32[]{:S(2)}) collective-permute-start(bf16[4,128,256]{2,1,0:T(8,128)(2,1)S(1)} %pad_maximum_fusion.1.refs_2_), channel_id=1, source_target_pairs={{0,8},{2,10},{4,12},{6,14},{8,16},{10,18},{12,20},{14,22},{16,24},... | collective-permute-start | bytes 786440 | tf_op jit(solution)/shard_map/ppermute | solution.py:345
  22.9 1.2 %collective-permute-done.5.refs_3_ = bf16[4,128,256]{2,1,0:T(8,128)(2,1)S(1)} collective-permute-done((bf16[4,128,256]{2,1,0:T(8,128)(2,1)S(1)}, bf16[4,128,256]{2,1,0:T(8,128)(2,1)S(1)}, u32[]{:S(2)}, u32[]{:S(2)}) %collective-permute-start.5) | collective-permute-done | bytes 262176 | tf_op jit(solution)/shard_map/ppermute | solution.py:341
  24.1 0.5 collective-permute-start.9
  24.6 1.7 %collective-permute-done.6.refs_4_ = bf16[4,128,256]{2,1,0:T(8,128)(2,1)S(1)} collective-permute-done((bf16[4,128,256]{2,1,0:T(8,128)(2,1)S(1)}, bf16[4,128,256]{2,1,0:T(8,128)(2,1)S(1)}, u32[]{:S(2)}, u32[]{:S(2)}) %collective-permute-start.6) | collective-permute-done | bytes 262176 | tf_op jit(solution)/shard_map/ppermute | solution.py:341
  26.2 1.6 %collective-permute-done.7.refs_5_ = bf16[4,128,256]{2,1,0:T(8,128)(2,1)S(1)} collective-permute-done((bf16[4,128,256]{2,1,0:T(8,128)(2,1)S(1)}, bf16[4,128,256]{2,1,0:T(8,128)(2,1)S(1)}, u32[]{:S(2)}, u32[]{:S(2)}) %collective-permute-start.7) | collective-permute-done | bytes 262176 | tf_op jit(solution)/shard_map/ppermute | solution.py:341
  27.9 9.2 %attention_backward.2 = (s32[2,8]{1,0:T(2,128)S(1)}, f32[2,8]{1,0:T(2,128)S(1)}, bf16[256,4096]{1,0:T(8,128)(2,1)S(1)}, bf16[256,4096]{1,0:T(8,128)(2,1)S(1)}, b...) custom-call(f32[1]{0:T(128)S(6)} %tanh.3.refs_0_.gate_ref, ...), custom_call_target="tpu_custom_call" | custom-call | flops 2147483648 | bytes 2097152 | tf_op jit(solution)/shard_map/attention_backward/pallas_call | solution.py:250
  37.1 0.9 %collective-permute-start.11 = (bf16[528,256]{1,0:T(8,128)(2,1)S(1)}, bf16[528,256]{1,0:T(8,128)(2,1)S(1)}, u32[]{:S(2)}, u32[]{:S(2)}) collective-permute-start(bf16[528,256]{1,0:T(8,128)(2,1)S(1)} %get-tuple-element.43), channel_id=1, source_target_pairs={{0,2},{2,0},{4,6},{6,4},{8,10},{10,8},{12,14},{14,12},{16,18},{18,... | collective-permute-start | bytes 811016 | tf_op jit(solution)/shard_map/ppermute | solution.py:341
  37.9 1.5 %collective-permute-start.12 = (bf16[528,256]{1,0:T(8,128)(2,1)S(1)}, bf16[528,256]{1,0:T(8,128)(2,1)S(1)}, u32[]{:S(2)}, u32[]{:S(2)}) collective-permute-start(bf16[528,256]{1,0:T(8,128)(2,1)S(1)} %get-tuple-element.44), channel_id=1, source_target_pairs={{0,4},{2,6},{4,0},{6,2},{8,12},{10,14},{12,8},{14,10},{16,20},{18,... | collective-permute-start | bytes 811016 | tf_op jit(solution)/shard_map/ppermute | solution.py:341
  39.5 1.2 %collective-permute-start.13 = (bf16[528,256]{1,0:T(8,128)(2,1)S(1)}, bf16[528,256]{1,0:T(8,128)(2,1)S(1)}, u32[]{:S(2)}, u32[]{:S(2)}) collective-permute-start(bf16[528,256]{1,0:T(8,128)(2,1)S(1)} %get-tuple-element.45), channel_id=1, source_target_pairs={{0,6},{2,4},{4,2},{6,0},{8,14},{10,12},{12,10},{14,8},{16,22},{18,... | collective-permute-start | bytes 811016 | tf_op jit(solution)/shard_map/ppermute | solution.py:341
  40.6 1.7 %query_gradient.2.rest_0_ = bf16[256,4096]{1,0:T(8,128)(2,1)} custom-call(f32[1]{0:T(128)S(6)} %tanh.3.refs_0_.gate_ref, bf16[2,16,512,128]{3,2,1,0:T(8,128)(2,1)S(1)} %get-tuple-element.51.ds_ref, bf16[2,128,512]{2,1,0:T(8,128)(2,1)S(1)} %get-tuple-element.52.kt_ref), custom_call_target="tpu_custom_call" | custom-call | flops 536870912 | bytes 4194304 | tf_op jit(solution)/shard_map/query_gradient/pallas_call | solution.py:310
  42.4 0.2 collective-permute-done.9.refs_4_
  42.6 8.1 %attention_backward.3 = (bf16[2,16,512,128]{3,2,1,0:T(8,128)(2,1)S(1)}, bf16[2,128,512]{2,1,0:T(8,128)(2,1)S(1)}, f32[4,128,256]{2,1,0:T(8,128)S(1)}, bf16[528,2...) custom-call(f32[1]{0:T(128)S(6)} %tanh.3.refs_0_.gate_ref, ...), custom_call_target="tpu_custom_call" | custom-call | flops 2147483648 | bytes 2097152 | tf_op jit(solution)/shard_map/attention_backward/pallas_call | solution.py:250
  50.7 1.1 %collective-permute-start.14 = (bf16[528,256]{1,0:T(8,128)(2,1)S(1)}, bf16[528,256]{1,0:T(8,128)(2,1)S(1)}, u32[]{:S(2)}, u32[]{:S(2)}) collective-permute-start(bf16[528,256]{1,0:T(8,128)(2,1)S(1)} %get-tuple-element.46), channel_id=1, source_target_pairs={{0,2},{2,0},{4,6},{6,4},{8,10},{10,8},{12,14},{14,12},{16,18},{18,... | collective-permute-start | bytes 811016 | tf_op jit(solution)/shard_map/ppermute | solution.py:341
  51.9 1.1 %collective-permute-start.15 = (bf16[528,256]{1,0:T(8,128)(2,1)S(1)}, bf16[528,256]{1,0:T(8,128)(2,1)S(1)}, u32[]{:S(2)}, u32[]{:S(2)}) collective-permute-start(bf16[528,256]{1,0:T(8,128)(2,1)S(1)} %get-tuple-element.47), channel_id=1, source_target_pairs={{0,4},{2,6},{4,0},{6,2},{8,12},{10,14},{12,8},{14,10},{16,20},{18,... | collective-permute-start | bytes 811016 | tf_op jit(solution)/shard_map/ppermute | solution.py:341
  53.0 1.3 %collective-permute-start.16 = (bf16[528,256]{1,0:T(8,128)(2,1)S(1)}, bf16[528,256]{1,0:T(8,128)(2,1)S(1)}, u32[]{:S(2)}, u32[]{:S(2)}) collective-permute-start(bf16[528,256]{1,0:T(8,128)(2,1)S(1)} %get-tuple-element.48), channel_id=1, source_target_pairs={{0,6},{2,4},{4,2},{6,0},{8,14},{10,12},{12,10},{14,8},{16,22},{18,... | collective-permute-start | bytes 811016 | tf_op jit(solution)/shard_map/ppermute | solution.py:341
  54.4 0.1 fusion.22
  54.5 2.7 %collective-permute-start.17 = (bf16[128,256]{1,0:T(8,128)(2,1)S(1)}, bf16[128,256]{1,0:T(8,128)(2,1)S(1)}, u32[]{:S(2)}, u32[]{:S(2)}) collective-permute-start(bf16[128,256]{1,0:T(8,128)(2,1)S(1)} %get-tuple-element.71), channel_id=1, source_target_pairs={{0,24},{2,26},{4,28},{6,30},{8,0},{10,2},{12,4},{14,6},{16,8},{18,... | collective-permute-start | bytes 196616 | tf_op jit(solution)/shard_map/ppermute | solution.py:345
  57.2 1.4 %collective-permute-done.14.rest_1_ = bf16[528,256]{1,0:T(8,128)(2,1)S(1)} collective-permute-done((bf16[528,256]{1,0:T(8,128)(2,1)S(1)}, bf16[528,256]{1,0:T(8,128)(2,1)S(1)}, u32[]{:S(2)}, u32[]{:S(2)}) %collective-permute-start.14) | collective-permute-done | bytes 270368 | tf_op jit(solution)/shard_map/ppermute | solution.py:341
  58.6 1.8 %collective-permute-start.19 = (bf16[128,256]{1,0:T(8,128)(2,1)S(1)}, bf16[128,256]{1,0:T(8,128)(2,1)S(1)}, u32[]{:S(2)}, u32[]{:S(2)}) collective-permute-start(bf16[128,256]{1,0:T(8,128)(2,1)S(1)} %get-tuple-element.72), channel_id=1, source_target_pairs={{0,8},{2,10},{4,12},{6,14},{8,16},{10,18},{12,20},{14,22},{16,24},... | collective-permute-start | bytes 196616 | tf_op jit(solution)/shard_map/ppermute | solution.py:345
  60.4 1.7 %query_gradient.3 = bf16[256,4096]{1,0:T(8,128)(2,1)} custom-call(f32[1]{0:T(128)S(6)} %tanh.3.refs_0_.gate_ref, bf16[2,16,512,128]{3,2,1,0:T(8,128)(2,1)S(1)} %get-tuple-element.49.ds_ref, bf16[2,128,512]{2,1,0:T(8,128)(2,1)S(1)} %get-tuple-element.50.kt_ref, bf16[256,4096]{1,0:T(8,128)(2,1)} %query_gradient.2.rest_0_, ...), custom_call_target="tpu_custom_call", output_to_operand_aliasing={{}: (3, {})} | custom-call | flops 536870912 | bytes 4194304 | tf_op jit(solution)/shard_map/query_gradient/pallas_call | solution.py:310
  62.1 0.3 collective-permute-done.16
  62.5 0.1 fusion.20
  62.7 0.1 select_convert_fusion
  62.8 2.4 %collective-permute-start.22 = (bf16[144,256]{1,0:T(8,128)(2,1)S(1)}, bf16[144,256]{1,0:T(8,128)(2,1)S(1)}, u32[]{:S(2)}, u32[]{:S(2)}) collective-permute-start(bf16[144,256]{1,0:T(8,128)(2,1)S(1)} %get-tuple-element.86), channel_id=1, source_target_pairs={{0,8},{2,10},{4,12},{6,14},{8,16},{10,18},{12,20},{14,22},{16,24},... | collective-permute-start | bytes 221192 | tf_op jit(solution)/shard_map/ppermute | solution.py:345
  65.2 3.0 %collective-permute-start.21 = (bf16[144,256]{1,0:T(8,128)(2,1)S(1)}, bf16[144,256]{1,0:T(8,128)(2,1)S(1)}, u32[]{:S(2)}, u32[]{:S(2)}) collective-permute-start(bf16[144,256]{1,0:T(8,128)(2,1)S(1)} %get-tuple-element.85), channel_id=1, source_target_pairs={{0,16},{2,18},{4,20},{6,22},{8,24},{10,26},{12,28},{14,30},{16,0},... | collective-permute-start | bytes 221192 | tf_op jit(solution)/shard_map/ppermute | solution.py:345
  68.3 0.4 collective-permute-start.20
  68.7 1.3 %collective-permute-done.22 = bf16[144,256]{1,0:T(8,128)(2,1)S(1)} collective-permute-done((bf16[144,256]{1,0:T(8,128)(2,1)S(1)}, bf16[144,256]{1,0:T(8,128)(2,1)S(1)}, u32[]{:S(2)}, u32[]{:S(2)}) %collective-permute-start.22) | collective-permute-done | bytes 73760 | tf_op jit(solution)/shard_map/ppermute | solution.py:345
  69.9 1.6 %collective-permute-done.21 = bf16[144,256]{1,0:T(8,128)(2,1)S(1)} collective-permute-done((bf16[144,256]{1,0:T(8,128)(2,1)S(1)}, bf16[144,256]{1,0:T(8,128)(2,1)S(1)}, u32[]{:S(2)}, u32[]{:S(2)}) %collective-permute-start.21) | collective-permute-done | bytes 73760 | tf_op jit(solution)/shard_map/ppermute | solution.py:345
  71.5 1.1 %collective-permute-done.20 = bf16[144,256]{1,0:T(8,128)(2,1)S(1)} collective-permute-done((bf16[144,256]{1,0:T(8,128)(2,1)S(1)}, bf16[144,256]{1,0:T(8,128)(2,1)S(1)}, u32[]{:S(2)}, u32[]{:S(2)}) %collective-permute-start.20) | collective-permute-done | bytes 73760 | tf_op jit(solution)/shard_map/ppermute | solution.py:345
  72.7 0.1 collective-permute-start.23
  72.8 0.7 fusion.10
  73.4 0.4 collective-permute-done.23
  73.9 0.5 fusion.17
  (41 shorter events, 0.4 us)
Async XLA Ops:
  1.5 8.6 %collective-permute-start.3 = (bf16[128,256]{1,0:T(8,128)(2,1)S(1)}, bf16[128,256]{1,0:T(8,128)(2,1)S(1)}, u32[]{:S(2)}, u32[]{:S(2)}) collective-permute-start(bf16[128,256]{1,0:T(8,128)(2,1)S(1)} %get-tuple-element.77), channel_id=1, source_target_pairs={{0,2},{2,0},{4,6},{6,4},{8,10},{10,8},{12,14},{14,12},{16,18},{18,... | collective-permute-start | bytes 196616 | tf_op jit(solution)/shard_map/ppermute | solution.py:341
  4.5 7.2 %collective-permute-start = (bf16[128,256]{1,0:T(8,128)(2,1)S(1)}, bf16[128,256]{1,0:T(8,128)(2,1)S(1)}, u32[]{:S(2)}, u32[]{:S(2)}) collective-permute-start(bf16[128,256]{1,0:T(8,128)(2,1)S(1)} %get-tuple-element.83), channel_id=1, source_target_pairs={{0,8},{2,10},{4,12},{6,14},{8,16},{10,18},{12,20},{14,22},{16,24},... | collective-permute-start | bytes 196616 | tf_op jit(solution)/shard_map/ppermute | solution.py:345
  6.1 7.3 %collective-permute-start.1 = (bf16[128,256]{1,0:T(8,128)(2,1)S(1)}, bf16[128,256]{1,0:T(8,128)(2,1)S(1)}, u32[]{:S(2)}, u32[]{:S(2)}) collective-permute-start(bf16[128,256]{1,0:T(8,128)(2,1)S(1)} %get-tuple-element.83), channel_id=1, source_target_pairs={{0,16},{2,18},{4,20},{6,22},{8,24},{10,26},{12,28},{14,30},{16,0},... | collective-permute-start | bytes 196616 | tf_op jit(solution)/shard_map/ppermute | solution.py:345
  8.7 4.8 %collective-permute-start.2 = (bf16[128,256]{1,0:T(8,128)(2,1)S(1)}, bf16[128,256]{1,0:T(8,128)(2,1)S(1)}, u32[]{:S(2)}, u32[]{:S(2)}) collective-permute-start(bf16[128,256]{1,0:T(8,128)(2,1)S(1)} %get-tuple-element.83), channel_id=1, source_target_pairs={{0,24},{2,26},{4,28},{6,30},{8,0},{10,2},{12,4},{14,6},{16,8},{18,... | collective-permute-start | bytes 196616 | tf_op jit(solution)/shard_map/ppermute | solution.py:345
  10.1 5.0 %collective-permute-start.4 = (bf16[2,128,256]{2,1,0:T(8,128)(2,1)S(1)}, bf16[2,128,256]{2,1,0:T(8,128)(2,1)S(1)}, u32[]{:S(2)}, u32[]{:S(2)}) collective-permute-start(bf16[2,128,256]{2,1,0:T(8,128)(2,1)S(1)} %pad_maximum_fusion.2), channel_id=1, source_target_pairs={{0,4},{2,6},{4,0},{6,2},{8,12},{10,14},{12,8},{14,10},{16,20},{18,... | collective-permute-start | bytes 393224 | tf_op jit(solution)/shard_map/ppermute | solution.py:341
  15.1 8.9 %collective-permute-start.5 = (bf16[4,128,256]{2,1,0:T(8,128)(2,1)S(1)}, bf16[4,128,256]{2,1,0:T(8,128)(2,1)S(1)}, u32[]{:S(2)}, u32[]{:S(2)}) collective-permute-start(bf16[4,128,256]{2,1,0:T(8,128)(2,1)S(1)} %pad_maximum_fusion.refs_2_), channel_id=1, source_target_pairs={{0,2},{2,0},{4,6},{6,4},{8,10},{10,8},{12,14},{14,12},{16,18},{18,... | collective-permute-start | bytes 786440 | tf_op jit(solution)/shard_map/ppermute | solution.py:341
  15.7 10.5 %collective-permute-start.6 = (bf16[4,128,256]{2,1,0:T(8,128)(2,1)S(1)}, bf16[4,128,256]{2,1,0:T(8,128)(2,1)S(1)}, u32[]{:S(2)}, u32[]{:S(2)}) collective-permute-start(bf16[4,128,256]{2,1,0:T(8,128)(2,1)S(1)} %pad_maximum_fusion.refs_2_), channel_id=1, source_target_pairs={{0,4},{2,6},{4,0},{6,2},{8,12},{10,14},{12,8},{14,10},{16,20},{18,... | collective-permute-start | bytes 786440 | tf_op jit(solution)/shard_map/ppermute | solution.py:341
  17.3 10.6 %collective-permute-start.7 = (bf16[4,128,256]{2,1,0:T(8,128)(2,1)S(1)}, bf16[4,128,256]{2,1,0:T(8,128)(2,1)S(1)}, u32[]{:S(2)}, u32[]{:S(2)}) collective-permute-start(bf16[4,128,256]{2,1,0:T(8,128)(2,1)S(1)} %pad_maximum_fusion.refs_2_), channel_id=1, source_target_pairs={{0,6},{2,4},{4,2},{6,0},{8,14},{10,12},{12,10},{14,8},{16,22},{18,... | collective-permute-start | bytes 786440 | tf_op jit(solution)/shard_map/ppermute | solution.py:341
  20.2 19.3 %collective-permute-start.10 = (bf16[4,128,256]{2,1,0:T(8,128)(2,1)S(1)}, bf16[4,128,256]{2,1,0:T(8,128)(2,1)S(1)}, u32[]{:S(2)}, u32[]{:S(2)}) collective-permute-start(bf16[4,128,256]{2,1,0:T(8,128)(2,1)S(1)} %pad_maximum_fusion.1.refs_2_), channel_id=1, source_target_pairs={{0,24},{2,26},{4,28},{6,30},{8,0},{10,2},{12,4},{14,6},{16,8},{18,... | collective-permute-start | bytes 786440 | tf_op jit(solution)/shard_map/ppermute | solution.py:345
  22.0 20.4 %collective-permute-start.8 = (bf16[4,128,256]{2,1,0:T(8,128)(2,1)S(1)}, bf16[4,128,256]{2,1,0:T(8,128)(2,1)S(1)}, u32[]{:S(2)}, u32[]{:S(2)}) collective-permute-start(bf16[4,128,256]{2,1,0:T(8,128)(2,1)S(1)} %pad_maximum_fusion.1.refs_2_), channel_id=1, source_target_pairs={{0,8},{2,10},{4,12},{6,14},{8,16},{10,18},{12,20},{14,22},{16,24},... | collective-permute-start | bytes 786440 | tf_op jit(solution)/shard_map/ppermute | solution.py:345
  24.1 18.5 %collective-permute-start.9 = (bf16[4,128,256]{2,1,0:T(8,128)(2,1)S(1)}, bf16[4,128,256]{2,1,0:T(8,128)(2,1)S(1)}, u32[]{:S(2)}, u32[]{:S(2)}) collective-permute-start(bf16[4,128,256]{2,1,0:T(8,128)(2,1)S(1)} %pad_maximum_fusion.1.refs_2_), channel_id=1, source_target_pairs={{0,16},{2,18},{4,20},{6,22},{8,24},{10,26},{12,28},{14,30},{16,0},... | collective-permute-start | bytes 786440 | tf_op jit(solution)/shard_map/ppermute | solution.py:345
  37.1 13.6 %collective-permute-start.11 = (bf16[528,256]{1,0:T(8,128)(2,1)S(1)}, bf16[528,256]{1,0:T(8,128)(2,1)S(1)}, u32[]{:S(2)}, u32[]{:S(2)}) collective-permute-start(bf16[528,256]{1,0:T(8,128)(2,1)S(1)} %get-tuple-element.43), channel_id=1, source_target_pairs={{0,2},{2,0},{4,6},{6,4},{8,10},{10,8},{12,14},{14,12},{16,18},{18,... | collective-permute-start | bytes 811016 | tf_op jit(solution)/shard_map/ppermute | solution.py:341
  37.9 12.8 %collective-permute-start.12 = (bf16[528,256]{1,0:T(8,128)(2,1)S(1)}, bf16[528,256]{1,0:T(8,128)(2,1)S(1)}, u32[]{:S(2)}, u32[]{:S(2)}) collective-permute-start(bf16[528,256]{1,0:T(8,128)(2,1)S(1)} %get-tuple-element.44), channel_id=1, source_target_pairs={{0,4},{2,6},{4,0},{6,2},{8,12},{10,14},{12,8},{14,10},{16,20},{18,... | collective-permute-start | bytes 811016 | tf_op jit(solution)/shard_map/ppermute | solution.py:341
  39.5 11.3 %collective-permute-start.13 = (bf16[528,256]{1,0:T(8,128)(2,1)S(1)}, bf16[528,256]{1,0:T(8,128)(2,1)S(1)}, u32[]{:S(2)}, u32[]{:S(2)}) collective-permute-start(bf16[528,256]{1,0:T(8,128)(2,1)S(1)} %get-tuple-element.45), channel_id=1, source_target_pairs={{0,6},{2,4},{4,2},{6,0},{8,14},{10,12},{12,10},{14,8},{16,22},{18,... | collective-permute-start | bytes 811016 | tf_op jit(solution)/shard_map/ppermute | solution.py:341
  50.7 7.9 %collective-permute-start.14 = (bf16[528,256]{1,0:T(8,128)(2,1)S(1)}, bf16[528,256]{1,0:T(8,128)(2,1)S(1)}, u32[]{:S(2)}, u32[]{:S(2)}) collective-permute-start(bf16[528,256]{1,0:T(8,128)(2,1)S(1)} %get-tuple-element.46), channel_id=1, source_target_pairs={{0,2},{2,0},{4,6},{6,4},{8,10},{10,8},{12,14},{14,12},{16,18},{18,... | collective-permute-start | bytes 811016 | tf_op jit(solution)/shard_map/ppermute | solution.py:341
  51.9 10.3 %collective-permute-start.15 = (bf16[528,256]{1,0:T(8,128)(2,1)S(1)}, bf16[528,256]{1,0:T(8,128)(2,1)S(1)}, u32[]{:S(2)}, u32[]{:S(2)}) collective-permute-start(bf16[528,256]{1,0:T(8,128)(2,1)S(1)} %get-tuple-element.47), channel_id=1, source_target_pairs={{0,4},{2,6},{4,0},{6,2},{8,12},{10,14},{12,8},{14,10},{16,20},{18,... | collective-permute-start | bytes 811016 | tf_op jit(solution)/shard_map/ppermute | solution.py:341
  53.0 9.5 %collective-permute-start.16 = (bf16[528,256]{1,0:T(8,128)(2,1)S(1)}, bf16[528,256]{1,0:T(8,128)(2,1)S(1)}, u32[]{:S(2)}, u32[]{:S(2)}) collective-permute-start(bf16[528,256]{1,0:T(8,128)(2,1)S(1)} %get-tuple-element.48), channel_id=1, source_target_pairs={{0,6},{2,4},{4,2},{6,0},{8,14},{10,12},{12,10},{14,8},{16,22},{18,... | collective-permute-start | bytes 811016 | tf_op jit(solution)/shard_map/ppermute | solution.py:341
  54.5 10.7 %collective-permute-start.17 = (bf16[128,256]{1,0:T(8,128)(2,1)S(1)}, bf16[128,256]{1,0:T(8,128)(2,1)S(1)}, u32[]{:S(2)}, u32[]{:S(2)}) collective-permute-start(bf16[128,256]{1,0:T(8,128)(2,1)S(1)} %get-tuple-element.71), channel_id=1, source_target_pairs={{0,24},{2,26},{4,28},{6,30},{8,0},{10,2},{12,4},{14,6},{16,8},{18,... | collective-permute-start | bytes 196616 | tf_op jit(solution)/shard_map/ppermute | solution.py:345
  57.2 8.0 %collective-permute-start.18 = (bf16[128,256]{1,0:T(8,128)(2,1)S(1)}, bf16[128,256]{1,0:T(8,128)(2,1)S(1)}, u32[]{:S(2)}, u32[]{:S(2)}) collective-permute-start(bf16[128,256]{1,0:T(8,128)(2,1)S(1)} %get-tuple-element.73), channel_id=1, source_target_pairs={{0,16},{2,18},{4,20},{6,22},{8,24},{10,26},{12,28},{14,30},{16,0},... | collective-permute-start | bytes 196616 | tf_op jit(solution)/shard_map/ppermute | solution.py:345
  58.6 6.6 %collective-permute-start.19 = (bf16[128,256]{1,0:T(8,128)(2,1)S(1)}, bf16[128,256]{1,0:T(8,128)(2,1)S(1)}, u32[]{:S(2)}, u32[]{:S(2)}) collective-permute-start(bf16[128,256]{1,0:T(8,128)(2,1)S(1)} %get-tuple-element.72), channel_id=1, source_target_pairs={{0,8},{2,10},{4,12},{6,14},{8,16},{10,18},{12,20},{14,22},{16,24},... | collective-permute-start | bytes 196616 | tf_op jit(solution)/shard_map/ppermute | solution.py:345
  62.8 7.1 %collective-permute-start.22 = (bf16[144,256]{1,0:T(8,128)(2,1)S(1)}, bf16[144,256]{1,0:T(8,128)(2,1)S(1)}, u32[]{:S(2)}, u32[]{:S(2)}) collective-permute-start(bf16[144,256]{1,0:T(8,128)(2,1)S(1)} %get-tuple-element.86), channel_id=1, source_target_pairs={{0,8},{2,10},{4,12},{6,14},{8,16},{10,18},{12,20},{14,22},{16,24},... | collective-permute-start | bytes 221192 | tf_op jit(solution)/shard_map/ppermute | solution.py:345
  65.2 6.3 %collective-permute-start.21 = (bf16[144,256]{1,0:T(8,128)(2,1)S(1)}, bf16[144,256]{1,0:T(8,128)(2,1)S(1)}, u32[]{:S(2)}, u32[]{:S(2)}) collective-permute-start(bf16[144,256]{1,0:T(8,128)(2,1)S(1)} %get-tuple-element.85), channel_id=1, source_target_pairs={{0,16},{2,18},{4,20},{6,22},{8,24},{10,26},{12,28},{14,30},{16,0},... | collective-permute-start | bytes 221192 | tf_op jit(solution)/shard_map/ppermute | solution.py:345
  68.3 4.4 %collective-permute-start.20 = (bf16[144,256]{1,0:T(8,128)(2,1)S(1)}, bf16[144,256]{1,0:T(8,128)(2,1)S(1)}, u32[]{:S(2)}, u32[]{:S(2)}) collective-permute-start(bf16[144,256]{1,0:T(8,128)(2,1)S(1)} %get-tuple-element.84), channel_id=1, source_target_pairs={{0,24},{2,26},{4,28},{6,30},{8,0},{10,2},{12,4},{14,6},{16,8},{18,... | collective-permute-start | bytes 221192 | tf_op jit(solution)/shard_map/ppermute | solution.py:345
  72.7 1.2 %collective-permute-start.23 = (f32[1,256]{1,0:T(1,128)S(1)}, f32[1,256]{1,0:T(1,128)S(1)}, u32[]{:S(2)}, u32[]{:S(2)}) collective-permute-start(f32[1,256]{1,0:T(1,128)S(1)} %fusion.11), channel_id=1, source_target_pairs={{0,1},{1,0},{2,3},{3,2},{4,5},{5,4},{6,7},{7,6},{8,9},{9,8},{10,11... | collective-permute-start | bytes 3080 | tf_op jit(solution)/shard_map/ppermute | solution.py:420

commit v5 on v4

v5 whole, which is shorter than its diff:
```python
import functools
import math

import jax
import jax.numpy as jnp
from jax import lax
from jax.experimental import pallas as pl
from jax.experimental.pallas import tpu as pltpu
from jax.sharding import PartitionSpec as P

HD = 128
BLK = 128
JOIN = 4
FIRST = 0
MERGE = 2
CHUNKS = 2
CODE = 16
NT = (((1,), (1,)), ((), ()))
F32, BF16 = jnp.float32, jnp.bfloat16


def coded(value, rows, rounded):
    high = rounded(value)
    middle = rounded(value - high)
    low = value - high - middle
    shape = (rows, value.shape[1])
    row = lax.broadcasted_iota(jnp.int32, shape, 0)
    parts = jnp.where(row == 0, high, jnp.zeros(shape, F32))
    return jnp.where(row == 1, middle, jnp.where(row == 2, low, parts)).astype(BF16)


def rounded_here(value):
    return value.astype(BF16).astype(F32)


def rounded_outside(value):
    return lax.reduce_precision(value, 8, 7)


def decoded(rows):
    rows = rows.astype(F32)
    return rows[0:1] + rows[1:2] + rows[2:3]


def plan_images(n, n_blocks, n_images, part_rows, plan_ref, place, bias):
    read_most = n_images // 2
    me = plan_ref[(n_blocks + 1) * n_images]
    for j in range(read_most):
        place[0, j] = 0
        place[1, j] = 0
        place[2, j] = 0
        for b in range(n_blocks):
            bias[b, j] = jnp.float32(-1e30)

    def look(i, count):
        reads = [plan_ref[b * n_images + i] > 0 for b in range(n_blocks)]
        any_read = functools.reduce(jnp.logical_or, reads)

        @pl.when(jnp.logical_and(any_read, count < read_most))
        def _():
            slot = plan_ref[n_blocks * n_images + i]
            column = jnp.bitwise_xor(lax.rem(slot, 4), lax.rem(me, 4))
            across = jnp.bitwise_xor(lax.div(slot, 4), lax.div(me, 4))
            place[0, count] = column * n + across
            place[1, count] = across * 4 + column
            place[2, count] = (column * n + across) * part_rows
            for b in range(n_blocks):
                bias[b, count] = jnp.where(reads[b], 0.0, -1e30).astype(F32)

        return count + any_read.astype(jnp.int32)

    lax.fori_loop(0, n_images, look, jnp.int32(0))


def prepare_kernel(n, n_blocks, n_images, part_rows, *refs):
    plan_ref, q_hbm, cot_hbm, _, place, bias, q_ref, cot_ref, sem = refs
    half = q_ref.shape[0] // 2
    copies = []
    for u, (src, dst) in enumerate(((q_hbm, q_ref), (cot_hbm, cot_ref))):
        for k in range(2):
            rows = slice(k * half, (k + 1) * half)
            copies.append(pltpu.make_async_copy(src.at[rows], dst.at[rows], sem.at[u, k]))
            copies[-1].start()
    plan_images(n, n_blocks, n_images, part_rows, plan_ref, place, bias)
    for copy in copies:
        copy.wait()


def prepare(sizes, img_tok, plan, queries, cotangent, after):
    n, n_blocks, n_images = sizes[:3]
    smem = pl.BlockSpec(memory_space=pltpu.SMEM)
    vmem = pl.BlockSpec(memory_space=pltpu.VMEM)
    hbm = pl.BlockSpec(memory_space=pltpu.HBM)
    wide = [pltpu.with_memory_space_constraint(x, pltpu.HBM) for x in (queries, cotangent)]
    return pl.pallas_call(
        functools.partial(prepare_kernel, n, n_blocks, n_images, 2 * img_tok),
        in_specs=[smem, hbm, hbm, pl.BlockSpec(memory_space=pl.ANY)],
        out_specs=[smem, smem, vmem, vmem],
        out_shape=[
            jax.ShapeDtypeStruct((3, n_images // 2), jnp.int32),
            jax.ShapeDtypeStruct((n_blocks, n_images // 2), F32),
            pltpu.VMEM(queries.shape, BF16),
            pltpu.VMEM(queries.shape, BF16),
        ],
        scratch_shapes=[pltpu.SemaphoreType.DMA((2, 2))],
        compiler_params=pltpu.CompilerParams(vmem_limit_bytes=4 * 1024 * 1024),
        cost_estimate=pl.CostEstimate(
            flops=0, bytes_accessed=8 * queries.size, transcendentals=0
        ),
        name="prepare",
    )(plan, *wide, after)


def attention_kernel(n, n_blocks, n_images, lead, first, heads, total_kv, n_columns, *refs):
    gate_ref, gate_in = refs[:2]
    columns = refs[2 : 2 + n_columns]
    refs = refs[2 + n_columns :]
    place, bias, q_ref, cot_ref = refs[:4]
    ds_ref, k_sel = refs[4:6]
    out_refs = refs[6:10]
    gate_out, out_ref, k_all, v_all, v_sel, dk_acc, dv_acc = refs[10:]
    read_most = n_images // 2
    img_tok = k_all.shape[2]
    per_head = ds_ref.shape[1]
    groups = per_head // n_blocks
    width = groups * HD
    gate_value = gate_ref[0]
    inv_root = 1.0 / math.sqrt(HD)
    to_exp2 = math.log2(math.e) * inv_root

    for h in range(heads):
        lanes = slice(h * HD, (h + 1) * HD)
        at = 0
        for column in columns:
            count = column.shape[0]
            k_all[h, at : at + count] = column[:, :img_tok, lanes]
            v_all[h, at : at + count] = column[:, img_tok:, lanes]
            at += count
        for j in range(read_most):
            rows = slice(j * img_tok, (j + 1) * img_tok)
            where = place[0 if lead else 1, j]
            k_sel[h, rows] = k_all[h, where]
            v_sel[h, rows] = v_all[h, where]
    out_ref[...] = jnp.zeros_like(out_ref)
    dk_acc[...] = jnp.zeros_like(dk_acc)
    dv_acc[...] = jnp.zeros_like(dv_acc)

    def tile_of(ref, i):
        h, b, g = i // per_head, i % per_head // groups, i % groups
        lane = ((first + h) * groups + g) * HD
        return ref[b * BLK : (b + 1) * BLK, lane : lane + HD]

    def score_product(i):
        h = i // per_head
        return lax.dot_general(k_sel[h], tile_of(q_ref, i), NT, preferred_element_type=F32)

    def value_product(i):
        h = i // per_head
        return lax.dot_general(v_sel[h], tile_of(cot_ref, i), NT, preferred_element_type=F32)

    def probabilities(i, scores):
        b = i % per_head // groups
        images = [scores[j * img_tok : (j + 1) * img_tok] for j in range(read_most)]
        tops = [
            jnp.max(image.reshape(img_tok // 8, 8, BLK), axis=0) + bias[b, j]
            for j, image in enumerate(images)
        ]
        row_max = jnp.max(functools.reduce(jnp.maximum, tops), axis=0, keepdims=True)
        terms = [
            jnp.exp2((image - (row_max - bias[b, j])) * to_exp2) for j, image in enumerate(images)
        ]
        terms = jnp.concatenate(terms, axis=0)
        return terms * (1.0 / jnp.sum(terms, axis=0, keepdims=True))

    def score_gradient(i, prob, prob_grad):
        delta = jnp.sum(prob * prob_grad, axis=0, keepdims=True)
        score_grad = (prob * (prob_grad - delta)).astype(BF16)
        ds_ref[i // per_head, i % per_head] = score_grad
        return prob.astype(BF16), score_grad

    def gradients(pieces):
        h = pieces[0][0] // per_head
        query = jnp.concatenate([tile_of(q_ref, i) for i, _, _ in pieces], axis=0)
        cot = jnp.concatenate([tile_of(cot_ref, i) for i, _, _ in pieces], axis=0)
        prob_half = jnp.concatenate([p for _, p, _ in pieces], axis=1)
        score_grad = jnp.concatenate([d for _, _, d in pieces], axis=1)
        dk_acc[h] += jnp.dot(score_grad, query, preferred_element_type=F32)
        dv_acc[h] += jnp.dot(prob_half, cot, preferred_element_type=F32)

    def finish(h):
        lanes = slice(h * HD, (h + 1) * HD)
        for j in range(read_most):
            rows = slice(j * img_tok, (j + 1) * img_tok)
            at = place[2, j]
            for u, (acc, scale) in enumerate(((dk_acc, gate_value * inv_root), (dv_acc, gate_value))):
                out_rows = pl.ds(pl.multiple_of(at + u * img_tok, 16), img_tok)
                out_ref[out_rows, lanes] = (acc[h, rows] * scale).astype(BF16)
        return jnp.sum(dv_acc[h] * v_sel[h].astype(F32), axis=0, keepdims=True)

    items = heads * per_head
    gate_row = jnp.zeros((1, HD), F32)
    ready, waiting, held = None, None, []
    for at in range(items + 3):
        scores = score_product(at) if at < items else None
        values = value_product(at - 1) if 0 < at <= items else None
        prob = probabilities(at - 1, ready) if ready is not None else None
        middle = (at - 2, *score_gradient(at - 2, *waiting)) if waiting is not None else None
        if len(held) == MERGE:
            gradients(held)
            if (held[-1][0] + 1) % per_head == 0:
                gate_row += finish(held[-1][0] // per_head)
            held = []
        if middle is not None:
            held.append(middle)
        waiting = (prob, values) if prob is not None else None
        ready = scores

    gate_row = jnp.broadcast_to(jnp.sum(gate_row, axis=1, keepdims=True), (1, HD))
    gate_row += gate_in[0:1]
    gate_out[...] = jnp.broadcast_to(gate_row, gate_out.shape)
    code = coded(gate_row, CODE, rounded_here)
    rows = out_ref.shape[0] // 4
    for a, out in enumerate(out_refs):
        out[:rows] = out_ref[a * rows : (a + 1) * rows]
        for h in range(heads):
            out[rows:, h * HD : (h + 1) * HD] = code


def attention(at, sizes, gate_value, gate_in, columns, shared):
    n, n_blocks, n_images, heads, total_kv, tokens = sizes
    lead = at == 0
    read_most = n_images // 2
    img_tok = columns[0].shape[1] // 2
    queries = shared[2]
    groups = queries.shape[1] // HD // total_kv
    per_head = groups * n_blocks
    n_keys = read_most * img_tok
    smem = pl.BlockSpec(memory_space=pltpu.SMEM)
    vmem = pl.BlockSpec(memory_space=pltpu.VMEM)
    span = heads * HD
    args = [gate_value, gate_in, *columns]
    in_specs = [smem] + [vmem] * (1 + len(columns))
    args += shared
    in_specs += [smem, smem, vmem, vmem]
    out_shape = [
        pltpu.VMEM((heads, per_head, n_keys, BLK), BF16),
        pltpu.VMEM((heads, n_keys, HD), BF16),
        *[pltpu.VMEM((2 * n * img_tok + CODE, span), BF16)] * 4,
        pltpu.VMEM((8, HD), F32),
    ]
    rows = tokens * groups * heads
    kernel = functools.partial(
        attention_kernel, n, n_blocks, n_images, lead, at * heads, heads, total_kv, len(columns)
    )
    return pl.pallas_call(
        kernel,
        in_specs=in_specs,
        out_specs=[vmem] * len(out_shape),
        out_shape=out_shape,
        scratch_shapes=[
            pltpu.VMEM((4 * 2 * n * img_tok, span), BF16),
            pltpu.VMEM((heads, 4 * n, img_tok, HD), BF16),
            pltpu.VMEM((heads, 4 * n, img_tok, HD), BF16),
            pltpu.VMEM((heads, n_keys, HD), BF16),
            pltpu.VMEM((heads, n_keys, HD), F32),
            pltpu.VMEM((heads, n_keys, HD), F32),
        ],
        compiler_params=pltpu.CompilerParams(vmem_limit_bytes=vmem_bytes(n_keys)),
        cost_estimate=pl.CostEstimate(
            flops=8 * rows * n_keys * HD,
            bytes_accessed=4 * rows * HD,
            transcendentals=rows * n_keys,
        ),
        name="attention_backward",
    )(*args)


def vmem_bytes(n_keys):
    return min(44, 14 + 15 * n_keys // 1024) * 1024 * 1024


def query_kernel(first, n_blocks, n_extra, gate_ref, ds_ref, k_ref, *rest):
    dq_hbm, dq_ref, sem = rest[n_extra:]
    heads, per_head = ds_ref.shape[:2]
    groups = per_head // n_blocks
    width = groups * HD
    scale = gate_ref[0] * (1.0 / math.sqrt(HD))
    copies = []
    for h in range(heads):
        turned = k_ref[h].astype(F32).T.astype(BF16)
        for i in range(0, per_head, JOIN):
            b, g = i // groups, i % groups
            score_grad = jnp.concatenate([ds_ref[h, i + u] for u in range(JOIN)], axis=1)
            dq = jnp.dot(turned, score_grad, preferred_element_type=F32)
            dq = (dq.T * scale).astype(BF16)
            for u in range(JOIN):
                lanes = slice((g + u) * HD, (g + u + 1) * HD)
                dq_ref[h, b * BLK : (b + 1) * BLK, lanes] = dq[u * BLK : (u + 1) * BLK]
        span = pl.ds((first + h) * width, width)
        copies.append(pltpu.make_async_copy(dq_ref.at[h], dq_hbm.at[:, span], sem.at[h]))
        copies[-1].start()
    for copy in copies:
        copy.wait()


def query_gradient(at, sizes, shape, prev, after, gate_value, ds, kt):
    n, n_blocks, n_images, heads, total_kv, tokens = sizes
    hbm = pl.BlockSpec(memory_space=pltpu.HBM)
    vmem = pl.BlockSpec(memory_space=pltpu.VMEM)
    anywhere = pl.BlockSpec(memory_space=pl.ANY)
    extra = ([] if prev is None else [prev]) + after
    specs = ([] if prev is None else [hbm]) + [anywhere] * len(after)
    return pl.pallas_call(
        functools.partial(query_kernel, at * heads, n_blocks, len(extra)),
        in_specs=[pl.BlockSpec(memory_space=pltpu.SMEM), vmem, vmem] + specs,
        out_specs=hbm,
        out_shape=pltpu.HBM(shape, BF16),
        input_output_aliases={} if prev is None else {3: 0},
        scratch_shapes=[
            pltpu.VMEM((heads, shape[0], shape[1] // total_kv), BF16),
            pltpu.SemaphoreType.DMA((heads,)),
        ],
        compiler_params=pltpu.CompilerParams(vmem_limit_bytes=16 * 1024 * 1024),
        cost_estimate=pl.CostEstimate(
            flops=2 * ds.size * HD, bytes_accessed=2 * ds.size, transcendentals=0
        ),
        name="query_gradient",
    )(gate_value, ds, kt, *extra)


def per_device(queries, cotangent, image_keys, image_values, attn_gate, block_mask, image_owner):
    n_ctx = lax.axis_size("ctx")
    n_tp = lax.axis_size("tp")
    n = n_ctx // 4
    img_tok = image_keys.shape[1]
    local_kv = image_keys.shape[2] // HD
    chunks = min(CHUNKS, local_kv)
    heads = local_kv // chunks
    me = lax.axis_index("ctx").astype(jnp.int32).reshape(1)
    plan = jnp.concatenate([block_mask.reshape(-1), image_owner, me])
    gate_value = jnp.tanh(attn_gate)

    def swap(value, bit):
        return lax.ppermute(value, "ctx", [(i, i ^ bit) for i in range(n_ctx)])

    def swap_z(value, bit):
        pairs = [(i, (i // 4 ^ bit) * 4 + i % 4) for i in range(n_ctx)]
        return lax.ppermute(value, "ctx", pairs)

    def own_columns(c):
        lanes = slice(c * heads * HD, (c + 1) * heads * HD)
        return jnp.concatenate([image_keys[0, :, lanes], image_values[0, :, lanes]], axis=0)

    def square_of(own):
        pair = jnp.stack([own, swap(own, 1)])
        return jnp.concatenate([pair, swap(pair, 2)])

    def column_of(own):
        near_z.extend(swap_z(own, k) for k in range(1, n))
        return jnp.stack([own, *near_z])

    rest = 2 * n * img_tok

    def square_sum(own, came):
        total = own[:rest].astype(F32)
        gate = decoded(own[rest:])
        for part in came:
            total = total + part[:rest].astype(F32)
            gate = gate + decoded(part[rest:])
        return total.reshape(n, 2 * img_tok, own.shape[1]), gate

    def column_sum(both, gate, last):
        total, gate_total, turns = both[0], gate, []
        sends = both.astype(BF16)
        for k in range(1, n):
            send = sends[k]
            if last:
                send = jnp.concatenate([send, coded(gate, CODE, rounded_outside)])
            came = swap_z(send, k)
            turns.append(came)
            total = total + came[: 2 * img_tok].astype(F32)
            if last:
                gate_total = gate_total + decoded(came[2 * img_tok :])
        return total, gate_total, turns

    near_z = []
    owns = [own_columns(c) for c in range(chunks)]
    starts = [square_of(own) if c else column_of(own) for c, own in enumerate(owns)]
    sizes = (n, *block_mask.shape, heads, local_kv, queries.shape[0])
    shared = prepare(sizes, img_tok, plan, queries, cotangent, near_z[0])
    shared, starts = lax.optimization_barrier((tuple(shared), starts))
    column = starts[0]
    gathered = [[column, swap(column, 1), swap(column, 2), swap(column, 3)]]
    for square in starts[1:]:
        far = [swap_z(square, k) for k in range(2, n)]
        gathered[0][1], near = lax.optimization_barrier((gathered[0][1], square))
        gathered.append([square, swap_z(near, 1)] + far)
    gate_part = jnp.zeros((8, HD), F32)
    parts, dq = [], None
    saved, waiting = [], None
    for c in range(chunks):
        last = c == chunks - 1
        outs = attention(c, sizes, gate_value, gate_part, gathered[c], shared)
        ds, k_read, own, *backs, gate_part = outs
        if c:
            held = lax.optimization_barrier((tuple(backs), waiting[1]))
            backs = held[0]
            total, gate_row, turns = column_sum(*square_sum(waiting[0], held[1]), False)
            parts.append(total.astype(BF16))
        came = [swap(back, a + 1) for a, back in enumerate(backs)]
        waiting = (own, tuple(came))
        saved.append((ds, k_read))
    for c, (ds, k_read) in enumerate(saved):
        after = came[FIRST] if c == chunks - 1 else turns[0]
        dq = query_gradient(c, sizes, queries.shape, dq, [after], gate_value, ds, k_read)
    *came, dq = lax.optimization_barrier((*came, dq))
    total, gate_row, turns = column_sum(*square_sum(own, came), True)
    parts.append(total.astype(BF16))
    grads = jnp.concatenate(parts, axis=1)
    key_grad, value_grad = grads[None, :img_tok], grads[None, img_tok:]
    gate_total = gate_row
    for k in range(1, n_tp):
        pairs = [(i, (i + k) % n_tp) for i in range(n_tp)]
        gate_total = gate_total + lax.ppermute(gate_row, "tp", pairs)
    term_count = queries.shape[0] * n_ctx * queries.shape[1] * n_tp
    gate_row = gate_total[0, :HD] * (1.0 / math.sqrt(term_count))
    gate_grad = ((1.0 - gate_value * gate_value) * gate_row)[:1]
    return (dq, key_grad, value_grad, gate_grad)


def solution(mesh):
    in_specs = (
        P("ctx", "tp"),
        P("ctx", "tp"),
        P("ctx", None, "tp"),
        P("ctx", None, "tp"),
        P(),
        P("ctx", None),
        P(),
    )
    out_specs = (P("ctx", "tp"), P("ctx", None, "tp"), P("ctx", None, "tp"), P())
    return jax.shard_map(
        per_device, mesh=mesh, in_specs=in_specs, out_specs=out_specs, check_vma=False
    )
```

time: 74.6 us -> 74.2 us (level)
  Pallas kernels: 20.8 us -> 21.8 us
    ppermute x11, waiting for transfers between devices: 7.74 us -> 5.43 us  [swap(): return lax.ppermute(value, 'ctx', [(i, i ^ bit) for i in range(n_ctx)])]
    ppermute x12, waiting for transfers between devices: 5.94 us -> 7.64 us  [swap_z(): return lax.ppermute(value, 'ctx', pairs)]
    pallas_call x2 -> x3, Pallas kernels: 17.3 us -> 18.4 us  [the longest x2 15 us: attention(): pl.pallas_call(kernel, in_specs=in_specs, out_specs=[vmem] * len(out_shap...]
  transfers between devices with their start and end apart: 24 -> 24, of which waited for: 12 -> 8; matrix products, arithmetic and copies ran while one was open for 4% -> 4% of each run, Pallas kernels for 28% -> 29%
where the time goes in v5:
time: 74.2 us; the launch traced here: 74 us
  starting transfers between devices  33 us (44%)
  Pallas kernels  21.8 us (29%)
  waiting for transfers between devices  13.5 us (18%)
  other arithmetic  2.55 us (3%)
  local copies, waits for them, and re-layouts  1.61 us (2%)
  between operations  1.52 us (2%)
    ppermute x12, starting transfers between devices, swap_z(): return lax.ppermute(value, 'ctx', pairs)  17.7 us
    ppermute x11, starting transfers between devices, swap(): return lax.ppermute(value, 'ctx', [(i, i ^ bit) for i in range(n_ctx)])  15.2 us
    pallas_call x2, Pallas kernels, attention(): pl.pallas_call(kernel, in_specs=in_specs, out_specs=[vmem] * len(out_shap...  15 us
    ppermute x12, waiting for transfers between devices, swap_z(): return lax.ppermute(value, 'ctx', pairs)  7.64 us
    ppermute x11, waiting for transfers between devices, swap(): return lax.ppermute(value, 'ctx', [(i, i ^ bit) for i in range(n_ctx)])  5.43 us
    pallas_call x2, Pallas kernels, query_gradient(): pl.pallas_call(functools.partial(query_kernel, at * heads, n_blocks, len(...  3.43 us
    pallas_call x1, Pallas kernels, prepare(): pl.pallas_call(functools.partial(prepare_kernel, n, n_blocks, n_images, 2...  3.38 us
  transfers between devices with their start and end apart: 24, of which 8 were waited for; matrix products, arithmetic and copies ran while one was open for 4% of the time, Pallas kernels for 29%

profile of v5, /device:TPU:0, one launch (start us, length us, event | category | flops | bytes accessed | tf_op | source)
XLA Modules:
  0.0 74.0 jit_solution(8439411690804358821)
XLA Ops:
  0.6 0.8 %slice_bitcast_fusion = (bf16[64,256]{1,0:T(8,128)(2,1)S(1)}, bf16[64,256]{1,0:T(8,128)(2,1)S(1)}, bf16[64,256]{1,0:T(8,128)(2,1)S(1)}, bf16[64,256]{1,0:T(8,128)(2,1)S(1)}) fusion(bf16[1,64,512]{2,1,0:T(8,128)(2,1)} %param.10, bf16[1,64,512]{2,1,0:T(8,128)(2,1)} %param.9), kind=kLoop, calls=%fused_computation.24 | loop fusion | bytes 262144 | tf_op jit(solution)/shard_map/squeeze | solution.py:352
  1.5 3.0 %collective-permute-start.3 = (bf16[128,256]{1,0:T(8,128)(2,1)S(1)}, bf16[128,256]{1,0:T(8,128)(2,1)S(1)}, u32[]{:S(2)}, u32[]{:S(2)}) collective-permute-start(bf16[128,256]{1,0:T(8,128)(2,1)S(1)} %get-tuple-element.89), channel_id=1, source_target_pairs={{0,2},{2,0},{4,6},{6,4},{8,10},{10,8},{12,14},{14,12},{16,18},{18,... | collective-permute-start | bytes 196616 | tf_op jit(solution)/shard_map/ppermute | solution.py:344
  4.5 1.6 %collective-permute-start = (bf16[128,256]{1,0:T(8,128)(2,1)S(1)}, bf16[128,256]{1,0:T(8,128)(2,1)S(1)}, u32[]{:S(2)}, u32[]{:S(2)}) collective-permute-start(bf16[128,256]{1,0:T(8,128)(2,1)S(1)} %get-tuple-element.95), channel_id=1, source_target_pairs={{0,8},{2,10},{4,12},{6,14},{8,0},{10,2},{12,4},{14,6},{16,24},{18,... | collective-permute-start | bytes 196616 | tf_op jit(solution)/shard_map/ppermute | solution.py:348
  6.1 2.6 %collective-permute-start.1 = (bf16[128,256]{1,0:T(8,128)(2,1)S(1)}, bf16[128,256]{1,0:T(8,128)(2,1)S(1)}, u32[]{:S(2)}, u32[]{:S(2)}) collective-permute-start(bf16[128,256]{1,0:T(8,128)(2,1)S(1)} %get-tuple-element.95), channel_id=1, source_target_pairs={{0,16},{2,18},{4,20},{6,22},{8,24},{10,26},{12,28},{14,30},{16,0},... | collective-permute-start | bytes 196616 | tf_op jit(solution)/shard_map/ppermute | solution.py:348
  8.7 0.2 collective-permute-start.2
  8.9 0.8 %reshape.39 = s32[32]{0:T(128)S(1)} reshape(s32[2,16]{1,0:T(2,128)} %param.12) | data formatting | bytes 256 | tf_op jit(solution)/shard_map/reshape | solution.py:340
  9.7 0.0 collective-permute-done.3
  9.7 1.6 %collective-permute-start.4 = (bf16[2,128,256]{2,1,0:T(8,128)(2,1)S(1)}, bf16[2,128,256]{2,1,0:T(8,128)(2,1)S(1)}, u32[]{:S(2)}, u32[]{:S(2)}) collective-permute-start(bf16[2,128,256]{2,1,0:T(8,128)(2,1)S(1)} %pad_maximum_fusion.2), channel_id=1, source_target_pairs={{0,4},{2,6},{4,0},{6,2},{8,12},{10,14},{12,8},{14,10},{16,20},{18,... | collective-permute-start | bytes 393224 | tf_op jit(solution)/shard_map/ppermute | solution.py:344
  11.3 0.7 pad_add_fusion.refs_0_
  12.0 0.0 collective-permute-done.refs_3_
  12.0 3.4 %prepare.1 = (s32[3,8]{1,0:T(4,128)S(1)}, f32[2,8]{1,0:T(2,128)S(1)}, bf16[256,4096]{1,0:T(8,128)(2,1)S(1)}, bf16[256,4096]{1,0:T(8,128)(2,1)S(1)}) custom-call(s32[49]{0:T(128)S(1)} %pad_add_fusion.refs_0_, bf16[256,4096]{1,0:T(8,128)(2,1)} %refs_1_.1, bf16[256,4096]{1,0:T(8,128)(2,1)} %refs_2_.1, bf16[128,256]{1,0:T(8,128)(2,1)S(1)} %collective-permute-done.refs_3_), custom_call_target="tpu_custom_call" | custom-call | bytes 8388608 | tf_op jit(solution)/shard_map/prepare/pallas_call | solution.py:95
  15.4 0.0 collective-permute-done.1
  15.4 0.0 collective-permute-done.2
  15.5 0.6 collective-permute-start.5
  16.1 0.8 %collective-permute-start.6 = (bf16[4,128,256]{2,1,0:T(8,128)(2,1)S(1)}, bf16[4,128,256]{2,1,0:T(8,128)(2,1)S(1)}, u32[]{:S(2)}, u32[]{:S(2)}) collective-permute-start(bf16[4,128,256]{2,1,0:T(8,128)(2,1)S(1)} %pad_maximum_fusion.refs_2_), channel_id=1, source_target_pairs={{0,4},{2,6},{4,0},{6,2},{8,12},{10,14},{12,8},{14,10},{16,20},{18,... | collective-permute-start | bytes 786440 | tf_op jit(solution)/shard_map/ppermute | solution.py:344
  17.0 2.1 %collective-permute-start.7 = (bf16[4,128,256]{2,1,0:T(8,128)(2,1)S(1)}, bf16[4,128,256]{2,1,0:T(8,128)(2,1)S(1)}, u32[]{:S(2)}, u32[]{:S(2)}) collective-permute-start(bf16[4,128,256]{2,1,0:T(8,128)(2,1)S(1)} %pad_maximum_fusion.refs_2_), channel_id=1, source_target_pairs={{0,6},{2,4},{4,2},{6,0},{8,14},{10,12},{12,10},{14,8},{16,22},{18,... | collective-permute-start | bytes 786440 | tf_op jit(solution)/shard_map/ppermute | solution.py:344
  19.8 3.7 %collective-permute-start.10 = (bf16[4,128,256]{2,1,0:T(8,128)(2,1)S(1)}, bf16[4,128,256]{2,1,0:T(8,128)(2,1)S(1)}, u32[]{:S(2)}, u32[]{:S(2)}) collective-permute-start(bf16[4,128,256]{2,1,0:T(8,128)(2,1)S(1)} %pad_maximum_fusion.1.refs_2_), channel_id=1, source_target_pairs={{0,24},{2,26},{4,28},{6,30},{8,16},{10,18},{12,20},{14,22},{16,8},... | collective-permute-start | bytes 786440 | tf_op jit(solution)/shard_map/ppermute | solution.py:348
  23.5 1.4 %collective-permute-done.5.refs_3_ = bf16[4,128,256]{2,1,0:T(8,128)(2,1)S(1)} collective-permute-done((bf16[4,128,256]{2,1,0:T(8,128)(2,1)S(1)}, bf16[4,128,256]{2,1,0:T(8,128)(2,1)S(1)}, u32[]{:S(2)}, u32[]{:S(2)}) %collective-permute-start.5) | collective-permute-done | bytes 262176 | tf_op jit(solution)/shard_map/ppermute | solution.py:344
  24.9 0.7 collective-permute-start.8
  25.5 2.7 %collective-permute-done.6.refs_4_ = bf16[4,128,256]{2,1,0:T(8,128)(2,1)S(1)} collective-permute-done((bf16[4,128,256]{2,1,0:T(8,128)(2,1)S(1)}, bf16[4,128,256]{2,1,0:T(8,128)(2,1)S(1)}, u32[]{:S(2)}, u32[]{:S(2)}) %collective-permute-start.6) | collective-permute-done | bytes 262176 | tf_op jit(solution)/shard_map/ppermute | solution.py:344
  28.2 7.1 %attention_backward.2 = (bf16[2,16,512,128]{3,2,1,0:T(8,128)(2,1)S(1)}, bf16[2,512,128]{2,1,0:T(8,128)(2,1)S(1)}, bf16[528,256]{1,0:T(8,128)(2,1)S(1)}, bf16[528...) custom-call(f32[1]{0:T(128)S(6)} %tanh.3.refs_0_.gate_ref, ...), custom_call_target="tpu_custom_call" | custom-call | flops 2147483648 | bytes 2097152 | tf_op jit(solution)/shard_map/attention_backward/pallas_call | solution.py:255
  35.3 1.6 %collective-permute-start.11 = (bf16[528,256]{1,0:T(8,128)(2,1)S(1)}, bf16[528,256]{1,0:T(8,128)(2,1)S(1)}, u32[]{:S(2)}, u32[]{:S(2)}) collective-permute-start(bf16[528,256]{1,0:T(8,128)(2,1)S(1)} %get-tuple-element.55), channel_id=1, source_target_pairs={{0,2},{2,0},{4,6},{6,4},{8,10},{10,8},{12,14},{14,12},{16,18},{18,... | collective-permute-start | bytes 811016 | tf_op jit(solution)/shard_map/ppermute | solution.py:344
  36.9 0.7 collective-permute-start.12
  37.5 1.3 %collective-permute-start.13 = (bf16[528,256]{1,0:T(8,128)(2,1)S(1)}, bf16[528,256]{1,0:T(8,128)(2,1)S(1)}, u32[]{:S(2)}, u32[]{:S(2)}) collective-permute-start(bf16[528,256]{1,0:T(8,128)(2,1)S(1)} %get-tuple-element.57), channel_id=1, source_target_pairs={{0,6},{2,4},{4,2},{6,0},{8,14},{10,12},{12,10},{14,8},{16,22},{18,... | collective-permute-start | bytes 811016 | tf_op jit(solution)/shard_map/ppermute | solution.py:344
  38.9 3.7 %collective-permute-done.9.refs_4_ = bf16[4,128,256]{2,1,0:T(8,128)(2,1)S(1)} collective-permute-done((bf16[4,128,256]{2,1,0:T(8,128)(2,1)S(1)}, bf16[4,128,256]{2,1,0:T(8,128)(2,1)S(1)}, u32[]{:S(2)}, u32[]{:S(2)}) %collective-permute-start.9) | collective-permute-done | bytes 262176 | tf_op jit(solution)/shard_map/ppermute | solution.py:348
  42.6 7.9 %attention_backward.3 = (bf16[2,16,512,128]{3,2,1,0:T(8,128)(2,1)S(1)}, bf16[2,512,128]{2,1,0:T(8,128)(2,1)S(1)}, bf16[528,256]{1,0:T(8,128)(2,1)S(1)}, bf16[528...) custom-call(f32[1]{0:T(128)S(6)} %tanh.3.refs_0_.gate_ref, ...), custom_call_target="tpu_custom_call" | custom-call | flops 2147483648 | bytes 2097152 | tf_op jit(solution)/shard_map/attention_backward/pallas_call | solution.py:255
  50.5 0.2 fusion.20
  50.7 0.1 collective-permute-start.17
  50.8 0.6 collective-permute-start.14
  51.4 0.5 collective-permute-start.15
  51.9 2.4 %collective-permute-start.16 = (bf16[528,256]{1,0:T(8,128)(2,1)S(1)}, bf16[528,256]{1,0:T(8,128)(2,1)S(1)}, u32[]{:S(2)}, u32[]{:S(2)}) collective-permute-start(bf16[528,256]{1,0:T(8,128)(2,1)S(1)} %get-tuple-element.60), channel_id=1, source_target_pairs={{0,6},{2,4},{4,2},{6,0},{8,14},{10,12},{12,10},{14,8},{16,22},{18,... | collective-permute-start | bytes 811016 | tf_op jit(solution)/shard_map/ppermute | solution.py:344
  54.3 3.0 %collective-permute-start.18 = (bf16[128,256]{1,0:T(8,128)(2,1)S(1)}, bf16[128,256]{1,0:T(8,128)(2,1)S(1)}, u32[]{:S(2)}, u32[]{:S(2)}) collective-permute-start(bf16[128,256]{1,0:T(8,128)(2,1)S(1)} %get-tuple-element.83), channel_id=1, source_target_pairs={{0,16},{2,18},{4,20},{6,22},{8,24},{10,26},{12,28},{14,30},{16,0},... | collective-permute-start | bytes 196616 | tf_op jit(solution)/shard_map/ppermute | solution.py:348
  57.3 1.3 %collective-permute-start.19 = (bf16[128,256]{1,0:T(8,128)(2,1)S(1)}, bf16[128,256]{1,0:T(8,128)(2,1)S(1)}, u32[]{:S(2)}, u32[]{:S(2)}) collective-permute-start(bf16[128,256]{1,0:T(8,128)(2,1)S(1)} %get-tuple-element.84), channel_id=1, source_target_pairs={{0,24},{2,26},{4,28},{6,30},{8,16},{10,18},{12,20},{14,22},{16,8},... | collective-permute-start | bytes 196616 | tf_op jit(solution)/shard_map/ppermute | solution.py:348
  58.6 1.7 %query_gradient.2.rest_0_ = bf16[256,4096]{1,0:T(8,128)(2,1)} custom-call(f32[1]{0:T(128)S(6)} %tanh.3.refs_0_.gate_ref, bf16[2,16,512,128]{3,2,1,0:T(8,128)(2,1)S(1)} %get-tuple-element.63.ds_ref, bf16[2,512,128]{2,1,0:T(8,128)(2,1)S(1)} %get-tuple-element.64.k_ref, bf16[128,256]{1,0:T(8,128)(2,1)S(1)} %collective-permute-done.17.rest_0_), custom_call_target="tpu_custom_call" | custom-call | flops 536870912 | bytes 4194304 | tf_op jit(solution)/shard_map/query_gradient/pallas_call | solution.py:313
  60.4 1.7 %query_gradient.3 = bf16[256,4096]{1,0:T(8,128)(2,1)} custom-call(f32[1]{0:T(128)S(6)} %tanh.3.refs_0_.gate_ref, bf16[2,16,512,128]{3,2,1,0:T(8,128)(2,1)S(1)} %get-tuple-element.61.ds_ref, bf16[2,512,128]{2,1,0:T(8,128)(2,1)S(1)} %get-tuple-element.62.k_ref, bf16[256,4096]{1,0:T(8,128)(2,1)} %query_gradient.2.rest_0_, ...), custom_call_target="tpu_custom_call", output_to_operand_aliasing={{}: (3, {})} | custom-call | flops 536870912 | bytes 4194304 | tf_op jit(solution)/shard_map/query_gradient/pallas_call | solution.py:313
  62.1 1.4 %collective-permute-done.15 = bf16[528,256]{1,0:T(8,128)(2,1)S(1)} collective-permute-done((bf16[528,256]{1,0:T(8,128)(2,1)S(1)}, bf16[528,256]{1,0:T(8,128)(2,1)S(1)}, u32[]{:S(2)}, u32[]{:S(2)}) %collective-permute-start.15) | collective-permute-done | bytes 270368 | tf_op jit(solution)/shard_map/ppermute | solution.py:344
  63.5 0.2 fusion.18
  63.7 0.1 select_convert_fusion
  63.8 1.5 %collective-permute-start.22 = (bf16[144,256]{1,0:T(8,128)(2,1)S(1)}, bf16[144,256]{1,0:T(8,128)(2,1)S(1)}, u32[]{:S(2)}, u32[]{:S(2)}) collective-permute-start(bf16[144,256]{1,0:T(8,128)(2,1)S(1)} %get-tuple-element.98), channel_id=1, source_target_pairs={{0,24},{2,26},{4,28},{6,30},{8,16},{10,18},{12,20},{14,22},{16,8},... | collective-permute-start | bytes 221192 | tf_op jit(solution)/shard_map/ppermute | solution.py:348
  65.3 1.8 %collective-permute-start.21 = (bf16[144,256]{1,0:T(8,128)(2,1)S(1)}, bf16[144,256]{1,0:T(8,128)(2,1)S(1)}, u32[]{:S(2)}, u32[]{:S(2)}) collective-permute-start(bf16[144,256]{1,0:T(8,128)(2,1)S(1)} %get-tuple-element.97), channel_id=1, source_target_pairs={{0,16},{2,18},{4,20},{6,22},{8,24},{10,26},{12,28},{14,30},{16,0},... | collective-permute-start | bytes 221192 | tf_op jit(solution)/shard_map/ppermute | solution.py:348
  67.1 1.3 %collective-permute-start.20 = (bf16[144,256]{1,0:T(8,128)(2,1)S(1)}, bf16[144,256]{1,0:T(8,128)(2,1)S(1)}, u32[]{:S(2)}, u32[]{:S(2)}) collective-permute-start(bf16[144,256]{1,0:T(8,128)(2,1)S(1)} %get-tuple-element.96), channel_id=1, source_target_pairs={{0,8},{2,10},{4,12},{6,14},{8,0},{10,2},{12,4},{14,6},{16,24},{18,... | collective-permute-start | bytes 221192 | tf_op jit(solution)/shard_map/ppermute | solution.py:348
  68.4 1.8 %collective-permute-done.22 = bf16[144,256]{1,0:T(8,128)(2,1)S(1)} collective-permute-done((bf16[144,256]{1,0:T(8,128)(2,1)S(1)}, bf16[144,256]{1,0:T(8,128)(2,1)S(1)}, u32[]{:S(2)}, u32[]{:S(2)}) %collective-permute-start.22) | collective-permute-done | bytes 73760 | tf_op jit(solution)/shard_map/ppermute | solution.py:348
  70.1 1.7 %collective-permute-done.21 = bf16[144,256]{1,0:T(8,128)(2,1)S(1)} collective-permute-done((bf16[144,256]{1,0:T(8,128)(2,1)S(1)}, bf16[144,256]{1,0:T(8,128)(2,1)S(1)}, u32[]{:S(2)}, u32[]{:S(2)}) %collective-permute-start.21) | collective-permute-done | bytes 73760 | tf_op jit(solution)/shard_map/ppermute | solution.py:348
  71.8 0.4 collective-permute-done.20
  72.3 0.1 collective-permute-start.23
  72.4 0.7 fusion.8
  73.0 0.4 collective-permute-done.23
  73.5 0.5 fusion.15
  (36 shorter events, 0.3 us)
Async XLA Ops:
  1.5 8.2 %collective-permute-start.3 = (bf16[128,256]{1,0:T(8,128)(2,1)S(1)}, bf16[128,256]{1,0:T(8,128)(2,1)S(1)}, u32[]{:S(2)}, u32[]{:S(2)}) collective-permute-start(bf16[128,256]{1,0:T(8,128)(2,1)S(1)} %get-tuple-element.89), channel_id=1, source_target_pairs={{0,2},{2,0},{4,6},{6,4},{8,10},{10,8},{12,14},{14,12},{16,18},{18,... | collective-permute-start | bytes 196616 | tf_op jit(solution)/shard_map/ppermute | solution.py:344
  4.5 7.6 %collective-permute-start = (bf16[128,256]{1,0:T(8,128)(2,1)S(1)}, bf16[128,256]{1,0:T(8,128)(2,1)S(1)}, u32[]{:S(2)}, u32[]{:S(2)}) collective-permute-start(bf16[128,256]{1,0:T(8,128)(2,1)S(1)} %get-tuple-element.95), channel_id=1, source_target_pairs={{0,8},{2,10},{4,12},{6,14},{8,0},{10,2},{12,4},{14,6},{16,24},{18,... | collective-permute-start | bytes 196616 | tf_op jit(solution)/shard_map/ppermute | solution.py:348
  6.1 9.3 %collective-permute-start.1 = (bf16[128,256]{1,0:T(8,128)(2,1)S(1)}, bf16[128,256]{1,0:T(8,128)(2,1)S(1)}, u32[]{:S(2)}, u32[]{:S(2)}) collective-permute-start(bf16[128,256]{1,0:T(8,128)(2,1)S(1)} %get-tuple-element.95), channel_id=1, source_target_pairs={{0,16},{2,18},{4,20},{6,22},{8,24},{10,26},{12,28},{14,30},{16,0},... | collective-permute-start | bytes 196616 | tf_op jit(solution)/shard_map/ppermute | solution.py:348
  8.7 6.7 %collective-permute-start.2 = (bf16[128,256]{1,0:T(8,128)(2,1)S(1)}, bf16[128,256]{1,0:T(8,128)(2,1)S(1)}, u32[]{:S(2)}, u32[]{:S(2)}) collective-permute-start(bf16[128,256]{1,0:T(8,128)(2,1)S(1)} %get-tuple-element.95), channel_id=1, source_target_pairs={{0,24},{2,26},{4,28},{6,30},{8,16},{10,18},{12,20},{14,22},{16,8},... | collective-permute-start | bytes 196616 | tf_op jit(solution)/shard_map/ppermute | solution.py:348
  9.7 5.8 %collective-permute-start.4 = (bf16[2,128,256]{2,1,0:T(8,128)(2,1)S(1)}, bf16[2,128,256]{2,1,0:T(8,128)(2,1)S(1)}, u32[]{:S(2)}, u32[]{:S(2)}) collective-permute-start(bf16[2,128,256]{2,1,0:T(8,128)(2,1)S(1)} %pad_maximum_fusion.2), channel_id=1, source_target_pairs={{0,4},{2,6},{4,0},{6,2},{8,12},{10,14},{12,8},{14,10},{16,20},{18,... | collective-permute-start | bytes 393224 | tf_op jit(solution)/shard_map/ppermute | solution.py:344
  15.5 9.3 %collective-permute-start.5 = (bf16[4,128,256]{2,1,0:T(8,128)(2,1)S(1)}, bf16[4,128,256]{2,1,0:T(8,128)(2,1)S(1)}, u32[]{:S(2)}, u32[]{:S(2)}) collective-permute-start(bf16[4,128,256]{2,1,0:T(8,128)(2,1)S(1)} %pad_maximum_fusion.refs_2_), channel_id=1, source_target_pairs={{0,2},{2,0},{4,6},{6,4},{8,10},{10,8},{12,14},{14,12},{16,18},{18,... | collective-permute-start | bytes 786440 | tf_op jit(solution)/shard_map/ppermute | solution.py:344
  16.1 12.0 %collective-permute-start.6 = (bf16[4,128,256]{2,1,0:T(8,128)(2,1)S(1)}, bf16[4,128,256]{2,1,0:T(8,128)(2,1)S(1)}, u32[]{:S(2)}, u32[]{:S(2)}) collective-permute-start(bf16[4,128,256]{2,1,0:T(8,128)(2,1)S(1)} %pad_maximum_fusion.refs_2_), channel_id=1, source_target_pairs={{0,4},{2,6},{4,0},{6,2},{8,12},{10,14},{12,8},{14,10},{16,20},{18,... | collective-permute-start | bytes 786440 | tf_op jit(solution)/shard_map/ppermute | solution.py:344
  17.0 11.2 %collective-permute-start.7 = (bf16[4,128,256]{2,1,0:T(8,128)(2,1)S(1)}, bf16[4,128,256]{2,1,0:T(8,128)(2,1)S(1)}, u32[]{:S(2)}, u32[]{:S(2)}) collective-permute-start(bf16[4,128,256]{2,1,0:T(8,128)(2,1)S(1)} %pad_maximum_fusion.refs_2_), channel_id=1, source_target_pairs={{0,6},{2,4},{4,2},{6,0},{8,14},{10,12},{12,10},{14,8},{16,22},{18,... | collective-permute-start | bytes 786440 | tf_op jit(solution)/shard_map/ppermute | solution.py:344
  19.8 17.7 %collective-permute-start.10 = (bf16[4,128,256]{2,1,0:T(8,128)(2,1)S(1)}, bf16[4,128,256]{2,1,0:T(8,128)(2,1)S(1)}, u32[]{:S(2)}, u32[]{:S(2)}) collective-permute-start(bf16[4,128,256]{2,1,0:T(8,128)(2,1)S(1)} %pad_maximum_fusion.1.refs_2_), channel_id=1, source_target_pairs={{0,24},{2,26},{4,28},{6,30},{8,16},{10,18},{12,20},{14,22},{16,8},... | collective-permute-start | bytes 786440 | tf_op jit(solution)/shard_map/ppermute | solution.py:348
  23.5 19.2 %collective-permute-start.9 = (bf16[4,128,256]{2,1,0:T(8,128)(2,1)S(1)}, bf16[4,128,256]{2,1,0:T(8,128)(2,1)S(1)}, u32[]{:S(2)}, u32[]{:S(2)}) collective-permute-start(bf16[4,128,256]{2,1,0:T(8,128)(2,1)S(1)} %pad_maximum_fusion.1.refs_2_), channel_id=1, source_target_pairs={{0,16},{2,18},{4,20},{6,22},{8,24},{10,26},{12,28},{14,30},{16,0},... | collective-permute-start | bytes 786440 | tf_op jit(solution)/shard_map/ppermute | solution.py:348
  24.9 17.8 %collective-permute-start.8 = (bf16[4,128,256]{2,1,0:T(8,128)(2,1)S(1)}, bf16[4,128,256]{2,1,0:T(8,128)(2,1)S(1)}, u32[]{:S(2)}, u32[]{:S(2)}) collective-permute-start(bf16[4,128,256]{2,1,0:T(8,128)(2,1)S(1)} %pad_maximum_fusion.1.refs_2_), channel_id=1, source_target_pairs={{0,8},{2,10},{4,12},{6,14},{8,0},{10,2},{12,4},{14,6},{16,24},{18,... | collective-permute-start | bytes 786440 | tf_op jit(solution)/shard_map/ppermute | solution.py:348
  35.3 15.2 %collective-permute-start.11 = (bf16[528,256]{1,0:T(8,128)(2,1)S(1)}, bf16[528,256]{1,0:T(8,128)(2,1)S(1)}, u32[]{:S(2)}, u32[]{:S(2)}) collective-permute-start(bf16[528,256]{1,0:T(8,128)(2,1)S(1)} %get-tuple-element.55), channel_id=1, source_target_pairs={{0,2},{2,0},{4,6},{6,4},{8,10},{10,8},{12,14},{14,12},{16,18},{18,... | collective-permute-start | bytes 811016 | tf_op jit(solution)/shard_map/ppermute | solution.py:344
  36.9 13.6 %collective-permute-start.12 = (bf16[528,256]{1,0:T(8,128)(2,1)S(1)}, bf16[528,256]{1,0:T(8,128)(2,1)S(1)}, u32[]{:S(2)}, u32[]{:S(2)}) collective-permute-start(bf16[528,256]{1,0:T(8,128)(2,1)S(1)} %get-tuple-element.56), channel_id=1, source_target_pairs={{0,4},{2,6},{4,0},{6,2},{8,12},{10,14},{12,8},{14,10},{16,20},{18,... | collective-permute-start | bytes 811016 | tf_op jit(solution)/shard_map/ppermute | solution.py:344
  37.5 13.0 %collective-permute-start.13 = (bf16[528,256]{1,0:T(8,128)(2,1)S(1)}, bf16[528,256]{1,0:T(8,128)(2,1)S(1)}, u32[]{:S(2)}, u32[]{:S(2)}) collective-permute-start(bf16[528,256]{1,0:T(8,128)(2,1)S(1)} %get-tuple-element.57), channel_id=1, source_target_pairs={{0,6},{2,4},{4,2},{6,0},{8,14},{10,12},{12,10},{14,8},{16,22},{18,... | collective-permute-start | bytes 811016 | tf_op jit(solution)/shard_map/ppermute | solution.py:344
  50.7 6.6 %collective-permute-start.17 = (bf16[128,256]{1,0:T(8,128)(2,1)S(1)}, bf16[128,256]{1,0:T(8,128)(2,1)S(1)}, u32[]{:S(2)}, u32[]{:S(2)}) collective-permute-start(bf16[128,256]{1,0:T(8,128)(2,1)S(1)} %get-tuple-element.85), channel_id=1, source_target_pairs={{0,8},{2,10},{4,12},{6,14},{8,0},{10,2},{12,4},{14,6},{16,24},{18,... | collective-permute-start | bytes 196616 | tf_op jit(solution)/shard_map/ppermute | solution.py:348
  50.8 9.6 %collective-permute-start.14 = (bf16[528,256]{1,0:T(8,128)(2,1)S(1)}, bf16[528,256]{1,0:T(8,128)(2,1)S(1)}, u32[]{:S(2)}, u32[]{:S(2)}) collective-permute-start(bf16[528,256]{1,0:T(8,128)(2,1)S(1)} %get-tuple-element.58), channel_id=1, source_target_pairs={{0,2},{2,0},{4,6},{6,4},{8,10},{10,8},{12,14},{14,12},{16,18},{18,... | collective-permute-start | bytes 811016 | tf_op jit(solution)/shard_map/ppermute | solution.py:344
  51.4 12.1 %collective-permute-start.15 = (bf16[528,256]{1,0:T(8,128)(2,1)S(1)}, bf16[528,256]{1,0:T(8,128)(2,1)S(1)}, u32[]{:S(2)}, u32[]{:S(2)}) collective-permute-start(bf16[528,256]{1,0:T(8,128)(2,1)S(1)} %get-tuple-element.59), channel_id=1, source_target_pairs={{0,4},{2,6},{4,0},{6,2},{8,12},{10,14},{12,8},{14,10},{16,20},{18,... | collective-permute-start | bytes 811016 | tf_op jit(solution)/shard_map/ppermute | solution.py:344
  51.9 11.6 %collective-permute-start.16 = (bf16[528,256]{1,0:T(8,128)(2,1)S(1)}, bf16[528,256]{1,0:T(8,128)(2,1)S(1)}, u32[]{:S(2)}, u32[]{:S(2)}) collective-permute-start(bf16[528,256]{1,0:T(8,128)(2,1)S(1)} %get-tuple-element.60), channel_id=1, source_target_pairs={{0,6},{2,4},{4,2},{6,0},{8,14},{10,12},{12,10},{14,8},{16,22},{18,... | collective-permute-start | bytes 811016 | tf_op jit(solution)/shard_map/ppermute | solution.py:344
  54.3 10.9 %collective-permute-start.18 = (bf16[128,256]{1,0:T(8,128)(2,1)S(1)}, bf16[128,256]{1,0:T(8,128)(2,1)S(1)}, u32[]{:S(2)}, u32[]{:S(2)}) collective-permute-start(bf16[128,256]{1,0:T(8,128)(2,1)S(1)} %get-tuple-element.83), channel_id=1, source_target_pairs={{0,16},{2,18},{4,20},{6,22},{8,24},{10,26},{12,28},{14,30},{16,0},... | collective-permute-start | bytes 196616 | tf_op jit(solution)/shard_map/ppermute | solution.py:348
  57.3 7.9 %collective-permute-start.19 = (bf16[128,256]{1,0:T(8,128)(2,1)S(1)}, bf16[128,256]{1,0:T(8,128)(2,1)S(1)}, u32[]{:S(2)}, u32[]{:S(2)}) collective-permute-start(bf16[128,256]{1,0:T(8,128)(2,1)S(1)} %get-tuple-element.84), channel_id=1, source_target_pairs={{0,24},{2,26},{4,28},{6,30},{8,16},{10,18},{12,20},{14,22},{16,8},... | collective-permute-start | bytes 196616 | tf_op jit(solution)/shard_map/ppermute | solution.py:348
  63.8 6.3 %collective-permute-start.22 = (bf16[144,256]{1,0:T(8,128)(2,1)S(1)}, bf16[144,256]{1,0:T(8,128)(2,1)S(1)}, u32[]{:S(2)}, u32[]{:S(2)}) collective-permute-start(bf16[144,256]{1,0:T(8,128)(2,1)S(1)} %get-tuple-element.98), channel_id=1, source_target_pairs={{0,24},{2,26},{4,28},{6,30},{8,16},{10,18},{12,20},{14,22},{16,8},... | collective-permute-start | bytes 221192 | tf_op jit(solution)/shard_map/ppermute | solution.py:348
  65.3 6.5 %collective-permute-start.21 = (bf16[144,256]{1,0:T(8,128)(2,1)S(1)}, bf16[144,256]{1,0:T(8,128)(2,1)S(1)}, u32[]{:S(2)}, u32[]{:S(2)}) collective-permute-start(bf16[144,256]{1,0:T(8,128)(2,1)S(1)} %get-tuple-element.97), channel_id=1, source_target_pairs={{0,16},{2,18},{4,20},{6,22},{8,24},{10,26},{12,28},{14,30},{16,0},... | collective-permute-start | bytes 221192 | tf_op jit(solution)/shard_map/ppermute | solution.py:348
  67.1 5.1 %collective-permute-start.20 = (bf16[144,256]{1,0:T(8,128)(2,1)S(1)}, bf16[144,256]{1,0:T(8,128)(2,1)S(1)}, u32[]{:S(2)}, u32[]{:S(2)}) collective-permute-start(bf16[144,256]{1,0:T(8,128)(2,1)S(1)} %get-tuple-element.96), channel_id=1, source_target_pairs={{0,8},{2,10},{4,12},{6,14},{8,0},{10,2},{12,4},{14,6},{16,24},{18,... | collective-permute-start | bytes 221192 | tf_op jit(solution)/shard_map/ppermute | solution.py:348
  72.3 1.2 %collective-permute-start.23 = (f32[1,256]{1,0:T(1,128)S(1)}, f32[1,256]{1,0:T(1,128)S(1)}, u32[]{:S(2)}, u32[]{:S(2)}) collective-permute-start(f32[1,256]{1,0:T(1,128)S(1)} %fusion.9), channel_id=1, source_target_pairs={{0,1},{1,0},{2,3},{3,2},{4,5},{5,4},{6,7},{7,6},{8,9},{9,8},{10,11... | collective-permute-start | bytes 3080 | tf_op jit(solution)/shard_map/ppermute | solution.py:424

commit v6 on v5

--- a/solution.py
+++ b/solution.py
@@ -387,10 +387,10 @@
     owns = [own_columns(c) for c in range(chunks)]
     starts = [square_of(own) if c else column_of(own) for c, own in enumerate(owns)]
     sizes = (n, *block_mask.shape, heads, local_kv, queries.shape[0])
-    shared = prepare(sizes, img_tok, plan, queries, cotangent, near_z[0])
-    shared, starts = lax.optimization_barrier((tuple(shared), starts))
+    plan, starts, gate_value = lax.optimization_barrier((plan, starts, gate_value))
     column = starts[0]
     gathered = [[column, swap(column, 1), swap(column, 2), swap(column, 3)]]
+    shared = tuple(prepare(sizes, img_tok, plan, queries, cotangent, gathered[0][1]))
     for square in starts[1:]:
         far = [swap_z(square, k) for k in range(2, n)]
         gathered[0][1], near = lax.optimization_barrier((gathered[0][1], square))

time: 74.2 us -> 73 us (0.984)
    ppermute x11, waiting for transfers between devices: 5.43 us -> 4.39 us  [swap(): return lax.ppermute(value, 'ctx', [(i, i ^ bit) for i in range(n_ctx)])]
  transfers between devices with their start and end apart: 24 -> 24, of which waited for: 8 -> 11; matrix products, arithmetic and copies ran while one was open for 4% -> 4% of each run, Pallas kernels for 29% -> 30%
where the time goes in v6:
time: 73 us; the launch traced here: 72.8 us
  starting transfers between devices  32.4 us (44%)
  Pallas kernels  21.8 us (30%)
  waiting for transfers between devices  13 us (18%)
  other arithmetic  2.53 us (3%)
  local copies, waits for them, and re-layouts  1.61 us (2%)
  between operations  1.52 us (2%)
    ppermute x12, starting transfers between devices, swap_z(): return lax.ppermute(value, 'ctx', pairs)  17.1 us
    ppermute x11, starting transfers between devices, swap(): return lax.ppermute(value, 'ctx', [(i, i ^ bit) for i in range(n_ctx)])  15.2 us
    pallas_call x2, Pallas kernels, attention(): pl.pallas_call(kernel, in_specs=in_specs, out_specs=[vmem] * len(out_shap...  15 us
    ppermute x12, waiting for transfers between devices, swap_z(): return lax.ppermute(value, 'ctx', pairs)  8.16 us
    ppermute x11, waiting for transfers between devices, swap(): return lax.ppermute(value, 'ctx', [(i, i ^ bit) for i in range(n_ctx)])  4.39 us
    pallas_call x2, Pallas kernels, query_gradient(): pl.pallas_call(functools.partial(query_kernel, at * heads, n_blocks, len(...  3.42 us
    pallas_call x1, Pallas kernels, prepare(): pl.pallas_call(functools.partial(prepare_kernel, n, n_blocks, n_images, 2...  3.38 us
  transfers between devices with their start and end apart: 24, of which 11 were waited for; matrix products, arithmetic and copies ran while one was open for 4% of the time, Pallas kernels for 30%

profile of v6, /device:TPU:0, one launch (start us, length us, event | category | flops | bytes accessed | tf_op | source)
XLA Modules:
  0.0 72.8 jit_solution(13159280051655888702)
XLA Ops:
  0.6 0.8 %slice_bitcast_fusion = (bf16[64,256]{1,0:T(8,128)(2,1)S(1)}, bf16[64,256]{1,0:T(8,128)(2,1)S(1)}, bf16[64,256]{1,0:T(8,128)(2,1)S(1)}, bf16[64,256]{1,0:T(8,128)(2,1)S(1)}) fusion(bf16[1,64,512]{2,1,0:T(8,128)(2,1)} %param.10, bf16[1,64,512]{2,1,0:T(8,128)(2,1)} %param.9), kind=kLoop, calls=%fused_computation.24 | loop fusion | bytes 262144 | tf_op jit(solution)/shard_map/squeeze | solution.py:352
  1.5 3.0 %collective-permute-start.3 = (bf16[128,256]{1,0:T(8,128)(2,1)S(1)}, bf16[128,256]{1,0:T(8,128)(2,1)S(1)}, u32[]{:S(2)}, u32[]{:S(2)}) collective-permute-start(bf16[128,256]{1,0:T(8,128)(2,1)S(1)} %get-tuple-element.85), channel_id=1, source_target_pairs={{0,2},{2,0},{4,6},{6,4},{8,10},{10,8},{12,14},{14,12},{16,18},{18,... | collective-permute-start | bytes 196616 | tf_op jit(solution)/shard_map/ppermute | solution.py:344
  4.5 1.6 %collective-permute-start = (bf16[128,256]{1,0:T(8,128)(2,1)S(1)}, bf16[128,256]{1,0:T(8,128)(2,1)S(1)}, u32[]{:S(2)}, u32[]{:S(2)}) collective-permute-start(bf16[128,256]{1,0:T(8,128)(2,1)S(1)} %get-tuple-element.91), channel_id=1, source_target_pairs={{0,8},{2,10},{4,12},{6,14},{8,0},{10,2},{12,4},{14,6},{16,24},{18,... | collective-permute-start | bytes 196616 | tf_op jit(solution)/shard_map/ppermute | solution.py:348
  6.1 2.6 %collective-permute-start.1 = (bf16[128,256]{1,0:T(8,128)(2,1)S(1)}, bf16[128,256]{1,0:T(8,128)(2,1)S(1)}, u32[]{:S(2)}, u32[]{:S(2)}) collective-permute-start(bf16[128,256]{1,0:T(8,128)(2,1)S(1)} %get-tuple-element.91), channel_id=1, source_target_pairs={{0,16},{2,18},{4,20},{6,22},{8,24},{10,26},{12,28},{14,30},{16,0},... | collective-permute-start | bytes 196616 | tf_op jit(solution)/shard_map/ppermute | solution.py:348
  8.7 0.2 collective-permute-start.2
  8.9 0.8 %reshape.39 = s32[32]{0:T(128)S(1)} reshape(s32[2,16]{1,0:T(2,128)} %param.12) | data formatting | bytes 256 | tf_op jit(solution)/shard_map/reshape | solution.py:340
  9.7 0.0 collective-permute-done.3
  9.7 1.6 %collective-permute-start.4 = (bf16[2,128,256]{2,1,0:T(8,128)(2,1)S(1)}, bf16[2,128,256]{2,1,0:T(8,128)(2,1)S(1)}, u32[]{:S(2)}, u32[]{:S(2)}) collective-permute-start(bf16[2,128,256]{2,1,0:T(8,128)(2,1)S(1)} %pad_maximum_fusion.2), channel_id=1, source_target_pairs={{0,4},{2,6},{4,0},{6,2},{8,12},{10,14},{12,8},{14,10},{16,20},{18,... | collective-permute-start | bytes 393224 | tf_op jit(solution)/shard_map/ppermute | solution.py:344
  11.3 0.7 %pad_add_fusion.refs_0_ = s32[49]{0:T(128)S(1)} fusion(s32[1]{0:T(128)} %bitcast, s32[16]{0:T(128)} %param.13, s32[32]{0:T(128)S(1)} %reshape.39), kind=kLoop, calls=%fused_computation.58 | loop fusion | flops 98 | bytes 392 | tf_op jit(solution)/shard_map/concatenate | solution.py:340
  12.7 0.4 collective-permute-done.1
  13.1 1.7 %collective-permute-done.2 = bf16[128,256]{1,0:T(8,128)(2,1)S(1)} collective-permute-done((bf16[128,256]{1,0:T(8,128)(2,1)S(1)}, bf16[128,256]{1,0:T(8,128)(2,1)S(1)}, u32[]{:S(2)}, u32[]{:S(2)}) %collective-permute-start.2) | collective-permute-done | bytes 65568 | tf_op jit(solution)/shard_map/ppermute | solution.py:348
  14.9 0.6 collective-permute-start.5
  15.5 1.5 %collective-permute-start.6 = (bf16[4,128,256]{2,1,0:T(8,128)(2,1)S(1)}, bf16[4,128,256]{2,1,0:T(8,128)(2,1)S(1)}, u32[]{:S(2)}, u32[]{:S(2)}) collective-permute-start(bf16[4,128,256]{2,1,0:T(8,128)(2,1)S(1)} %pad_maximum_fusion.refs_2_), channel_id=1, source_target_pairs={{0,4},{2,6},{4,0},{6,2},{8,12},{10,14},{12,8},{14,10},{16,20},{18,... | collective-permute-start | bytes 786440 | tf_op jit(solution)/shard_map/ppermute | solution.py:344
  17.0 1.4 %collective-permute-start.7 = (bf16[4,128,256]{2,1,0:T(8,128)(2,1)S(1)}, bf16[4,128,256]{2,1,0:T(8,128)(2,1)S(1)}, u32[]{:S(2)}, u32[]{:S(2)}) collective-permute-start(bf16[4,128,256]{2,1,0:T(8,128)(2,1)S(1)} %pad_maximum_fusion.refs_2_), channel_id=1, source_target_pairs={{0,6},{2,4},{4,2},{6,0},{8,14},{10,12},{12,10},{14,8},{16,22},{18,... | collective-permute-start | bytes 786440 | tf_op jit(solution)/shard_map/ppermute | solution.py:344
  18.4 3.5 %collective-permute-start.10 = (bf16[4,128,256]{2,1,0:T(8,128)(2,1)S(1)}, bf16[4,128,256]{2,1,0:T(8,128)(2,1)S(1)}, u32[]{:S(2)}, u32[]{:S(2)}) collective-permute-start(bf16[4,128,256]{2,1,0:T(8,128)(2,1)S(1)} %pad_maximum_fusion.1.refs_2_), channel_id=1, source_target_pairs={{0,24},{2,26},{4,28},{6,30},{8,16},{10,18},{12,20},{14,22},{16,8},... | collective-permute-start | bytes 786440 | tf_op jit(solution)/shard_map/ppermute | solution.py:348
  22.0 1.9 %collective-permute-done.5.refs_3_ = bf16[4,128,256]{2,1,0:T(8,128)(2,1)S(1)} collective-permute-done((bf16[4,128,256]{2,1,0:T(8,128)(2,1)S(1)}, bf16[4,128,256]{2,1,0:T(8,128)(2,1)S(1)}, u32[]{:S(2)}, u32[]{:S(2)}) %collective-permute-start.5) | collective-permute-done | bytes 262176 | tf_op jit(solution)/shard_map/ppermute | solution.py:344
  23.9 0.2 collective-permute-start.8
  24.1 3.4 %prepare.1 = (s32[3,8]{1,0:T(4,128)S(1)}, f32[2,8]{1,0:T(2,128)S(1)}, bf16[256,4096]{1,0:T(8,128)(2,1)S(1)}, bf16[256,4096]{1,0:T(8,128)(2,1)S(1)}) custom-call(s32[49]{0:T(128)S(1)} %pad_add_fusion.refs_0_, bf16[256,4096]{1,0:T(8,128)(2,1)} %refs_1_.1, bf16[256,4096]{1,0:T(8,128)(2,1)} %refs_2_.1, bf16[4,128,256]{2,1,0:T(8,128)(2,1)S(1)} %collective-permute-done.5.refs_3_), custom_call_target="tpu_custom_call" | custom-call | bytes 8388608 | tf_op jit(solution)/shard_map/prepare/pallas_call | solution.py:95
  27.5 0.1 collective-permute-done.7.refs_5_
  27.7 7.2 %attention_backward.2 = (bf16[2,16,512,128]{3,2,1,0:T(8,128)(2,1)S(1)}, bf16[2,512,128]{2,1,0:T(8,128)(2,1)S(1)}, bf16[528,256]{1,0:T(8,128)(2,1)S(1)}, bf16[528...) custom-call(f32[1]{0:T(128)S(6)} %tanh.3.refs_0_.gate_ref, ...), custom_call_target="tpu_custom_call" | custom-call | flops 2147483648 | bytes 2097152 | tf_op jit(solution)/shard_map/attention_backward/pallas_call | solution.py:255
  34.9 0.9 %collective-permute-start.11 = (bf16[528,256]{1,0:T(8,128)(2,1)S(1)}, bf16[528,256]{1,0:T(8,128)(2,1)S(1)}, u32[]{:S(2)}, u32[]{:S(2)}) collective-permute-start(bf16[528,256]{1,0:T(8,128)(2,1)S(1)} %get-tuple-element.51), channel_id=1, source_target_pairs={{0,2},{2,0},{4,6},{6,4},{8,10},{10,8},{12,14},{14,12},{16,18},{18,... | collective-permute-start | bytes 811016 | tf_op jit(solution)/shard_map/ppermute | solution.py:344
  35.7 1.5 %collective-permute-start.12 = (bf16[528,256]{1,0:T(8,128)(2,1)S(1)}, bf16[528,256]{1,0:T(8,128)(2,1)S(1)}, u32[]{:S(2)}, u32[]{:S(2)}) collective-permute-start(bf16[528,256]{1,0:T(8,128)(2,1)S(1)} %get-tuple-element.52), channel_id=1, source_target_pairs={{0,4},{2,6},{4,0},{6,2},{8,12},{10,14},{12,8},{14,10},{16,20},{18,... | collective-permute-start | bytes 811016 | tf_op jit(solution)/shard_map/ppermute | solution.py:344
  37.2 1.2 %collective-permute-start.13 = (bf16[528,256]{1,0:T(8,128)(2,1)S(1)}, bf16[528,256]{1,0:T(8,128)(2,1)S(1)}, u32[]{:S(2)}, u32[]{:S(2)}) collective-permute-start(bf16[528,256]{1,0:T(8,128)(2,1)S(1)} %get-tuple-element.53), channel_id=1, source_target_pairs={{0,6},{2,4},{4,2},{6,0},{8,14},{10,12},{12,10},{14,8},{16,22},{18,... | collective-permute-start | bytes 811016 | tf_op jit(solution)/shard_map/ppermute | solution.py:344
  38.4 2.4 %collective-permute-done.9.refs_4_ = bf16[4,128,256]{2,1,0:T(8,128)(2,1)S(1)} collective-permute-done((bf16[4,128,256]{2,1,0:T(8,128)(2,1)S(1)}, bf16[4,128,256]{2,1,0:T(8,128)(2,1)S(1)}, u32[]{:S(2)}, u32[]{:S(2)}) %collective-permute-start.9) | collective-permute-done | bytes 262176 | tf_op jit(solution)/shard_map/ppermute | solution.py:348
  40.9 7.8 %attention_backward.3 = (bf16[2,16,512,128]{3,2,1,0:T(8,128)(2,1)S(1)}, bf16[2,512,128]{2,1,0:T(8,128)(2,1)S(1)}, bf16[528,256]{1,0:T(8,128)(2,1)S(1)}, bf16[528...) custom-call(f32[1]{0:T(128)S(6)} %tanh.3.refs_0_.gate_ref, ...), custom_call_target="tpu_custom_call" | custom-call | flops 2147483648 | bytes 2097152 | tf_op jit(solution)/shard_map/attention_backward/pallas_call | solution.py:255
  48.7 0.1 fusion.20
  48.8 0.1 collective-permute-start.17
  48.9 0.6 collective-permute-start.14
  49.5 1.5 %collective-permute-start.15 = (bf16[528,256]{1,0:T(8,128)(2,1)S(1)}, bf16[528,256]{1,0:T(8,128)(2,1)S(1)}, u32[]{:S(2)}, u32[]{:S(2)}) collective-permute-start(bf16[528,256]{1,0:T(8,128)(2,1)S(1)} %get-tuple-element.55), channel_id=1, source_target_pairs={{0,4},{2,6},{4,0},{6,2},{8,12},{10,14},{12,8},{14,10},{16,20},{18,... | collective-permute-start | bytes 811016 | tf_op jit(solution)/shard_map/ppermute | solution.py:344
  51.0 1.4 %collective-permute-start.16 = (bf16[528,256]{1,0:T(8,128)(2,1)S(1)}, bf16[528,256]{1,0:T(8,128)(2,1)S(1)}, u32[]{:S(2)}, u32[]{:S(2)}) collective-permute-start(bf16[528,256]{1,0:T(8,128)(2,1)S(1)} %get-tuple-element.56), channel_id=1, source_target_pairs={{0,6},{2,4},{4,2},{6,0},{8,14},{10,12},{12,10},{14,8},{16,22},{18,... | collective-permute-start | bytes 811016 | tf_op jit(solution)/shard_map/ppermute | solution.py:344
  52.5 3.1 %collective-permute-start.18 = (bf16[128,256]{1,0:T(8,128)(2,1)S(1)}, bf16[128,256]{1,0:T(8,128)(2,1)S(1)}, u32[]{:S(2)}, u32[]{:S(2)}) collective-permute-start(bf16[128,256]{1,0:T(8,128)(2,1)S(1)} %get-tuple-element.79), channel_id=1, source_target_pairs={{0,16},{2,18},{4,20},{6,22},{8,24},{10,26},{12,28},{14,30},{16,0},... | collective-permute-start | bytes 196616 | tf_op jit(solution)/shard_map/ppermute | solution.py:348
  55.6 1.2 %collective-permute-start.19 = (bf16[128,256]{1,0:T(8,128)(2,1)S(1)}, bf16[128,256]{1,0:T(8,128)(2,1)S(1)}, u32[]{:S(2)}, u32[]{:S(2)}) collective-permute-start(bf16[128,256]{1,0:T(8,128)(2,1)S(1)} %get-tuple-element.80), channel_id=1, source_target_pairs={{0,24},{2,26},{4,28},{6,30},{8,16},{10,18},{12,20},{14,22},{16,8},... | collective-permute-start | bytes 196616 | tf_op jit(solution)/shard_map/ppermute | solution.py:348
  56.8 1.7 %query_gradient.2.rest_0_ = bf16[256,4096]{1,0:T(8,128)(2,1)} custom-call(f32[1]{0:T(128)S(6)} %tanh.3.refs_0_.gate_ref, bf16[2,16,512,128]{3,2,1,0:T(8,128)(2,1)S(1)} %get-tuple-element.59.ds_ref, bf16[2,512,128]{2,1,0:T(8,128)(2,1)S(1)} %get-tuple-element.60.k_ref, bf16[128,256]{1,0:T(8,128)(2,1)S(1)} %collective-permute-done.17.rest_0_), custom_call_target="tpu_custom_call" | custom-call | flops 536870912 | bytes 4194304 | tf_op jit(solution)/shard_map/query_gradient/pallas_call | solution.py:313
  58.5 1.7 %query_gradient.3 = bf16[256,4096]{1,0:T(8,128)(2,1)} custom-call(f32[1]{0:T(128)S(6)} %tanh.3.refs_0_.gate_ref, bf16[2,16,512,128]{3,2,1,0:T(8,128)(2,1)S(1)} %get-tuple-element.57.ds_ref, bf16[2,512,128]{2,1,0:T(8,128)(2,1)S(1)} %get-tuple-element.58.k_ref, bf16[256,4096]{1,0:T(8,128)(2,1)} %query_gradient.2.rest_0_, ...), custom_call_target="tpu_custom_call", output_to_operand_aliasing={{}: (3, {})} | custom-call | flops 536870912 | bytes 4194304 | tf_op jit(solution)/shard_map/query_gradient/pallas_call | solution.py:313
  60.2 0.7 collective-permute-done.15
  60.9 1.6 %collective-permute-done.16 = bf16[528,256]{1,0:T(8,128)(2,1)S(1)} collective-permute-done((bf16[528,256]{1,0:T(8,128)(2,1)S(1)}, bf16[528,256]{1,0:T(8,128)(2,1)S(1)}, u32[]{:S(2)}, u32[]{:S(2)}) %collective-permute-start.16) | collective-permute-done | bytes 270368 | tf_op jit(solution)/shard_map/ppermute | solution.py:344
  62.5 0.2 fusion.18
  62.7 0.1 select_convert_fusion
  62.8 1.9 %collective-permute-start.22 = (bf16[144,256]{1,0:T(8,128)(2,1)S(1)}, bf16[144,256]{1,0:T(8,128)(2,1)S(1)}, u32[]{:S(2)}, u32[]{:S(2)}) collective-permute-start(bf16[144,256]{1,0:T(8,128)(2,1)S(1)} %get-tuple-element.94), channel_id=1, source_target_pairs={{0,24},{2,26},{4,28},{6,30},{8,16},{10,18},{12,20},{14,22},{16,8},... | collective-permute-start | bytes 221192 | tf_op jit(solution)/shard_map/ppermute | solution.py:348
  64.8 1.3 %collective-permute-start.21 = (bf16[144,256]{1,0:T(8,128)(2,1)S(1)}, bf16[144,256]{1,0:T(8,128)(2,1)S(1)}, u32[]{:S(2)}, u32[]{:S(2)}) collective-permute-start(bf16[144,256]{1,0:T(8,128)(2,1)S(1)} %get-tuple-element.93), channel_id=1, source_target_pairs={{0,16},{2,18},{4,20},{6,22},{8,24},{10,26},{12,28},{14,30},{16,0},... | collective-permute-start | bytes 221192 | tf_op jit(solution)/shard_map/ppermute | solution.py:348
  66.1 1.3 %collective-permute-start.20 = (bf16[144,256]{1,0:T(8,128)(2,1)S(1)}, bf16[144,256]{1,0:T(8,128)(2,1)S(1)}, u32[]{:S(2)}, u32[]{:S(2)}) collective-permute-start(bf16[144,256]{1,0:T(8,128)(2,1)S(1)} %get-tuple-element.92), channel_id=1, source_target_pairs={{0,8},{2,10},{4,12},{6,14},{8,0},{10,2},{12,4},{14,6},{16,24},{18,... | collective-permute-start | bytes 221192 | tf_op jit(solution)/shard_map/ppermute | solution.py:348
  67.4 1.7 %collective-permute-done.22 = bf16[144,256]{1,0:T(8,128)(2,1)S(1)} collective-permute-done((bf16[144,256]{1,0:T(8,128)(2,1)S(1)}, bf16[144,256]{1,0:T(8,128)(2,1)S(1)}, u32[]{:S(2)}, u32[]{:S(2)}) %collective-permute-start.22) | collective-permute-done | bytes 73760 | tf_op jit(solution)/shard_map/ppermute | solution.py:348
  69.1 1.9 %collective-permute-done.21 = bf16[144,256]{1,0:T(8,128)(2,1)S(1)} collective-permute-done((bf16[144,256]{1,0:T(8,128)(2,1)S(1)}, bf16[144,256]{1,0:T(8,128)(2,1)S(1)}, u32[]{:S(2)}, u32[]{:S(2)}) %collective-permute-start.21) | collective-permute-done | bytes 73760 | tf_op jit(solution)/shard_map/ppermute | solution.py:348
  71.0 0.1 collective-permute-done.20
  71.1 0.1 collective-permute-start.23
  71.2 0.7 fusion.8
  71.9 0.4 collective-permute-done.23
  72.3 0.5 fusion.15
  (36 shorter events, 0.3 us)
Async XLA Ops:
  1.5 8.2 %collective-permute-start.3 = (bf16[128,256]{1,0:T(8,128)(2,1)S(1)}, bf16[128,256]{1,0:T(8,128)(2,1)S(1)}, u32[]{:S(2)}, u32[]{:S(2)}) collective-permute-start(bf16[128,256]{1,0:T(8,128)(2,1)S(1)} %get-tuple-element.85), channel_id=1, source_target_pairs={{0,2},{2,0},{4,6},{6,4},{8,10},{10,8},{12,14},{14,12},{16,18},{18,... | collective-permute-start | bytes 196616 | tf_op jit(solution)/shard_map/ppermute | solution.py:344
  4.5 8.2 %collective-permute-start = (bf16[128,256]{1,0:T(8,128)(2,1)S(1)}, bf16[128,256]{1,0:T(8,128)(2,1)S(1)}, u32[]{:S(2)}, u32[]{:S(2)}) collective-permute-start(bf16[128,256]{1,0:T(8,128)(2,1)S(1)} %get-tuple-element.91), channel_id=1, source_target_pairs={{0,8},{2,10},{4,12},{6,14},{8,0},{10,2},{12,4},{14,6},{16,24},{18,... | collective-permute-start | bytes 196616 | tf_op jit(solution)/shard_map/ppermute | solution.py:348
  6.1 7.0 %collective-permute-start.1 = (bf16[128,256]{1,0:T(8,128)(2,1)S(1)}, bf16[128,256]{1,0:T(8,128)(2,1)S(1)}, u32[]{:S(2)}, u32[]{:S(2)}) collective-permute-start(bf16[128,256]{1,0:T(8,128)(2,1)S(1)} %get-tuple-element.91), channel_id=1, source_target_pairs={{0,16},{2,18},{4,20},{6,22},{8,24},{10,26},{12,28},{14,30},{16,0},... | collective-permute-start | bytes 196616 | tf_op jit(solution)/shard_map/ppermute | solution.py:348
  8.7 6.1 %collective-permute-start.2 = (bf16[128,256]{1,0:T(8,128)(2,1)S(1)}, bf16[128,256]{1,0:T(8,128)(2,1)S(1)}, u32[]{:S(2)}, u32[]{:S(2)}) collective-permute-start(bf16[128,256]{1,0:T(8,128)(2,1)S(1)} %get-tuple-element.91), channel_id=1, source_target_pairs={{0,24},{2,26},{4,28},{6,30},{8,16},{10,18},{12,20},{14,22},{16,8},... | collective-permute-start | bytes 196616 | tf_op jit(solution)/shard_map/ppermute | solution.py:348
  9.7 5.1 %collective-permute-start.4 = (bf16[2,128,256]{2,1,0:T(8,128)(2,1)S(1)}, bf16[2,128,256]{2,1,0:T(8,128)(2,1)S(1)}, u32[]{:S(2)}, u32[]{:S(2)}) collective-permute-start(bf16[2,128,256]{2,1,0:T(8,128)(2,1)S(1)} %pad_maximum_fusion.2), channel_id=1, source_target_pairs={{0,4},{2,6},{4,0},{6,2},{8,12},{10,14},{12,8},{14,10},{16,20},{18,... | collective-permute-start | bytes 393224 | tf_op jit(solution)/shard_map/ppermute | solution.py:344
  14.9 9.0 %collective-permute-start.5 = (bf16[4,128,256]{2,1,0:T(8,128)(2,1)S(1)}, bf16[4,128,256]{2,1,0:T(8,128)(2,1)S(1)}, u32[]{:S(2)}, u32[]{:S(2)}) collective-permute-start(bf16[4,128,256]{2,1,0:T(8,128)(2,1)S(1)} %pad_maximum_fusion.refs_2_), channel_id=1, source_target_pairs={{0,2},{2,0},{4,6},{6,4},{8,10},{10,8},{12,14},{14,12},{16,18},{18,... | collective-permute-start | bytes 786440 | tf_op jit(solution)/shard_map/ppermute | solution.py:344
  15.5 12.0 %collective-permute-start.6 = (bf16[4,128,256]{2,1,0:T(8,128)(2,1)S(1)}, bf16[4,128,256]{2,1,0:T(8,128)(2,1)S(1)}, u32[]{:S(2)}, u32[]{:S(2)}) collective-permute-start(bf16[4,128,256]{2,1,0:T(8,128)(2,1)S(1)} %pad_maximum_fusion.refs_2_), channel_id=1, source_target_pairs={{0,4},{2,6},{4,0},{6,2},{8,12},{10,14},{12,8},{14,10},{16,20},{18,... | collective-permute-start | bytes 786440 | tf_op jit(solution)/shard_map/ppermute | solution.py:344
  17.0 10.7 %collective-permute-start.7 = (bf16[4,128,256]{2,1,0:T(8,128)(2,1)S(1)}, bf16[4,128,256]{2,1,0:T(8,128)(2,1)S(1)}, u32[]{:S(2)}, u32[]{:S(2)}) collective-permute-start(bf16[4,128,256]{2,1,0:T(8,128)(2,1)S(1)} %pad_maximum_fusion.refs_2_), channel_id=1, source_target_pairs={{0,6},{2,4},{4,2},{6,0},{8,14},{10,12},{12,10},{14,8},{16,22},{18,... | collective-permute-start | bytes 786440 | tf_op jit(solution)/shard_map/ppermute | solution.py:344
  18.4 18.8 %collective-permute-start.10 = (bf16[4,128,256]{2,1,0:T(8,128)(2,1)S(1)}, bf16[4,128,256]{2,1,0:T(8,128)(2,1)S(1)}, u32[]{:S(2)}, u32[]{:S(2)}) collective-permute-start(bf16[4,128,256]{2,1,0:T(8,128)(2,1)S(1)} %pad_maximum_fusion.1.refs_2_), channel_id=1, source_target_pairs={{0,24},{2,26},{4,28},{6,30},{8,16},{10,18},{12,20},{14,22},{16,8},... | collective-permute-start | bytes 786440 | tf_op jit(solution)/shard_map/ppermute | solution.py:348
  21.9 18.9 %collective-permute-start.9 = (bf16[4,128,256]{2,1,0:T(8,128)(2,1)S(1)}, bf16[4,128,256]{2,1,0:T(8,128)(2,1)S(1)}, u32[]{:S(2)}, u32[]{:S(2)}) collective-permute-start(bf16[4,128,256]{2,1,0:T(8,128)(2,1)S(1)} %pad_maximum_fusion.1.refs_2_), channel_id=1, source_target_pairs={{0,16},{2,18},{4,20},{6,22},{8,24},{10,26},{12,28},{14,30},{16,0},... | collective-permute-start | bytes 786440 | tf_op jit(solution)/shard_map/ppermute | solution.py:348
  23.9 17.0 %collective-permute-start.8 = (bf16[4,128,256]{2,1,0:T(8,128)(2,1)S(1)}, bf16[4,128,256]{2,1,0:T(8,128)(2,1)S(1)}, u32[]{:S(2)}, u32[]{:S(2)}) collective-permute-start(bf16[4,128,256]{2,1,0:T(8,128)(2,1)S(1)} %pad_maximum_fusion.1.refs_2_), channel_id=1, source_target_pairs={{0,8},{2,10},{4,12},{6,14},{8,0},{10,2},{12,4},{14,6},{16,24},{18,... | collective-permute-start | bytes 786440 | tf_op jit(solution)/shard_map/ppermute | solution.py:348
  34.9 13.8 %collective-permute-start.11 = (bf16[528,256]{1,0:T(8,128)(2,1)S(1)}, bf16[528,256]{1,0:T(8,128)(2,1)S(1)}, u32[]{:S(2)}, u32[]{:S(2)}) collective-permute-start(bf16[528,256]{1,0:T(8,128)(2,1)S(1)} %get-tuple-element.51), channel_id=1, source_target_pairs={{0,2},{2,0},{4,6},{6,4},{8,10},{10,8},{12,14},{14,12},{16,18},{18,... | collective-permute-start | bytes 811016 | tf_op jit(solution)/shard_map/ppermute | solution.py:344
  35.7 12.9 %collective-permute-start.12 = (bf16[528,256]{1,0:T(8,128)(2,1)S(1)}, bf16[528,256]{1,0:T(8,128)(2,1)S(1)}, u32[]{:S(2)}, u32[]{:S(2)}) collective-permute-start(bf16[528,256]{1,0:T(8,128)(2,1)S(1)} %get-tuple-element.52), channel_id=1, source_target_pairs={{0,4},{2,6},{4,0},{6,2},{8,12},{10,14},{12,8},{14,10},{16,20},{18,... | collective-permute-start | bytes 811016 | tf_op jit(solution)/shard_map/ppermute | solution.py:344
  37.2 11.4 %collective-permute-start.13 = (bf16[528,256]{1,0:T(8,128)(2,1)S(1)}, bf16[528,256]{1,0:T(8,128)(2,1)S(1)}, u32[]{:S(2)}, u32[]{:S(2)}) collective-permute-start(bf16[528,256]{1,0:T(8,128)(2,1)S(1)} %get-tuple-element.53), channel_id=1, source_target_pairs={{0,6},{2,4},{4,2},{6,0},{8,14},{10,12},{12,10},{14,8},{16,22},{18,... | collective-permute-start | bytes 811016 | tf_op jit(solution)/shard_map/ppermute | solution.py:344
  48.8 6.8 %collective-permute-start.17 = (bf16[128,256]{1,0:T(8,128)(2,1)S(1)}, bf16[128,256]{1,0:T(8,128)(2,1)S(1)}, u32[]{:S(2)}, u32[]{:S(2)}) collective-permute-start(bf16[128,256]{1,0:T(8,128)(2,1)S(1)} %get-tuple-element.81), channel_id=1, source_target_pairs={{0,8},{2,10},{4,12},{6,14},{8,0},{10,2},{12,4},{14,6},{16,24},{18,... | collective-permute-start | bytes 196616 | tf_op jit(solution)/shard_map/ppermute | solution.py:348
  48.9 9.6 %collective-permute-start.14 = (bf16[528,256]{1,0:T(8,128)(2,1)S(1)}, bf16[528,256]{1,0:T(8,128)(2,1)S(1)}, u32[]{:S(2)}, u32[]{:S(2)}) collective-permute-start(bf16[528,256]{1,0:T(8,128)(2,1)S(1)} %get-tuple-element.54), channel_id=1, source_target_pairs={{0,2},{2,0},{4,6},{6,4},{8,10},{10,8},{12,14},{14,12},{16,18},{18,... | collective-permute-start | bytes 811016 | tf_op jit(solution)/shard_map/ppermute | solution.py:344
  49.5 11.4 %collective-permute-start.15 = (bf16[528,256]{1,0:T(8,128)(2,1)S(1)}, bf16[528,256]{1,0:T(8,128)(2,1)S(1)}, u32[]{:S(2)}, u32[]{:S(2)}) collective-permute-start(bf16[528,256]{1,0:T(8,128)(2,1)S(1)} %get-tuple-element.55), channel_id=1, source_target_pairs={{0,4},{2,6},{4,0},{6,2},{8,12},{10,14},{12,8},{14,10},{16,20},{18,... | collective-permute-start | bytes 811016 | tf_op jit(solution)/shard_map/ppermute | solution.py:344
  51.0 11.5 %collective-permute-start.16 = (bf16[528,256]{1,0:T(8,128)(2,1)S(1)}, bf16[528,256]{1,0:T(8,128)(2,1)S(1)}, u32[]{:S(2)}, u32[]{:S(2)}) collective-permute-start(bf16[528,256]{1,0:T(8,128)(2,1)S(1)} %get-tuple-element.56), channel_id=1, source_target_pairs={{0,6},{2,4},{4,2},{6,0},{8,14},{10,12},{12,10},{14,8},{16,22},{18,... | collective-permute-start | bytes 811016 | tf_op jit(solution)/shard_map/ppermute | solution.py:344
  52.5 12.3 %collective-permute-start.18 = (bf16[128,256]{1,0:T(8,128)(2,1)S(1)}, bf16[128,256]{1,0:T(8,128)(2,1)S(1)}, u32[]{:S(2)}, u32[]{:S(2)}) collective-permute-start(bf16[128,256]{1,0:T(8,128)(2,1)S(1)} %get-tuple-element.79), channel_id=1, source_target_pairs={{0,16},{2,18},{4,20},{6,22},{8,24},{10,26},{12,28},{14,30},{16,0},... | collective-permute-start | bytes 196616 | tf_op jit(solution)/shard_map/ppermute | solution.py:348
  55.6 9.2 %collective-permute-start.19 = (bf16[128,256]{1,0:T(8,128)(2,1)S(1)}, bf16[128,256]{1,0:T(8,128)(2,1)S(1)}, u32[]{:S(2)}, u32[]{:S(2)}) collective-permute-start(bf16[128,256]{1,0:T(8,128)(2,1)S(1)} %get-tuple-element.80), channel_id=1, source_target_pairs={{0,24},{2,26},{4,28},{6,30},{8,16},{10,18},{12,20},{14,22},{16,8},... | collective-permute-start | bytes 196616 | tf_op jit(solution)/shard_map/ppermute | solution.py:348
  62.8 6.3 %collective-permute-start.22 = (bf16[144,256]{1,0:T(8,128)(2,1)S(1)}, bf16[144,256]{1,0:T(8,128)(2,1)S(1)}, u32[]{:S(2)}, u32[]{:S(2)}) collective-permute-start(bf16[144,256]{1,0:T(8,128)(2,1)S(1)} %get-tuple-element.94), channel_id=1, source_target_pairs={{0,24},{2,26},{4,28},{6,30},{8,16},{10,18},{12,20},{14,22},{16,8},... | collective-permute-start | bytes 221192 | tf_op jit(solution)/shard_map/ppermute | solution.py:348
  64.8 6.2 %collective-permute-start.21 = (bf16[144,256]{1,0:T(8,128)(2,1)S(1)}, bf16[144,256]{1,0:T(8,128)(2,1)S(1)}, u32[]{:S(2)}, u32[]{:S(2)}) collective-permute-start(bf16[144,256]{1,0:T(8,128)(2,1)S(1)} %get-tuple-element.93), channel_id=1, source_target_pairs={{0,16},{2,18},{4,20},{6,22},{8,24},{10,26},{12,28},{14,30},{16,0},... | collective-permute-start | bytes 221192 | tf_op jit(solution)/shard_map/ppermute | solution.py:348
  66.1 4.9 %collective-permute-start.20 = (bf16[144,256]{1,0:T(8,128)(2,1)S(1)}, bf16[144,256]{1,0:T(8,128)(2,1)S(1)}, u32[]{:S(2)}, u32[]{:S(2)}) collective-permute-start(bf16[144,256]{1,0:T(8,128)(2,1)S(1)} %get-tuple-element.92), channel_id=1, source_target_pairs={{0,8},{2,10},{4,12},{6,14},{8,0},{10,2},{12,4},{14,6},{16,24},{18,... | collective-permute-start | bytes 221192 | tf_op jit(solution)/shard_map/ppermute | solution.py:348
  71.1 1.2 %collective-permute-start.23 = (f32[1,256]{1,0:T(1,128)S(1)}, f32[1,256]{1,0:T(1,128)S(1)}, u32[]{:S(2)}, u32[]{:S(2)}) collective-permute-start(f32[1,256]{1,0:T(1,128)S(1)} %fusion.9), channel_id=1, source_target_pairs={{0,1},{1,0},{2,3},{3,2},{4,5},{5,4},{6,7},{7,6},{8,9},{9,8},{10,11... | collective-permute-start | bytes 3080 | tf_op jit(solution)/shard_map/ppermute | solution.py:424

commit v7 on v6

--- a/solution.py
+++ b/solution.py
@@ -203,13 +203,13 @@
     for at in range(items + 3):
         scores = score_product(at) if at < items else None
         values = value_product(at - 1) if 0 < at <= items else None
-        prob = probabilities(at - 1, ready) if ready is not None else None
-        middle = (at - 2, *score_gradient(at - 2, *waiting)) if waiting is not None else None
         if len(held) == MERGE:
             gradients(held)
             if (held[-1][0] + 1) % per_head == 0:
                 gate_row += finish(held[-1][0] // per_head)
             held = []
+        prob = probabilities(at - 1, ready) if ready is not None else None
+        middle = (at - 2, *score_gradient(at - 2, *waiting)) if waiting is not None else None
         if middle is not None:
             held.append(middle)
         waiting = (prob, values) if prob is not None else None

time: 73 us -> 73 us (level)
  no operation moved by 1% of the time
where the time goes in v7:
time: 73 us; the launch traced here: 72.8 us
  starting transfers between devices  32.4 us (44%)
  Pallas kernels  21.8 us (30%)
  waiting for transfers between devices  13 us (18%)
  other arithmetic  2.53 us (3%)
  local copies, waits for them, and re-layouts  1.61 us (2%)
  between operations  1.52 us (2%)
    ppermute x12, starting transfers between devices, swap_z(): return lax.ppermute(value, 'ctx', pairs)  17.1 us
    ppermute x11, starting transfers between devices, swap(): return lax.ppermute(value, 'ctx', [(i, i ^ bit) for i in range(n_ctx)])  15.2 us
    pallas_call x2, Pallas kernels, attention(): pl.pallas_call(kernel, in_specs=in_specs, out_specs=[vmem] * len(out_shap...  14.9 us
    ppermute x12, waiting for transfers between devices, swap_z(): return lax.ppermute(value, 'ctx', pairs)  8.18 us
    ppermute x11, waiting for transfers between devices, swap(): return lax.ppermute(value, 'ctx', [(i, i ^ bit) for i in range(n_ctx)])  4.39 us
    pallas_call x2, Pallas kernels, query_gradient(): pl.pallas_call(functools.partial(query_kernel, at * heads, n_blocks, len(...  3.43 us
    pallas_call x1, Pallas kernels, prepare(): pl.pallas_call(functools.partial(prepare_kernel, n, n_blocks, n_images, 2...  3.38 us
  transfers between devices with their start and end apart: 24, of which 11 were waited for; matrix products, arithmetic and copies ran while one was open for 4% of the time, Pallas kernels for 30%

profile of v7, /device:TPU:0, one launch (start us, length us, event | category | flops | bytes accessed | tf_op | source)
XLA Modules:
  0.0 72.8 jit_solution(7693329752446409203)
XLA Ops:
  0.6 0.8 %slice_bitcast_fusion = (bf16[64,256]{1,0:T(8,128)(2,1)S(1)}, bf16[64,256]{1,0:T(8,128)(2,1)S(1)}, bf16[64,256]{1,0:T(8,128)(2,1)S(1)}, bf16[64,256]{1,0:T(8,128)(2,1)S(1)}) fusion(bf16[1,64,512]{2,1,0:T(8,128)(2,1)} %param.10, bf16[1,64,512]{2,1,0:T(8,128)(2,1)} %param.9), kind=kLoop, calls=%fused_computation.24 | loop fusion | bytes 262144 | tf_op jit(solution)/shard_map/squeeze | solution.py:352
  1.5 3.0 %collective-permute-start.3 = (bf16[128,256]{1,0:T(8,128)(2,1)S(1)}, bf16[128,256]{1,0:T(8,128)(2,1)S(1)}, u32[]{:S(2)}, u32[]{:S(2)}) collective-permute-start(bf16[128,256]{1,0:T(8,128)(2,1)S(1)} %get-tuple-element.85), channel_id=1, source_target_pairs={{0,2},{2,0},{4,6},{6,4},{8,10},{10,8},{12,14},{14,12},{16,18},{18,... | collective-permute-start | bytes 196616 | tf_op jit(solution)/shard_map/ppermute | solution.py:344
  4.5 1.6 %collective-permute-start = (bf16[128,256]{1,0:T(8,128)(2,1)S(1)}, bf16[128,256]{1,0:T(8,128)(2,1)S(1)}, u32[]{:S(2)}, u32[]{:S(2)}) collective-permute-start(bf16[128,256]{1,0:T(8,128)(2,1)S(1)} %get-tuple-element.91), channel_id=1, source_target_pairs={{0,8},{2,10},{4,12},{6,14},{8,0},{10,2},{12,4},{14,6},{16,24},{18,... | collective-permute-start | bytes 196616 | tf_op jit(solution)/shard_map/ppermute | solution.py:348
  6.1 2.6 %collective-permute-start.1 = (bf16[128,256]{1,0:T(8,128)(2,1)S(1)}, bf16[128,256]{1,0:T(8,128)(2,1)S(1)}, u32[]{:S(2)}, u32[]{:S(2)}) collective-permute-start(bf16[128,256]{1,0:T(8,128)(2,1)S(1)} %get-tuple-element.91), channel_id=1, source_target_pairs={{0,16},{2,18},{4,20},{6,22},{8,24},{10,26},{12,28},{14,30},{16,0},... | collective-permute-start | bytes 196616 | tf_op jit(solution)/shard_map/ppermute | solution.py:348
  8.7 0.2 collective-permute-start.2
  8.9 0.8 %reshape.39 = s32[32]{0:T(128)S(1)} reshape(s32[2,16]{1,0:T(2,128)} %param.12) | data formatting | bytes 256 | tf_op jit(solution)/shard_map/reshape | solution.py:340
  9.7 0.0 collective-permute-done.3
  9.7 1.6 %collective-permute-start.4 = (bf16[2,128,256]{2,1,0:T(8,128)(2,1)S(1)}, bf16[2,128,256]{2,1,0:T(8,128)(2,1)S(1)}, u32[]{:S(2)}, u32[]{:S(2)}) collective-permute-start(bf16[2,128,256]{2,1,0:T(8,128)(2,1)S(1)} %pad_maximum_fusion.2), channel_id=1, source_target_pairs={{0,4},{2,6},{4,0},{6,2},{8,12},{10,14},{12,8},{14,10},{16,20},{18,... | collective-permute-start | bytes 393224 | tf_op jit(solution)/shard_map/ppermute | solution.py:344
  11.3 0.7 %pad_add_fusion.refs_0_ = s32[49]{0:T(128)S(1)} fusion(s32[1]{0:T(128)} %bitcast, s32[16]{0:T(128)} %param.13, s32[32]{0:T(128)S(1)} %reshape.39), kind=kLoop, calls=%fused_computation.58 | loop fusion | flops 98 | bytes 392 | tf_op jit(solution)/shard_map/concatenate | solution.py:340
  12.7 0.4 collective-permute-done.1
  13.1 1.7 %collective-permute-done.2 = bf16[128,256]{1,0:T(8,128)(2,1)S(1)} collective-permute-done((bf16[128,256]{1,0:T(8,128)(2,1)S(1)}, bf16[128,256]{1,0:T(8,128)(2,1)S(1)}, u32[]{:S(2)}, u32[]{:S(2)}) %collective-permute-start.2) | collective-permute-done | bytes 65568 | tf_op jit(solution)/shard_map/ppermute | solution.py:348
  14.9 0.6 collective-permute-start.5
  15.5 1.5 %collective-permute-start.6 = (bf16[4,128,256]{2,1,0:T(8,128)(2,1)S(1)}, bf16[4,128,256]{2,1,0:T(8,128)(2,1)S(1)}, u32[]{:S(2)}, u32[]{:S(2)}) collective-permute-start(bf16[4,128,256]{2,1,0:T(8,128)(2,1)S(1)} %pad_maximum_fusion.refs_2_), channel_id=1, source_target_pairs={{0,4},{2,6},{4,0},{6,2},{8,12},{10,14},{12,8},{14,10},{16,20},{18,... | collective-permute-start | bytes 786440 | tf_op jit(solution)/shard_map/ppermute | solution.py:344
  17.0 1.4 %collective-permute-start.7 = (bf16[4,128,256]{2,1,0:T(8,128)(2,1)S(1)}, bf16[4,128,256]{2,1,0:T(8,128)(2,1)S(1)}, u32[]{:S(2)}, u32[]{:S(2)}) collective-permute-start(bf16[4,128,256]{2,1,0:T(8,128)(2,1)S(1)} %pad_maximum_fusion.refs_2_), channel_id=1, source_target_pairs={{0,6},{2,4},{4,2},{6,0},{8,14},{10,12},{12,10},{14,8},{16,22},{18,... | collective-permute-start | bytes 786440 | tf_op jit(solution)/shard_map/ppermute | solution.py:344
  18.4 3.5 %collective-permute-start.10 = (bf16[4,128,256]{2,1,0:T(8,128)(2,1)S(1)}, bf16[4,128,256]{2,1,0:T(8,128)(2,1)S(1)}, u32[]{:S(2)}, u32[]{:S(2)}) collective-permute-start(bf16[4,128,256]{2,1,0:T(8,128)(2,1)S(1)} %pad_maximum_fusion.1.refs_2_), channel_id=1, source_target_pairs={{0,24},{2,26},{4,28},{6,30},{8,16},{10,18},{12,20},{14,22},{16,8},... | collective-permute-start | bytes 786440 | tf_op jit(solution)/shard_map/ppermute | solution.py:348
  22.0 1.9 %collective-permute-done.5.refs_3_ = bf16[4,128,256]{2,1,0:T(8,128)(2,1)S(1)} collective-permute-done((bf16[4,128,256]{2,1,0:T(8,128)(2,1)S(1)}, bf16[4,128,256]{2,1,0:T(8,128)(2,1)S(1)}, u32[]{:S(2)}, u32[]{:S(2)}) %collective-permute-start.5) | collective-permute-done | bytes 262176 | tf_op jit(solution)/shard_map/ppermute | solution.py:344
  23.9 0.2 collective-permute-start.8
  24.1 3.4 %prepare.1 = (s32[3,8]{1,0:T(4,128)S(1)}, f32[2,8]{1,0:T(2,128)S(1)}, bf16[256,4096]{1,0:T(8,128)(2,1)S(1)}, bf16[256,4096]{1,0:T(8,128)(2,1)S(1)}) custom-call(s32[49]{0:T(128)S(1)} %pad_add_fusion.refs_0_, bf16[256,4096]{1,0:T(8,128)(2,1)} %refs_1_.1, bf16[256,4096]{1,0:T(8,128)(2,1)} %refs_2_.1, bf16[4,128,256]{2,1,0:T(8,128)(2,1)S(1)} %collective-permute-done.5.refs_3_), custom_call_target="tpu_custom_call" | custom-call | bytes 8388608 | tf_op jit(solution)/shard_map/prepare/pallas_call | solution.py:95
  27.5 0.1 collective-permute-done.7.refs_5_
  27.7 7.2 %attention_backward.2 = (bf16[2,16,512,128]{3,2,1,0:T(8,128)(2,1)S(1)}, bf16[2,512,128]{2,1,0:T(8,128)(2,1)S(1)}, bf16[528,256]{1,0:T(8,128)(2,1)S(1)}, bf16[528...) custom-call(f32[1]{0:T(128)S(6)} %tanh.3.refs_0_.gate_ref, ...), custom_call_target="tpu_custom_call" | custom-call | flops 2147483648 | bytes 2097152 | tf_op jit(solution)/shard_map/attention_backward/pallas_call | solution.py:255
  34.8 0.9 %collective-permute-start.11 = (bf16[528,256]{1,0:T(8,128)(2,1)S(1)}, bf16[528,256]{1,0:T(8,128)(2,1)S(1)}, u32[]{:S(2)}, u32[]{:S(2)}) collective-permute-start(bf16[528,256]{1,0:T(8,128)(2,1)S(1)} %get-tuple-element.51), channel_id=1, source_target_pairs={{0,2},{2,0},{4,6},{6,4},{8,10},{10,8},{12,14},{14,12},{16,18},{18,... | collective-permute-start | bytes 811016 | tf_op jit(solution)/shard_map/ppermute | solution.py:344
  35.7 1.5 %collective-permute-start.12 = (bf16[528,256]{1,0:T(8,128)(2,1)S(1)}, bf16[528,256]{1,0:T(8,128)(2,1)S(1)}, u32[]{:S(2)}, u32[]{:S(2)}) collective-permute-start(bf16[528,256]{1,0:T(8,128)(2,1)S(1)} %get-tuple-element.52), channel_id=1, source_target_pairs={{0,4},{2,6},{4,0},{6,2},{8,12},{10,14},{12,8},{14,10},{16,20},{18,... | collective-permute-start | bytes 811016 | tf_op jit(solution)/shard_map/ppermute | solution.py:344
  37.2 1.2 %collective-permute-start.13 = (bf16[528,256]{1,0:T(8,128)(2,1)S(1)}, bf16[528,256]{1,0:T(8,128)(2,1)S(1)}, u32[]{:S(2)}, u32[]{:S(2)}) collective-permute-start(bf16[528,256]{1,0:T(8,128)(2,1)S(1)} %get-tuple-element.53), channel_id=1, source_target_pairs={{0,6},{2,4},{4,2},{6,0},{8,14},{10,12},{12,10},{14,8},{16,22},{18,... | collective-permute-start | bytes 811016 | tf_op jit(solution)/shard_map/ppermute | solution.py:344
  38.4 2.5 %collective-permute-done.9.refs_4_ = bf16[4,128,256]{2,1,0:T(8,128)(2,1)S(1)} collective-permute-done((bf16[4,128,256]{2,1,0:T(8,128)(2,1)S(1)}, bf16[4,128,256]{2,1,0:T(8,128)(2,1)S(1)}, u32[]{:S(2)}, u32[]{:S(2)}) %collective-permute-start.9) | collective-permute-done | bytes 262176 | tf_op jit(solution)/shard_map/ppermute | solution.py:348
  40.9 7.8 %attention_backward.3 = (bf16[2,16,512,128]{3,2,1,0:T(8,128)(2,1)S(1)}, bf16[2,512,128]{2,1,0:T(8,128)(2,1)S(1)}, bf16[528,256]{1,0:T(8,128)(2,1)S(1)}, bf16[528...) custom-call(f32[1]{0:T(128)S(6)} %tanh.3.refs_0_.gate_ref, ...), custom_call_target="tpu_custom_call" | custom-call | flops 2147483648 | bytes 2097152 | tf_op jit(solution)/shard_map/attention_backward/pallas_call | solution.py:255
  48.7 0.1 fusion.20
  48.8 0.1 collective-permute-start.17
  48.9 0.6 collective-permute-start.14
  49.5 1.5 %collective-permute-start.15 = (bf16[528,256]{1,0:T(8,128)(2,1)S(1)}, bf16[528,256]{1,0:T(8,128)(2,1)S(1)}, u32[]{:S(2)}, u32[]{:S(2)}) collective-permute-start(bf16[528,256]{1,0:T(8,128)(2,1)S(1)} %get-tuple-element.55), channel_id=1, source_target_pairs={{0,4},{2,6},{4,0},{6,2},{8,12},{10,14},{12,8},{14,10},{16,20},{18,... | collective-permute-start | bytes 811016 | tf_op jit(solution)/shard_map/ppermute | solution.py:344
  51.0 1.4 %collective-permute-start.16 = (bf16[528,256]{1,0:T(8,128)(2,1)S(1)}, bf16[528,256]{1,0:T(8,128)(2,1)S(1)}, u32[]{:S(2)}, u32[]{:S(2)}) collective-permute-start(bf16[528,256]{1,0:T(8,128)(2,1)S(1)} %get-tuple-element.56), channel_id=1, source_target_pairs={{0,6},{2,4},{4,2},{6,0},{8,14},{10,12},{12,10},{14,8},{16,22},{18,... | collective-permute-start | bytes 811016 | tf_op jit(solution)/shard_map/ppermute | solution.py:344
  52.5 3.1 %collective-permute-start.18 = (bf16[128,256]{1,0:T(8,128)(2,1)S(1)}, bf16[128,256]{1,0:T(8,128)(2,1)S(1)}, u32[]{:S(2)}, u32[]{:S(2)}) collective-permute-start(bf16[128,256]{1,0:T(8,128)(2,1)S(1)} %get-tuple-element.79), channel_id=1, source_target_pairs={{0,16},{2,18},{4,20},{6,22},{8,24},{10,26},{12,28},{14,30},{16,0},... | collective-permute-start | bytes 196616 | tf_op jit(solution)/shard_map/ppermute | solution.py:348
  55.6 1.2 %collective-permute-start.19 = (bf16[128,256]{1,0:T(8,128)(2,1)S(1)}, bf16[128,256]{1,0:T(8,128)(2,1)S(1)}, u32[]{:S(2)}, u32[]{:S(2)}) collective-permute-start(bf16[128,256]{1,0:T(8,128)(2,1)S(1)} %get-tuple-element.80), channel_id=1, source_target_pairs={{0,24},{2,26},{4,28},{6,30},{8,16},{10,18},{12,20},{14,22},{16,8},... | collective-permute-start | bytes 196616 | tf_op jit(solution)/shard_map/ppermute | solution.py:348
  56.8 1.7 %query_gradient.2.rest_0_ = bf16[256,4096]{1,0:T(8,128)(2,1)} custom-call(f32[1]{0:T(128)S(6)} %tanh.3.refs_0_.gate_ref, bf16[2,16,512,128]{3,2,1,0:T(8,128)(2,1)S(1)} %get-tuple-element.59.ds_ref, bf16[2,512,128]{2,1,0:T(8,128)(2,1)S(1)} %get-tuple-element.60.k_ref, bf16[128,256]{1,0:T(8,128)(2,1)S(1)} %collective-permute-done.17.rest_0_), custom_call_target="tpu_custom_call" | custom-call | flops 536870912 | bytes 4194304 | tf_op jit(solution)/shard_map/query_gradient/pallas_call | solution.py:313
  58.5 1.7 %query_gradient.3 = bf16[256,4096]{1,0:T(8,128)(2,1)} custom-call(f32[1]{0:T(128)S(6)} %tanh.3.refs_0_.gate_ref, bf16[2,16,512,128]{3,2,1,0:T(8,128)(2,1)S(1)} %get-tuple-element.57.ds_ref, bf16[2,512,128]{2,1,0:T(8,128)(2,1)S(1)} %get-tuple-element.58.k_ref, bf16[256,4096]{1,0:T(8,128)(2,1)} %query_gradient.2.rest_0_, ...), custom_call_target="tpu_custom_call", output_to_operand_aliasing={{}: (3, {})} | custom-call | flops 536870912 | bytes 4194304 | tf_op jit(solution)/shard_map/query_gradient/pallas_call | solution.py:313
  60.2 0.7 collective-permute-done.15
  60.9 1.6 %collective-permute-done.16 = bf16[528,256]{1,0:T(8,128)(2,1)S(1)} collective-permute-done((bf16[528,256]{1,0:T(8,128)(2,1)S(1)}, bf16[528,256]{1,0:T(8,128)(2,1)S(1)}, u32[]{:S(2)}, u32[]{:S(2)}) %collective-permute-start.16) | collective-permute-done | bytes 270368 | tf_op jit(solution)/shard_map/ppermute | solution.py:344
  62.5 0.2 fusion.18
  62.7 0.1 select_convert_fusion
  62.8 1.9 %collective-permute-start.22 = (bf16[144,256]{1,0:T(8,128)(2,1)S(1)}, bf16[144,256]{1,0:T(8,128)(2,1)S(1)}, u32[]{:S(2)}, u32[]{:S(2)}) collective-permute-start(bf16[144,256]{1,0:T(8,128)(2,1)S(1)} %get-tuple-element.94), channel_id=1, source_target_pairs={{0,24},{2,26},{4,28},{6,30},{8,16},{10,18},{12,20},{14,22},{16,8},... | collective-permute-start | bytes 221192 | tf_op jit(solution)/shard_map/ppermute | solution.py:348
  64.8 1.3 %collective-permute-start.21 = (bf16[144,256]{1,0:T(8,128)(2,1)S(1)}, bf16[144,256]{1,0:T(8,128)(2,1)S(1)}, u32[]{:S(2)}, u32[]{:S(2)}) collective-permute-start(bf16[144,256]{1,0:T(8,128)(2,1)S(1)} %get-tuple-element.93), channel_id=1, source_target_pairs={{0,16},{2,18},{4,20},{6,22},{8,24},{10,26},{12,28},{14,30},{16,0},... | collective-permute-start | bytes 221192 | tf_op jit(solution)/shard_map/ppermute | solution.py:348
  66.1 1.3 %collective-permute-start.20 = (bf16[144,256]{1,0:T(8,128)(2,1)S(1)}, bf16[144,256]{1,0:T(8,128)(2,1)S(1)}, u32[]{:S(2)}, u32[]{:S(2)}) collective-permute-start(bf16[144,256]{1,0:T(8,128)(2,1)S(1)} %get-tuple-element.92), channel_id=1, source_target_pairs={{0,8},{2,10},{4,12},{6,14},{8,0},{10,2},{12,4},{14,6},{16,24},{18,... | collective-permute-start | bytes 221192 | tf_op jit(solution)/shard_map/ppermute | solution.py:348
  67.4 1.7 %collective-permute-done.22 = bf16[144,256]{1,0:T(8,128)(2,1)S(1)} collective-permute-done((bf16[144,256]{1,0:T(8,128)(2,1)S(1)}, bf16[144,256]{1,0:T(8,128)(2,1)S(1)}, u32[]{:S(2)}, u32[]{:S(2)}) %collective-permute-start.22) | collective-permute-done | bytes 73760 | tf_op jit(solution)/shard_map/ppermute | solution.py:348
  69.1 1.9 %collective-permute-done.21 = bf16[144,256]{1,0:T(8,128)(2,1)S(1)} collective-permute-done((bf16[144,256]{1,0:T(8,128)(2,1)S(1)}, bf16[144,256]{1,0:T(8,128)(2,1)S(1)}, u32[]{:S(2)}, u32[]{:S(2)}) %collective-permute-start.21) | collective-permute-done | bytes 73760 | tf_op jit(solution)/shard_map/ppermute | solution.py:348
  71.0 0.1 collective-permute-done.20
  71.1 0.1 collective-permute-start.23
  71.2 0.7 fusion.8
  71.9 0.4 collective-permute-done.23
  72.3 0.5 fusion.15
  (36 shorter events, 0.3 us)
Async XLA Ops:
  1.5 8.2 %collective-permute-start.3 = (bf16[128,256]{1,0:T(8,128)(2,1)S(1)}, bf16[128,256]{1,0:T(8,128)(2,1)S(1)}, u32[]{:S(2)}, u32[]{:S(2)}) collective-permute-start(bf16[128,256]{1,0:T(8,128)(2,1)S(1)} %get-tuple-element.85), channel_id=1, source_target_pairs={{0,2},{2,0},{4,6},{6,4},{8,10},{10,8},{12,14},{14,12},{16,18},{18,... | collective-permute-start | bytes 196616 | tf_op jit(solution)/shard_map/ppermute | solution.py:344
  4.5 8.2 %collective-permute-start = (bf16[128,256]{1,0:T(8,128)(2,1)S(1)}, bf16[128,256]{1,0:T(8,128)(2,1)S(1)}, u32[]{:S(2)}, u32[]{:S(2)}) collective-permute-start(bf16[128,256]{1,0:T(8,128)(2,1)S(1)} %get-tuple-element.91), channel_id=1, source_target_pairs={{0,8},{2,10},{4,12},{6,14},{8,0},{10,2},{12,4},{14,6},{16,24},{18,... | collective-permute-start | bytes 196616 | tf_op jit(solution)/shard_map/ppermute | solution.py:348
  6.1 7.0 %collective-permute-start.1 = (bf16[128,256]{1,0:T(8,128)(2,1)S(1)}, bf16[128,256]{1,0:T(8,128)(2,1)S(1)}, u32[]{:S(2)}, u32[]{:S(2)}) collective-permute-start(bf16[128,256]{1,0:T(8,128)(2,1)S(1)} %get-tuple-element.91), channel_id=1, source_target_pairs={{0,16},{2,18},{4,20},{6,22},{8,24},{10,26},{12,28},{14,30},{16,0},... | collective-permute-start | bytes 196616 | tf_op jit(solution)/shard_map/ppermute | solution.py:348
  8.7 6.1 %collective-permute-start.2 = (bf16[128,256]{1,0:T(8,128)(2,1)S(1)}, bf16[128,256]{1,0:T(8,128)(2,1)S(1)}, u32[]{:S(2)}, u32[]{:S(2)}) collective-permute-start(bf16[128,256]{1,0:T(8,128)(2,1)S(1)} %get-tuple-element.91), channel_id=1, source_target_pairs={{0,24},{2,26},{4,28},{6,30},{8,16},{10,18},{12,20},{14,22},{16,8},... | collective-permute-start | bytes 196616 | tf_op jit(solution)/shard_map/ppermute | solution.py:348
  9.7 5.1 %collective-permute-start.4 = (bf16[2,128,256]{2,1,0:T(8,128)(2,1)S(1)}, bf16[2,128,256]{2,1,0:T(8,128)(2,1)S(1)}, u32[]{:S(2)}, u32[]{:S(2)}) collective-permute-start(bf16[2,128,256]{2,1,0:T(8,128)(2,1)S(1)} %pad_maximum_fusion.2), channel_id=1, source_target_pairs={{0,4},{2,6},{4,0},{6,2},{8,12},{10,14},{12,8},{14,10},{16,20},{18,... | collective-permute-start | bytes 393224 | tf_op jit(solution)/shard_map/ppermute | solution.py:344
  14.9 9.0 %collective-permute-start.5 = (bf16[4,128,256]{2,1,0:T(8,128)(2,1)S(1)}, bf16[4,128,256]{2,1,0:T(8,128)(2,1)S(1)}, u32[]{:S(2)}, u32[]{:S(2)}) collective-permute-start(bf16[4,128,256]{2,1,0:T(8,128)(2,1)S(1)} %pad_maximum_fusion.refs_2_), channel_id=1, source_target_pairs={{0,2},{2,0},{4,6},{6,4},{8,10},{10,8},{12,14},{14,12},{16,18},{18,... | collective-permute-start | bytes 786440 | tf_op jit(solution)/shard_map/ppermute | solution.py:344
  15.5 12.0 %collective-permute-start.6 = (bf16[4,128,256]{2,1,0:T(8,128)(2,1)S(1)}, bf16[4,128,256]{2,1,0:T(8,128)(2,1)S(1)}, u32[]{:S(2)}, u32[]{:S(2)}) collective-permute-start(bf16[4,128,256]{2,1,0:T(8,128)(2,1)S(1)} %pad_maximum_fusion.refs_2_), channel_id=1, source_target_pairs={{0,4},{2,6},{4,0},{6,2},{8,12},{10,14},{12,8},{14,10},{16,20},{18,... | collective-permute-start | bytes 786440 | tf_op jit(solution)/shard_map/ppermute | solution.py:344
  17.0 10.7 %collective-permute-start.7 = (bf16[4,128,256]{2,1,0:T(8,128)(2,1)S(1)}, bf16[4,128,256]{2,1,0:T(8,128)(2,1)S(1)}, u32[]{:S(2)}, u32[]{:S(2)}) collective-permute-start(bf16[4,128,256]{2,1,0:T(8,128)(2,1)S(1)} %pad_maximum_fusion.refs_2_), channel_id=1, source_target_pairs={{0,6},{2,4},{4,2},{6,0},{8,14},{10,12},{12,10},{14,8},{16,22},{18,... | collective-permute-start | bytes 786440 | tf_op jit(solution)/shard_map/ppermute | solution.py:344
  18.4 18.8 %collective-permute-start.10 = (bf16[4,128,256]{2,1,0:T(8,128)(2,1)S(1)}, bf16[4,128,256]{2,1,0:T(8,128)(2,1)S(1)}, u32[]{:S(2)}, u32[]{:S(2)}) collective-permute-start(bf16[4,128,256]{2,1,0:T(8,128)(2,1)S(1)} %pad_maximum_fusion.1.refs_2_), channel_id=1, source_target_pairs={{0,24},{2,26},{4,28},{6,30},{8,16},{10,18},{12,20},{14,22},{16,8},... | collective-permute-start | bytes 786440 | tf_op jit(solution)/shard_map/ppermute | solution.py:348
  21.9 18.9 %collective-permute-start.9 = (bf16[4,128,256]{2,1,0:T(8,128)(2,1)S(1)}, bf16[4,128,256]{2,1,0:T(8,128)(2,1)S(1)}, u32[]{:S(2)}, u32[]{:S(2)}) collective-permute-start(bf16[4,128,256]{2,1,0:T(8,128)(2,1)S(1)} %pad_maximum_fusion.1.refs_2_), channel_id=1, source_target_pairs={{0,16},{2,18},{4,20},{6,22},{8,24},{10,26},{12,28},{14,30},{16,0},... | collective-permute-start | bytes 786440 | tf_op jit(solution)/shard_map/ppermute | solution.py:348
  23.9 17.0 %collective-permute-start.8 = (bf16[4,128,256]{2,1,0:T(8,128)(2,1)S(1)}, bf16[4,128,256]{2,1,0:T(8,128)(2,1)S(1)}, u32[]{:S(2)}, u32[]{:S(2)}) collective-permute-start(bf16[4,128,256]{2,1,0:T(8,128)(2,1)S(1)} %pad_maximum_fusion.1.refs_2_), channel_id=1, source_target_pairs={{0,8},{2,10},{4,12},{6,14},{8,0},{10,2},{12,4},{14,6},{16,24},{18,... | collective-permute-start | bytes 786440 | tf_op jit(solution)/shard_map/ppermute | solution.py:348
  34.8 13.8 %collective-permute-start.11 = (bf16[528,256]{1,0:T(8,128)(2,1)S(1)}, bf16[528,256]{1,0:T(8,128)(2,1)S(1)}, u32[]{:S(2)}, u32[]{:S(2)}) collective-permute-start(bf16[528,256]{1,0:T(8,128)(2,1)S(1)} %get-tuple-element.51), channel_id=1, source_target_pairs={{0,2},{2,0},{4,6},{6,4},{8,10},{10,8},{12,14},{14,12},{16,18},{18,... | collective-permute-start | bytes 811016 | tf_op jit(solution)/shard_map/ppermute | solution.py:344
  35.7 13.0 %collective-permute-start.12 = (bf16[528,256]{1,0:T(8,128)(2,1)S(1)}, bf16[528,256]{1,0:T(8,128)(2,1)S(1)}, u32[]{:S(2)}, u32[]{:S(2)}) collective-permute-start(bf16[528,256]{1,0:T(8,128)(2,1)S(1)} %get-tuple-element.52), channel_id=1, source_target_pairs={{0,4},{2,6},{4,0},{6,2},{8,12},{10,14},{12,8},{14,10},{16,20},{18,... | collective-permute-start | bytes 811016 | tf_op jit(solution)/shard_map/ppermute | solution.py:344
  37.2 11.4 %collective-permute-start.13 = (bf16[528,256]{1,0:T(8,128)(2,1)S(1)}, bf16[528,256]{1,0:T(8,128)(2,1)S(1)}, u32[]{:S(2)}, u32[]{:S(2)}) collective-permute-start(bf16[528,256]{1,0:T(8,128)(2,1)S(1)} %get-tuple-element.53), channel_id=1, source_target_pairs={{0,6},{2,4},{4,2},{6,0},{8,14},{10,12},{12,10},{14,8},{16,22},{18,... | collective-permute-start | bytes 811016 | tf_op jit(solution)/shard_map/ppermute | solution.py:344
  48.8 6.8 %collective-permute-start.17 = (bf16[128,256]{1,0:T(8,128)(2,1)S(1)}, bf16[128,256]{1,0:T(8,128)(2,1)S(1)}, u32[]{:S(2)}, u32[]{:S(2)}) collective-permute-start(bf16[128,256]{1,0:T(8,128)(2,1)S(1)} %get-tuple-element.81), channel_id=1, source_target_pairs={{0,8},{2,10},{4,12},{6,14},{8,0},{10,2},{12,4},{14,6},{16,24},{18,... | collective-permute-start | bytes 196616 | tf_op jit(solution)/shard_map/ppermute | solution.py:348
  48.9 9.6 %collective-permute-start.14 = (bf16[528,256]{1,0:T(8,128)(2,1)S(1)}, bf16[528,256]{1,0:T(8,128)(2,1)S(1)}, u32[]{:S(2)}, u32[]{:S(2)}) collective-permute-start(bf16[528,256]{1,0:T(8,128)(2,1)S(1)} %get-tuple-element.54), channel_id=1, source_target_pairs={{0,2},{2,0},{4,6},{6,4},{8,10},{10,8},{12,14},{14,12},{16,18},{18,... | collective-permute-start | bytes 811016 | tf_op jit(solution)/shard_map/ppermute | solution.py:344
  49.5 11.4 %collective-permute-start.15 = (bf16[528,256]{1,0:T(8,128)(2,1)S(1)}, bf16[528,256]{1,0:T(8,128)(2,1)S(1)}, u32[]{:S(2)}, u32[]{:S(2)}) collective-permute-start(bf16[528,256]{1,0:T(8,128)(2,1)S(1)} %get-tuple-element.55), channel_id=1, source_target_pairs={{0,4},{2,6},{4,0},{6,2},{8,12},{10,14},{12,8},{14,10},{16,20},{18,... | collective-permute-start | bytes 811016 | tf_op jit(solution)/shard_map/ppermute | solution.py:344
  51.0 11.5 %collective-permute-start.16 = (bf16[528,256]{1,0:T(8,128)(2,1)S(1)}, bf16[528,256]{1,0:T(8,128)(2,1)S(1)}, u32[]{:S(2)}, u32[]{:S(2)}) collective-permute-start(bf16[528,256]{1,0:T(8,128)(2,1)S(1)} %get-tuple-element.56), channel_id=1, source_target_pairs={{0,6},{2,4},{4,2},{6,0},{8,14},{10,12},{12,10},{14,8},{16,22},{18,... | collective-permute-start | bytes 811016 | tf_op jit(solution)/shard_map/ppermute | solution.py:344
  52.5 12.3 %collective-permute-start.18 = (bf16[128,256]{1,0:T(8,128)(2,1)S(1)}, bf16[128,256]{1,0:T(8,128)(2,1)S(1)}, u32[]{:S(2)}, u32[]{:S(2)}) collective-permute-start(bf16[128,256]{1,0:T(8,128)(2,1)S(1)} %get-tuple-element.79), channel_id=1, source_target_pairs={{0,16},{2,18},{4,20},{6,22},{8,24},{10,26},{12,28},{14,30},{16,0},... | collective-permute-start | bytes 196616 | tf_op jit(solution)/shard_map/ppermute | solution.py:348
  55.6 9.2 %collective-permute-start.19 = (bf16[128,256]{1,0:T(8,128)(2,1)S(1)}, bf16[128,256]{1,0:T(8,128)(2,1)S(1)}, u32[]{:S(2)}, u32[]{:S(2)}) collective-permute-start(bf16[128,256]{1,0:T(8,128)(2,1)S(1)} %get-tuple-element.80), channel_id=1, source_target_pairs={{0,24},{2,26},{4,28},{6,30},{8,16},{10,18},{12,20},{14,22},{16,8},... | collective-permute-start | bytes 196616 | tf_op jit(solution)/shard_map/ppermute | solution.py:348
  62.8 6.3 %collective-permute-start.22 = (bf16[144,256]{1,0:T(8,128)(2,1)S(1)}, bf16[144,256]{1,0:T(8,128)(2,1)S(1)}, u32[]{:S(2)}, u32[]{:S(2)}) collective-permute-start(bf16[144,256]{1,0:T(8,128)(2,1)S(1)} %get-tuple-element.94), channel_id=1, source_target_pairs={{0,24},{2,26},{4,28},{6,30},{8,16},{10,18},{12,20},{14,22},{16,8},... | collective-permute-start | bytes 221192 | tf_op jit(solution)/shard_map/ppermute | solution.py:348
  64.8 6.2 %collective-permute-start.21 = (bf16[144,256]{1,0:T(8,128)(2,1)S(1)}, bf16[144,256]{1,0:T(8,128)(2,1)S(1)}, u32[]{:S(2)}, u32[]{:S(2)}) collective-permute-start(bf16[144,256]{1,0:T(8,128)(2,1)S(1)} %get-tuple-element.93), channel_id=1, source_target_pairs={{0,16},{2,18},{4,20},{6,22},{8,24},{10,26},{12,28},{14,30},{16,0},... | collective-permute-start | bytes 221192 | tf_op jit(solution)/shard_map/ppermute | solution.py:348
  66.1 4.9 %collective-permute-start.20 = (bf16[144,256]{1,0:T(8,128)(2,1)S(1)}, bf16[144,256]{1,0:T(8,128)(2,1)S(1)}, u32[]{:S(2)}, u32[]{:S(2)}) collective-permute-start(bf16[144,256]{1,0:T(8,128)(2,1)S(1)} %get-tuple-element.92), channel_id=1, source_target_pairs={{0,8},{2,10},{4,12},{6,14},{8,0},{10,2},{12,4},{14,6},{16,24},{18,... | collective-permute-start | bytes 221192 | tf_op jit(solution)/shard_map/ppermute | solution.py:348
  71.1 1.2 %collective-permute-start.23 = (f32[1,256]{1,0:T(1,128)S(1)}, f32[1,256]{1,0:T(1,128)S(1)}, u32[]{:S(2)}, u32[]{:S(2)}) collective-permute-start(f32[1,256]{1,0:T(1,128)S(1)} %fusion.9), channel_id=1, source_target_pairs={{0,1},{1,0},{2,3},{3,2},{4,5},{5,4},{6,7},{7,6},{8,9},{9,8},{10,11... | collective-permute-start | bytes 3080 | tf_op jit(solution)/shard_map/ppermute | solution.py:424
